TPU v7x, 32 devices: a whole 2x2x4 slice. The times are simulated.
32 devices in a mesh: survey: 2 (over x), freq: 16 (over z, y, core).
Axes of the slice: x: 2, y: 2, z: 4, core: 2. Of those that a mesh axis runs over, the one named last changes fastest.
Arguments:
- gathers: float32 [4096, 2048], P(('survey', 'freq')), parts along dimension 0, may hold values from -6 to 6
- operator: bfloat16 [64, 2, 1024, 1024], P(('survey', 'freq')), parts along dimension 0, may hold values from -0.125 to 0.125
- filters: float32 [32, 4, 9, 31], P(('survey', 'freq')), parts along dimension 0, may hold values from -0.18 to 0.18
- tile_of: int32 [32], P('survey'), parts along dimension 0, may hold values from 0 to 15, each once
- slice_len: int32 [32], P('survey'), parts along dimension 0, may hold values from 1 to 2, 20 in all
Outputs:
- primaries: float32 [4096, 2048], P(('survey', 'freq')), parts along dimension 0
There are 2 independent parts, one for each index of `survey`. A program takes and returns all parts, laid end to end along the dimension named above; each array names one. Nothing has to cross between parts.
Inputs may be any that keep to these rules, and one draw needn't show every extreme that they name: `tile_of`: each tile is held by exactly one block of rows. `slice_len`: the entries sum to 20; the largest equals 2.
All inputs are finite; a program needn't handle non-finite values.
Results may differ from a plain program's by a relative error of at most 0.0027.
Values may be sent and summed in bfloat16 or wider, within the bound.
No kernel may reach another device: no remote copies, remote signals or barrier semaphores. Data moves between devices by JAX's collectives and lax.ppermute only.
A program may use at most 64 MiB of HBM per device.

v0:
```python
import math

import jax
import jax.numpy as jnp
from jax import lax
from jax.sharding import PartitionSpec as P

FIRST = 40


def band_tables(first_bin, band_bins, length):
    bin_ids = first_bin + jnp.arange(band_bins, dtype=jnp.int32)
    time_ids = jnp.arange(length, dtype=jnp.int32)
    phase_ids = bin_ids[:, None] * time_ids[None, :] % length
    angles = 2.0 * math.pi / length * phase_ids.astype(jnp.float32)
    return (jnp.cos(angles), jnp.sin(angles))


def forward_table(first_bin, band_bins, length):
    cosine_rows, sine_rows = band_tables(first_bin, band_bins, length)
    return jnp.concatenate([cosine_rows, -sine_rows], axis=0) * (1.0 / math.sqrt(length))


def band_mask(slice_len, band_bins, slot_count):
    bin_ids = jnp.arange(band_bins, dtype=jnp.int32)
    device_ids = jnp.arange(slice_len.shape[0], dtype=jnp.int32)
    group_ids = bin_ids // slot_count
    kept_count = jnp.sum(
        jnp.where(group_ids[:, None] == device_ids[None, :], slice_len[None, :], 0), axis=1
    )
    return (bin_ids % slot_count < kept_count).astype(jnp.float32)


def match_response(band_rows, kept, filters, first_bin, length, kept_bins):
    band_bins = band_rows.shape[0]
    traces = band_rows.shape[2] - 8
    bin_ids = first_bin + jnp.arange(band_bins, dtype=jnp.int32)
    lag_ids = jnp.arange(31, dtype=jnp.int32) - 15
    phase_ids = bin_ids[:, None] * lag_ids[None, :] % length
    angles = 2.0 * math.pi / length * phase_ids.astype(jnp.float32)
    h_real = jnp.einsum("cab,fb->caf", filters, jnp.cos(angles), precision=lax.Precision.HIGHEST)
    h_imag = jnp.einsum("cab,fb->caf", filters, jnp.sin(angles), precision=lax.Precision.HIGHEST)
    weight = bin_ids.astype(jnp.float32) / (first_bin + band_bins)
    k_real = h_real[0] + h_imag[1] - weight * h_imag[2] + weight * h_real[3]
    k_imag = h_imag[0] - h_real[1] + weight * h_real[2] + weight * h_imag[3]
    rows = band_rows.astype(jnp.float32)
    s_real = jnp.zeros((band_bins, traces), jnp.float32)
    s_imag = jnp.zeros((band_bins, traces), jnp.float32)
    for offset in range(9):
        real_rows = rows[:, 0, offset : offset + traces]
        imag_rows = rows[:, 1, offset : offset + traces]
        s_real = s_real + k_real[offset][:, None] * real_rows - k_imag[offset][:, None] * imag_rows
        s_imag = s_imag + k_real[offset][:, None] * imag_rows + k_imag[offset][:, None] * real_rows
    scale = (math.sqrt(2.0 / kept_bins) * kept)[:, None]
    stacked = jnp.concatenate([s_real * scale, s_imag * scale], axis=0)
    cosine_rows, sine_rows = band_tables(first_bin, band_bins, length)
    table = jnp.concatenate([cosine_rows, -sine_rows], axis=0)
    return lax.dot_general(
        stacked,
        table,
        (((0,), (0,)), ((), ())),
        precision=lax.Precision.HIGHEST,
        preferred_element_type=jnp.float32,
    )


def local(gathers, operator, filters, tile_of, slice_len):
    devices = lax.axis_size("freq")
    traces = gathers.shape[0]
    length = gathers.shape[1]
    slot_count = operator.shape[0]
    band_bins = slot_count * devices
    receivers = operator.shape[3]
    per_shot = receivers // traces
    shot_count = devices * traces // receivers
    kept_bins = 5 * devices // 4
    dest_shot = tile_of // per_shot
    holder = jnp.argsort(tile_of)
    anchor = jnp.zeros((), jnp.int32)
    spectrum = lax.dot_general(
        forward_table(FIRST, band_bins, length),
        gathers,
        (((1,), (1,)), ((), ())),
        precision=lax.Precision.HIGHEST,
        preferred_element_type=jnp.float32,
    ).astype(jnp.bfloat16)
    outgoing = spectrum.reshape(2, devices, slot_count, traces)
    incoming = lax.all_to_all(outgoing, "freq", split_axis=1, concat_axis=1, tiled=True)
    arranged = jnp.take(incoming, holder, axis=1).reshape(
        2, shot_count, per_shot, slot_count, traces
    )
    slice_operator = operator.reshape(slot_count, 2, receivers, per_shot, traces)
    products = jnp.einsum(
        "csqmx,mdoqx->mcdso", arranged, slice_operator, preferred_element_type=jnp.float32
    )
    predicted = jnp.stack(
        [products[:, 0, 0] - products[:, 1, 1], products[:, 0, 1] + products[:, 1, 0]], axis=1
    ).astype(jnp.bfloat16)
    widened = jnp.pad(predicted, ((0, 0), (0, 0), (0, 0), (4, 4)))

    def cut_rows(shot_index, start_index):
        return lax.dynamic_slice(
            widened, (anchor, anchor, shot_index, start_index), (slot_count, 2, 1, traces + 8)
        )[:, :, 0]

    sending = jax.vmap(cut_rows)(dest_shot, tile_of % per_shot * traces)
    returned = lax.all_to_all(sending, "freq", split_axis=0, concat_axis=0, tiled=True)
    band_rows = returned.reshape(band_bins, 2, traces + 8)
    kept = band_mask(slice_len, band_bins, slot_count)
    return gathers - match_response(band_rows, kept, filters[0], FIRST, length, kept_bins)


def solution(mesh):
    placed = (
        P(("survey", "freq"), None),
        P(("survey", "freq"), None, None, None),
        P(("survey", "freq"), None, None, None),
        P("survey"),
        P("survey"),
    )
    return jax.shard_map(
        local, mesh=mesh, in_specs=placed, out_specs=P(("survey", "freq"), None), check_vma=False
    )
```

profile of v0, /device:TPU:0, one launch (start us, length us, event | category | flops | bytes accessed | tf_op | source)
XLA Modules:
  0.0 56.3 jit_solution(10247699216002887555)
XLA Ops:
  0.0 1.1 %fusion.13 = (f32[32,2048]{1,0:T(8,128)S(1)}, f32[32,2048]{1,0:T(8,128)S(1)}) fusion(s32[32]{0:T(128)S(1)} %iota_add_fusion.1), kind=kLoop, calls=%fused_computation.22 | loop fusion | flops 983040 | bytes 524416 | tf_op jit(solution)/shard_map/cos | solution.py:16
  1.1 2.4 %convolution_convert_fusion = bf16[64,128]{1,0:T(8,128)(2,1)S(1)} fusion(f32[128,2048]{1,0:T(8,128)} %param.5, f32[32,2048]{1,0:T(8,128)S(1)} %get-tuple-element.46, f32[32,2048]{1,0:T(8,128)S(1)} %get-tuple-element.45), kind=kOutput, calls=%fused_computation.8 | convolution fusion | flops 201596928 | bytes 1589248 | tf_op jit(solution)/shard_map/dot_general | solution.py:80
  3.6 0.6 %copy.94 = bf16[2,16,2,128]{3,2,0,1:T(2,128)(2,1)} copy(bf16[2,16,2,128]{3,2,1,0:T(2,128)(2,1)S(1)} %bitcast.217) | data formatting | bytes 32768 | tf_op jit(solution)/shard_map/reshape | solution.py:87
  4.2 7.4 %all-to-all-start = ((bf16[2,16,2,128]{3,2,0,1:T(2,128)(2,1)}), bf16[2,16,2,128]{3,2,0,1:T(2,128)(2,1)S(1)}, u32[]{:S(2)}, u32[]{:S(2)}) async-start(bf16[2,16,2,128]{3,2,0,1:T(2,128)(2,1)} %copy.94), calls=%async_computation | async-start | bytes 32768 | tf_op jit(solution)/shard_map/all_to_all | solution.py:88
  11.6 2.0 %sort.17 = (s32[16]{0:T(128)}, s32[16]{0:T(128)S(1)}) sort(s32[16]{0:T(128)} %param.8, s32[16]{0:T(128)S(1)} %iota.56), dimensions={0}, to_apply=%region_0.1 | sort | flops 64 | bytes 256 | tf_op jit(solution)/shard_map/jit(argsort)/sort | solution.py:78
  13.6 0.7 %fusion.48 = s32[16]{0:T(128)S(1)} fusion(s32[16]{0:T(128)} %param.8), kind=kLoop, calls=%fused_computation.91 | loop fusion | flops 496 | bytes 128 | tf_op jit(solution)/shard_map/vmap()/concatenate | solution.py:102
  14.3 0.3 convolution_bitcast_fusion
  14.6 0.3 convolution_bitcast_fusion.1
  15.0 0.7 %select_reduce_fusion = s32[32]{0:T(128)S(1)} fusion(s32[16]{0:T(128)} %param.9, s32[32]{0:T(128)S(1)} %and_select_fusion), kind=kLoop, calls=%fused_computation.69 | loop fusion | flops 1504 | bytes 320 | tf_op jit(solution)/shard_map/reduce_sum | solution.py:28
  15.7 0.1 broadcast_in_dim.46
  15.8 8.8 %copy.147 = bf16[512,8,8,128]{3,2,1,0:T(8,128)(2,1)} copy(bf16[512,8,8,128]{3,1,2,0:T(8,128)(2,1)} %bitcast.180) | data formatting | bytes 16777216
  24.6 0.6 %gather_fusion = bf16[16,2,2,128]{3,2,1,0:T(2,128)(2,1)S(1)} fusion(bf16[2,16,2,128]{3,2,1,0:T(2,128)(2,1)S(1)} %copy.95, s32[1024]{0:T(1024)S(1)} %pad_clamp_fusion), kind=kCustom, calls=%fused_computation | custom fusion | bytes 32832 | tf_op jit(solution)/shard_map/jit(_take)/gather | solution.py:89
  25.2 0.1 fusion.26
  25.3 5.7 %fusion.2 = f32[2,2,2,2,1024]{4,3,2,1,0:T(2,128)S(1)} fusion(bf16[2,2,1024,8,128,1]{4,3,2,1,0,5:T(8,128)(2,1)} %bitcast.179, bf16[2,2,8,2,128,1]{4,2,1,3,0,5:T(8,128)(2,1)S(1)} %fusion.26), kind=kOutput, calls=%fused_computation.5 | convolution fusion | flops 33554432 | bytes 8470528 | tf_op jit(solution)/shard_map/csqmx,mdoqx->mcdso/dot_general | solution.py:93
  31.0 0.9 %copy.146 = bf16[2,2,2,1024]{1,0,2,3:T(2,128)(2,1)S(1)} copy(bf16[2,2,2,1024]{3,2,0,1:T(2,128)(2,1)S(1)} %pad_maximum_fusion.3) | data formatting | bytes 32768
  31.9 2.0 %pad.4.clone = bf16[2,2,2,1032]{1,0,2,3:T(2,128)(2,1)} pad(bf16[2,2,2,1024]{1,0,2,3:T(2,128)(2,1)S(1)} %copy.146, bf16[]{:T(256)} %constant.110.clone.1), padding=0_0x0_0x0_0x4_4 | pad | bytes 32898 | tf_op jit(solution)/shard_map/jit(_pad)/pad | solution.py:99
  33.9 4.8 %gather_fusion.1 = bf16[16,2,2,136]{2,1,3,0:T(2,128)(2,1)S(1)} fusion(bf16[2,2,2,1032]{1,0,2,3:T(2,128)(2,1)} %pad.4.clone, s32[16]{0:T(128)S(1)} %fusion.48), kind=kCustom, calls=%fused_computation.1 | custom fusion | bytes 35072 | tf_op jit(solution)/shard_map/vmap()/gather | solution.py:102
  38.6 2.0 %copy.102 = bf16[16,2,2,136]{3,2,1,0:T(2,128)(2,1)} copy(bf16[16,2,2,136]{2,1,3,0:T(2,128)(2,1)S(1)} %gather_fusion.1) | data formatting | bytes 34816 | tf_op jit(solution)/shard_map/vmap()/gather | solution.py:102
  40.6 6.0 %all-to-all-start.1 = ((bf16[16,2,2,136]{3,2,1,0:T(2,128)(2,1)}), bf16[16,2,2,136]{3,2,1,0:T(2,128)(2,1)S(1)}, u32[]{:S(2)}, u32[]{:S(2)}) async-start(bf16[16,2,2,136]{3,2,1,0:T(2,128)(2,1)} %copy.102), calls=%async_computation.1 | async-start | bytes 65536 | tf_op jit(solution)/shard_map/all_to_all | solution.py:107
  46.6 6.6 %all-to-all-done.1 = bf16[16,2,2,136]{3,2,1,0:T(2,128)(2,1)S(1)} async-done(((bf16[16,2,2,136]{3,2,1,0:T(2,128)(2,1)}), bf16[16,2,2,136]{3,2,1,0:T(2,128)(2,1)S(1)}, u32[]{:S(2)}, u32[]{:S(2)}) %all-to-all-start.1) | async-done | bytes 17440 | tf_op jit(solution)/shard_map/all_to_all | solution.py:107
  53.3 0.6 %fusion.62 = (f32[32,1,128]{2,1,0:T(1,128)S(1)}, f32[32,1,128]{2,1,0:T(1,128)S(1)}, f32[32,1,128]{2,1,0:T(1,128)S(1)}, f32[32,1,128]{2,1,0:T(1,128)S(1)}, f32[32...) fusion(f32[32,2,136]{2,1,0:T(2,128)S(1)} %bitcast_convert_fusion), kind=kLoop, calls=%fused_computation.127 | loop fusion | bytes 589824 | tf_op jit(solution)/shard_map/slice | solution.py:51
  53.9 0.2 subtract_multiply_fusion
  54.1 0.2 add_multiply_fusion
  54.3 2.0 %convolution_subtract_fusion = f32[128,2048]{1,0:T(8,128)} fusion(f32[128,2048]{1,0:T(8,128)S(1)} %copy-done.1, f32[32,2048]{1,0:T(8,128)S(1)} %get-tuple-element.46, f32[32,2048]{1,0:T(8,128)S(1)} %get-tuple-element.45, f32[32,128]{1,0:T(8,128)S(1)} %add_multiply_fusion, f32[32,128]{1,0:T(8,128)S(1)} %subtract_multiply_fusion), kind=kOutput, calls=%fused_computation.4 | convolution fusion | flops 201728000 | bytes 2654208 | tf_op jit(solution)/shard_map/dot_general | solution.py:58
  (21 shorter events, 0.2 us)
Async XLA Ops:
  0.0 14.3 %copy-start = (f32[1,4,9,31]{3,1,2,0:T(4,128)S(1)}, f32[1,4,9,31]{3,1,2,0:T(4,128)}, u32[]{:S(2)}) copy-start(f32[1,4,9,31]{3,1,2,0:T(4,128)} %param.7) | copy-start | bytes 13396
  4.2 20.4 %all-to-all-start = ((bf16[2,16,2,128]{3,2,0,1:T(2,128)(2,1)}), bf16[2,16,2,128]{3,2,0,1:T(2,128)(2,1)S(1)}, u32[]{:S(2)}, u32[]{:S(2)}) async-start(bf16[2,16,2,128]{3,2,0,1:T(2,128)(2,1)} %copy.94), calls=%async_computation | async-start | bytes 32768 | tf_op jit(solution)/shard_map/all_to_all | solution.py:88
  24.6 29.7 %copy-start.1 = (f32[128,2048]{1,0:T(8,128)S(1)}, f32[128,2048]{1,0:T(8,128)}, u32[]{:S(2)}) copy-start(f32[128,2048]{1,0:T(8,128)} %param.5) | copy-start | bytes 3145732
  40.6 12.6 %all-to-all-start.1 = ((bf16[16,2,2,136]{3,2,1,0:T(2,128)(2,1)}), bf16[16,2,2,136]{3,2,1,0:T(2,128)(2,1)S(1)}, u32[]{:S(2)}, u32[]{:S(2)}) async-start(bf16[16,2,2,136]{3,2,1,0:T(2,128)(2,1)} %copy.102), calls=%async_computation.1 | async-start | bytes 65536 | tf_op jit(solution)/shard_map/all_to_all | solution.py:107
where the time goes:
time: 56.7 us; the launch traced here: 56.3 us
  local copies, waits for them, and re-layouts  20.3 us (36%)
  starting transfers between devices  13.4 us (24%)
  matrix products  10.8 us (19%)
  waiting for transfers between devices  6.62 us (12%)
  other arithmetic  5.05 us (9%)
    unnamed x6, local copies, waits for them, and re-layouts  9.65 us
    all_to_all x1, starting transfers between devices, local(): lax.all_to_all(outgoing, 'freq', split_axis=1, concat_axis=1, tiled=True)  7.38 us
    gather x2, local copies, waits for them, and re-layouts, cut_rows(): lax.dynamic_slice(widened, (anchor, anchor, shot_index, start_index), (sl...  6.7 us
    all_to_all x1, waiting for transfers between devices, local(): lax.all_to_all(sending, 'freq', split_axis=0, concat_axis=0, tiled=True)  6.62 us
    all_to_all x1, starting transfers between devices, local(): lax.all_to_all(sending, 'freq', split_axis=0, concat_axis=0, tiled=True)  6 us
    dot_general x1, matrix products, local(): jnp.einsum('csqmx,mdoqx->mcdso', arranged, slice_operator, preferred_elem...  5.7 us
    dot_general x1, matrix products, local(): lax.dot_general(forward_table(FIRST, band_bins, length), gathers, (((1,),...  2.44 us
    dot_general x1, matrix products, match_response(): lax.dot_general(stacked, table, (((0,), (0,)), ((), ())), precision=lax.P...  2.04 us
  transfers between devices with their start and end apart: 2, of which 1 were waited for; matrix products, arithmetic and copies ran while one was open for 23% of the time, Pallas kernels for 0%

commit v1 on v0

v1 whole, which is shorter than its diff:
```python
import functools
import math

import jax
import jax.numpy as jnp
import ml_dtypes
import numpy as np
from jax import lax
from jax.experimental import pallas as pl
from jax.experimental.pallas import tpu as pltpu
from jax.sharding import PartitionSpec as P

FIRST = 40
REACH = 4
VMEM_LIMIT = 40 * 1024 * 1024


def split_halves(values):
    values = values.astype(np.float32)
    high = values.astype(ml_dtypes.bfloat16)
    low = (values - high.astype(np.float32)).astype(ml_dtypes.bfloat16)
    return high, low


def row_tables(band_bins, length):
    bin_ids = FIRST + np.arange(band_bins)
    angles = 2.0 * np.pi / length * (bin_ids[:, None] * np.arange(length)[None, :] % length)
    return np.stack([np.cos(angles), -np.sin(angles)], axis=1).reshape(2 * band_bins, length)


def lag_tables(band_bins, lags, length):
    bin_ids = FIRST + np.arange(band_bins)
    lag_ids = np.arange(lags) - lags // 2
    angles = 2.0 * np.pi / length * (bin_ids[:, None] * lag_ids[None, :] % length)
    cosine, sine = np.cos(angles), np.sin(angles)
    weight = (bin_ids / (FIRST + band_bins))[:, None]
    real = np.stack([cosine, sine, -weight * sine, weight * cosine])
    imag = np.stack([sine, -cosine, weight * cosine, weight * sine])
    own = np.stack([real, real], axis=2).reshape(4, 2 * band_bins, lags)
    partner = np.stack([-imag, imag], axis=2).reshape(4, 2 * band_bins, lags)
    return np.concatenate([own, partner], axis=1).astype(np.float32)


def split_array(values):
    high = values.astype(jnp.bfloat16)
    low = (values - high.astype(jnp.float32)).astype(jnp.bfloat16)
    return high, low


def swap_pairs(values):
    rows = values.shape[0]
    parity = lax.broadcasted_iota(jnp.int32, values.shape, 0) % 2
    return jnp.where(
        parity == 0, pltpu.roll(values, rows - 1, 0), pltpu.roll(values, 1, 0)
    )


def spectrum_kernel(gathers_ref, high_ref, low_ref, out_ref):
    nt = (((1,), (1,)), ((), ()))
    high, low = split_array(gathers_ref[...])
    dot = functools.partial(
        lax.dot_general, dimension_numbers=nt, preferred_element_type=jnp.float32
    )
    total = dot(high_ref[...], high) + (dot(high_ref[...], low) + dot(low_ref[...], high))
    out_ref[...] = total.astype(jnp.bfloat16).reshape(out_ref.shape)


def coefficient_kernel(kept_bins, slots, slice_ref, filters_ref, table_ref, out_ref):
    rows = out_ref.shape[1]
    offsets = filters_ref.shape[2]
    width = out_ref.shape[2]
    total = jnp.zeros((2 * rows, offsets), jnp.float32)
    for part in range(filters_ref.shape[1]):
        total = total + lax.dot_general(
            table_ref[part],
            filters_ref[0, part],
            (((1,), (1,)), ((), ())),
            precision=lax.Precision.HIGHEST,
            preferred_element_type=jnp.float32,
        )
    row_ids = lax.broadcasted_iota(jnp.int32, (rows, width), 0)
    group = row_ids // (2 * slots)
    slot = row_ids // 2 % slots
    count = jnp.zeros((rows, width), jnp.int32)
    for device in range(rows // (2 * slots)):
        count = jnp.where(group == device, slice_ref[device], count)
    scale = jnp.where(slot < count, math.sqrt(2.0 / kept_bins), 0.0)
    for offset in range(offsets):
        out_ref[offset] = total[:rows, offset : offset + 1] * scale
        out_ref[offsets + offset] = total[rows:, offset : offset + 1] * scale


def predict_kernel(tile_ref, incoming_ref, operator_ref, out_ref, holder_ref, tiles_ref):
    devices, group_rows, traces = incoming_ref.shape
    slots, _, receivers, _ = operator_ref.shape
    per_shot = receivers // traces
    shots = devices // per_shot
    for k in range(devices):
        holder_ref[tile_ref[k]] = k
    columns = []
    for q in range(per_shot):
        parts = [
            incoming_ref[holder_ref[s * per_shot + q]].astype(jnp.float32) for s in range(shots)
        ]
        columns.append(jnp.concatenate(parts, axis=0))
    spectrum = jnp.concatenate(columns, axis=1).astype(jnp.bfloat16)
    rows = shots * group_rows
    row_ids = lax.broadcasted_iota(jnp.int32, (rows, receivers), 0)
    dot = functools.partial(
        lax.dot_general,
        dimension_numbers=(((1,), (1,)), ((), ())),
        preferred_element_type=jnp.float32,
    )
    predicted = jnp.zeros((rows, receivers), jnp.float32)
    for slot in range(slots):
        by_real = dot(spectrum, operator_ref[slot, 0])
        by_imag = swap_pairs(dot(spectrum, operator_ref[slot, 1]))
        product = jnp.where(row_ids % 2 == 0, by_real - by_imag, by_real + by_imag)
        predicted = jnp.where(row_ids // 2 % slots == slot, product, predicted)
    for s in range(shots):
        for q in range(per_shot):
            tiles_ref[s * per_shot + q] = predicted[
                s * group_rows : (s + 1) * group_rows, q * traces : (q + 1) * traces
            ]
    lane_ids = lax.broadcasted_iota(jnp.int32, (group_rows, traces), 1)
    for k in range(devices):
        tile = tile_ref[k]
        place = tile % per_shot
        before = tiles_ref[jnp.maximum(tile - 1, 0)]
        after = tiles_ref[jnp.minimum(tile + 1, devices - 1)]
        first_lanes = jnp.where(place < per_shot - 1, REACH, 0)
        last_lanes = jnp.where(place > 0, traces - REACH, traces)
        halo = jnp.where(lane_ids < first_lanes, after, 0.0)
        halo = jnp.where(lane_ids >= last_lanes, before, halo)
        both = jnp.concatenate([tiles_ref[tile], halo], axis=1)
        out_ref[k] = both.astype(jnp.bfloat16)


def subtract_kernel(returned_ref, coefficient_ref, table_ref, gathers_ref, out_ref):
    devices, group_rows, width = returned_ref.shape
    rows = devices * group_rows
    traces = gathers_ref.shape[0]
    own = returned_ref[...].astype(jnp.float32).reshape(rows, width)
    partner = swap_pairs(own)
    offsets = coefficient_ref.shape[0] // 2
    total = jnp.zeros((rows, traces), jnp.float32)
    for offset in range(offsets):
        shift = (offsets // 2 - offset) % width
        moved = pltpu.roll(own, shift, 1)[:, :traces]
        moved_partner = pltpu.roll(partner, shift, 1)[:, :traces]
        total = total + coefficient_ref[offset] * moved
        total = total + coefficient_ref[offsets + offset] * moved_partner
    high, low = split_array(jnp.transpose(total))
    stacked = jnp.concatenate([high, low, high], axis=1)
    response = jnp.dot(stacked, table_ref[...], preferred_element_type=jnp.float32)
    out_ref[...] = gathers_ref[...] - response


def vmem_spec():
    return pl.BlockSpec(memory_space=pltpu.VMEM)


def smem_spec():
    return pl.BlockSpec(memory_space=pltpu.SMEM)


def local(gathers, operator, filters, tile_of, slice_len):
    devices = lax.axis_size("freq")
    traces, length = gathers.shape
    slots, _, receivers, _ = operator.shape
    band_bins = slots * devices
    rows = 2 * band_bins
    group_rows = 2 * slots
    kept_bins = 5 * devices // 4
    offsets, lags = filters.shape[2], filters.shape[3]
    params = pltpu.CompilerParams(vmem_limit_bytes=VMEM_LIMIT)
    table = row_tables(band_bins, length)
    forward_high, forward_low = split_halves(table / math.sqrt(length))
    back_high, back_low = split_halves(table)
    back_table = np.concatenate([back_high, back_high, back_low], axis=0)

    with jax.named_scope("spectrum"):
        outgoing = pl.pallas_call(
            spectrum_kernel,
            out_shape=jax.ShapeDtypeStruct((devices, group_rows, traces), jnp.bfloat16),
            in_specs=[vmem_spec()] * 3,
            out_specs=vmem_spec(),
            compiler_params=params,
            name="spectrum",
        )(gathers, jnp.asarray(forward_high), jnp.asarray(forward_low))
    incoming = lax.all_to_all(outgoing, "freq", split_axis=0, concat_axis=0, tiled=True)
    with jax.named_scope("coefficients"):
        coefficients = pl.pallas_call(
            functools.partial(coefficient_kernel, kept_bins, slots),
            out_shape=jax.ShapeDtypeStruct((2 * offsets, rows, traces), jnp.float32),
            in_specs=[smem_spec(), vmem_spec(), vmem_spec()],
            out_specs=vmem_spec(),
            compiler_params=params,
            name="coefficients",
        )(slice_len, filters, jnp.asarray(lag_tables(band_bins, lags, length)))
    with jax.named_scope("predict"):
        sending = pl.pallas_call(
            predict_kernel,
            out_shape=jax.ShapeDtypeStruct((devices, group_rows, 2 * traces), jnp.bfloat16),
            in_specs=[smem_spec(), vmem_spec(), vmem_spec()],
            out_specs=vmem_spec(),
            scratch_shapes=[
                pltpu.SMEM((devices,), jnp.int32),
                pltpu.VMEM((devices, group_rows, traces), jnp.float32),
            ],
            compiler_params=params,
            name="predict",
        )(tile_of, incoming, operator)
    returned = lax.all_to_all(sending, "freq", split_axis=0, concat_axis=0, tiled=True)
    with jax.named_scope("subtract"):
        return pl.pallas_call(
            subtract_kernel,
            out_shape=jax.ShapeDtypeStruct((traces, length), jnp.float32),
            in_specs=[vmem_spec()] * 4,
            out_specs=vmem_spec(),
            compiler_params=params,
            name="subtract",
        )(returned, coefficients, jnp.asarray(back_table), gathers)


def solution(mesh):
    placed = (
        P(("survey", "freq"), None),
        P(("survey", "freq"), None, None, None),
        P(("survey", "freq"), None, None, None),
        P("survey"),
        P("survey"),
    )
    return jax.shard_map(
        local, mesh=mesh, in_specs=placed, out_specs=P(("survey", "freq"), None), check_vma=False
    )
```

time: 56.7 us -> 37.1 us (0.65)
  blocking collectives: 0 us -> 13.7 us
  local copies, waits for them, and re-layouts: 20.3 us -> 7.18 us
  matrix products: 10.8 us -> 0 us
  starting transfers between devices: 13.4 us -> 3.5 us
  Pallas kernels: 0 us -> 6.9 us
  other arithmetic: 5.05 us -> 0 us
  waiting for transfers between devices: 6.62 us -> 5.41 us
    all_to_all x0 -> x1, blocking collectives: none -> 13.7 us  [local(): lax.all_to_all(outgoing, 'freq', split_axis=0, concat_axis=0, tiled=True)]
    dot_general x5 -> x0, matrix products: 10.8 us -> none  [the longest x1 5.7 us: local(): jnp.einsum('csqmx,mdoqx->mcdso', arranged, slice_operator, preferred_elem...]
    all_to_all x1 -> x0, starting transfers between devices: 7.38 us -> none  [local(): lax.all_to_all(outgoing, 'freq', split_axis=1, concat_axis=1, tiled=True)]
    gather x3 -> x0, local copies, waits for them, and re-layouts: 7.3 us -> none  [the longest x2 6.7 us: cut_rows(): lax.dynamic_slice(widened, (anchor, anchor, shot_index, start_index), (sl...]
    pallas_call x0 -> x4, Pallas kernels: none -> 6.9 us  [the longest x1 3.51 us: local(): pl.pallas_call(predict_kernel, out_shape=jax.ShapeDtypeStruct((devices, g...]
    all_to_all x1, starting transfers between devices: 6 us -> 3.5 us  [local(): lax.all_to_all(sending, 'freq', split_axis=0, concat_axis=0, tiled=True)]
    unnamed x6 -> x21, local copies, waits for them, and re-layouts: 9.65 us -> 7.18 us
    sort x1 -> x0, other arithmetic: 1.98 us -> none  [local(): holder = jnp.argsort(tile_of)]
  transfers between devices with their start and end apart: 2 -> 1, of which waited for: 1 -> 1; matrix products, arithmetic and copies ran while one was open for 23% -> 0% of each run, Pallas kernels for 0% -> 3%
where the time goes in v1:
time: 37.1 us; the launch traced here: 36.7 us
  blocking collectives  13.7 us (37%)
  local copies, waits for them, and re-layouts  7.18 us (19%)
  Pallas kernels  6.9 us (19%)
  waiting for transfers between devices  5.41 us (15%)
  starting transfers between devices  3.5 us (9%)
    all_to_all x1, blocking collectives, local(): lax.all_to_all(outgoing, 'freq', split_axis=0, concat_axis=0, tiled=True)  13.7 us
    unnamed x21, local copies, waits for them, and re-layouts  7.18 us
    all_to_all x1, waiting for transfers between devices, local(): lax.all_to_all(sending, 'freq', split_axis=0, concat_axis=0, tiled=True)  5.41 us
    pallas_call x1, Pallas kernels, local(): pl.pallas_call(predict_kernel, out_shape=jax.ShapeDtypeStruct((devices, g...  3.51 us
    all_to_all x1, starting transfers between devices, local(): lax.all_to_all(sending, 'freq', split_axis=0, concat_axis=0, tiled=True)  3.5 us
    pallas_call x1, Pallas kernels, local(): pl.pallas_call(subtract_kernel, out_shape=jax.ShapeDtypeStruct((traces, l...  1.58 us
    pallas_call x1, Pallas kernels, local(): pl.pallas_call(functools.partial(coefficient_kernel, kept_bins, slots), o...  1.14 us
  transfers between devices with their start and end apart: 1, of which 1 were waited for; matrix products, arithmetic and copies ran while one was open for 0% of the time, Pallas kernels for 3%

profile of v1, /device:TPU:0, one launch (start us, length us, event | category | flops | bytes accessed | tf_op | source)
XLA Modules:
  0.0 36.7 jit_solution(5641290593688830058)
XLA Ops:
  0.0 0.0 copy-start.1
  0.0 1.2 %copy-done.1 = f32[128,2048]{1,0:T(8,128)S(1)} copy-done((f32[128,2048]{1,0:T(8,128)S(1)}, f32[128,2048]{1,0:T(8,128)}, u32[]{:S(2)}) %copy-start.1) | copy-done | bytes 1048600
  1.2 0.0 copy-start.5
  1.2 0.9 %copy-done.5 = bf16[64,2048]{1,0:T(8,128)(2,1)S(1)} copy-done((bf16[64,2048]{1,0:T(8,128)(2,1)S(1)}, bf16[64,2048]{1,0:T(8,128)(2,1)}, u32[]{:S(2)}) %copy-start.5) | copy-done | bytes 262168
  2.2 0.0 copy-start.6
  2.2 0.9 %copy-done.6 = bf16[64,2048]{1,0:T(8,128)(2,1)S(1)} copy-done((bf16[64,2048]{1,0:T(8,128)(2,1)S(1)}, bf16[64,2048]{1,0:T(8,128)(2,1)}, u32[]{:S(2)}) %copy-start.6) | copy-done | bytes 262168
  3.1 0.0 copy-start.9
  3.1 0.0 copy-start.4
  3.1 0.0 copy-start.8
  3.1 0.0 copy-start.2
  3.1 0.7 %spectrum.1 = bf16[16,4,128]{2,1,0:T(4,128)(2,1)S(1)} custom-call(f32[128,2048]{1,0:T(8,128)S(1)} %copy-done.1, bf16[64,2048]{1,0:T(8,128)(2,1)S(1)} %copy-done.6, bf16[64,2048]{1,0:T(8,128)(2,1)S(1)} %copy-done.5), custom_call_target="tpu_custom_call" | custom-call | tf_op jit(solution)/shard_map/spectrum/spectrum/pallas_call | solution.py:183
  3.8 13.7 %all_to_all.10.incoming_ref = bf16[16,4,128]{2,1,0:T(4,128)(2,1)S(1)} all-to-all(bf16[16,4,128]{2,1,0:T(4,128)(2,1)S(1)} %spectrum.1), channel_id=1, replica_groups=mesh['survey'=2,'freq'=16] {'freq'}, dimensions={0} | all-to-all | bytes 32768 | tf_op jit(solution)/shard_map/all_to_all | solution.py:191
  17.5 3.4 %copy-done = bf16[2,2,1024,1024]{3,2,1,0:T(8,128)(2,1)S(1)} copy-done((bf16[2,2,1024,1024]{3,2,1,0:T(8,128)(2,1)S(1)}, bf16[2,2,1024,1024]{3,2,1,0:T(8,128)(2,1)}, u32[]{:S(2)}) %copy-start) | copy-done | bytes 8388632
  20.9 0.7 %copy-done.7 = s32[16]{0:T(128)S(1)} copy-done((s32[16]{0:T(128)S(1)}, s32[16]{0:T(128)}, u32[]{:S(2)}) %copy-start.7) | copy-done | bytes 88
  21.5 3.5 %predict.1 = bf16[16,4,256]{2,1,0:T(4,128)(2,1)} custom-call(s32[16]{0:T(128)S(1)} %copy-done.7, bf16[16,4,128]{2,1,0:T(4,128)(2,1)S(1)} %all_to_all.10.incoming_ref, bf16[2,2,1024,1024]{3,2,1,0:T(8,128)(2,1)S(1)} %copy-done), custom_call_target="tpu_custom_call" | custom-call | tf_op jit(solution)/shard_map/predict/predict/pallas_call | solution.py:202
  25.0 3.5 %all-to-all-start.1 = ((bf16[16,4,256]{2,1,0:T(4,128)(2,1)}), bf16[16,4,256]{2,1,0:T(4,128)(2,1)S(1)}, u32[]{:S(2)}, u32[]{:S(2)}) async-start(bf16[16,4,256]{2,1,0:T(4,128)(2,1)} %predict.1), calls=%async_computation.1 | async-start | bytes 65536 | tf_op jit(solution)/shard_map/all_to_all | solution.py:214
  28.5 0.0 copy-done.9
  28.6 0.0 copy-done.4
  28.6 0.0 copy-done.8
  28.6 1.1 %coefficients.1.coefficient_ref = f32[18,64,128]{2,1,0:T(8,128)S(1)} custom-call(s32[16]{0:T(128)S(1)} %copy-done.8, f32[1,4,9,31]{3,2,1,0:T(8,128)S(1)} %copy.10.filters_ref, f32[4,128,31]{2,1,0:T(8,128)S(1)} %copy-done.4), custom_call_target="tpu_custom_call" | custom-call | tf_op jit(solution)/shard_map/coefficients/coefficients/pallas_call | solution.py:193
  29.7 5.4 %all-to-all-done.1.returned_ref = bf16[16,4,256]{2,1,0:T(4,128)(2,1)S(1)} async-done(((bf16[16,4,256]{2,1,0:T(4,128)(2,1)}), bf16[16,4,256]{2,1,0:T(4,128)(2,1)S(1)}, u32[]{:S(2)}, u32[]{:S(2)}) %all-to-all-start.1) | async-done | bytes 32800 | tf_op jit(solution)/shard_map/all_to_all | solution.py:214
  35.1 0.0 copy-done.2
  35.1 0.0 copy-done.3
  35.1 1.6 %subtract.1 = f32[128,2048]{1,0:T(8,128)} custom-call(bf16[16,4,256]{2,1,0:T(4,128)(2,1)S(1)} %all-to-all-done.1.returned_ref, f32[18,64,128]{2,1,0:T(8,128)S(1)} %coefficients.1.coefficient_ref, bf16[192,2048]{1,0:T(8,128)(2,1)S(1)} %copy-done.3, f32[128,2048]{1,0:T(8,128)S(1)} %copy-done.2), custom_call_target="tpu_custom_call" | custom-call | tf_op jit(solution)/shard_map/subtract/subtract/pallas_call | solution.py:216
  (4 shorter events, 0.0 us)
Async XLA Ops:
  0.0 1.2 %copy-start.1 = (f32[128,2048]{1,0:T(8,128)S(1)}, f32[128,2048]{1,0:T(8,128)}, u32[]{:S(2)}) copy-start(f32[128,2048]{1,0:T(8,128)} %gathers_ref.3) | copy-start | bytes 3145732
  1.2 0.9 %copy-start.5 = (bf16[64,2048]{1,0:T(8,128)(2,1)S(1)}, bf16[64,2048]{1,0:T(8,128)(2,1)}, u32[]{:S(2)}) copy-start(bf16[64,2048]{1,0:T(8,128)(2,1)} %constant.9.clone.low_ref) | copy-start | bytes 786436
  2.2 0.9 %copy-start.6 = (bf16[64,2048]{1,0:T(8,128)(2,1)S(1)}, bf16[64,2048]{1,0:T(8,128)(2,1)}, u32[]{:S(2)}) copy-start(bf16[64,2048]{1,0:T(8,128)(2,1)} %constant.8.clone.high_ref) | copy-start | bytes 786436
  3.1 25.4 %copy-start.9 = (f32[1,4,9,31]{3,1,2,0:T(4,128)S(1)}, f32[1,4,9,31]{3,1,2,0:T(4,128)}, u32[]{:S(2)}) copy-start(f32[1,4,9,31]{3,1,2,0:T(4,128)} %param.11) | copy-start | bytes 13396
  3.1 25.4 %copy-start.4 = (f32[4,128,31]{2,1,0:T(8,128)S(1)}, f32[4,128,31]{2,1,0:T(8,128)}, u32[]{:S(2)}) copy-start(f32[4,128,31]{2,1,0:T(8,128)} %constant.10.clone.table_ref) | copy-start | bytes 190468
  3.1 25.4 %copy-start.8 = (s32[16]{0:T(128)S(1)}, s32[16]{0:T(128)}, u32[]{:S(2)}) copy-start(s32[16]{0:T(128)} %slice_ref.1) | copy-start | bytes 196
  3.1 32.0 %copy-start.2 = (f32[128,2048]{1,0:T(8,128)S(1)}, f32[128,2048]{1,0:T(8,128)}, u32[]{:S(2)}) copy-start(f32[128,2048]{1,0:T(8,128)} %gathers_ref.3) | copy-start | bytes 3145732
  17.5 3.4 %copy-start = (bf16[2,2,1024,1024]{3,2,1,0:T(8,128)(2,1)S(1)}, bf16[2,2,1024,1024]{3,2,1,0:T(8,128)(2,1)}, u32[]{:S(2)}) copy-start(bf16[2,2,1024,1024]{3,2,1,0:T(8,128)(2,1)} %operator_ref.1) | copy-start | bytes 25165828
  20.9 0.7 %copy-start.7 = (s32[16]{0:T(128)S(1)}, s32[16]{0:T(128)}, u32[]{:S(2)}) copy-start(s32[16]{0:T(128)} %tile_ref.1) | copy-start | bytes 196
  21.5 13.6 %copy-start.3 = (bf16[192,2048]{1,0:T(8,128)(2,1)S(1)}, bf16[192,2048]{1,0:T(8,128)(2,1)}, u32[]{:S(2)}) copy-start(bf16[192,2048]{1,0:T(8,128)(2,1)} %constant.11.clone.table_ref) | copy-start | bytes 2359300
  25.0 10.1 %all-to-all-start.1 = ((bf16[16,4,256]{2,1,0:T(4,128)(2,1)}), bf16[16,4,256]{2,1,0:T(4,128)(2,1)S(1)}, u32[]{:S(2)}, u32[]{:S(2)}) async-start(bf16[16,4,256]{2,1,0:T(4,128)(2,1)} %predict.1), calls=%async_computation.1 | async-start | bytes 65536 | tf_op jit(solution)/shard_map/all_to_all | solution.py:214

commit v2 on v1

--- a/solution.py
+++ b/solution.py
@@ -55,17 +55,48 @@
     )
 
 
-def spectrum_kernel(gathers_ref, high_ref, low_ref, out_ref):
-    nt = (((1,), (1,)), ((), ()))
-    high, low = split_array(gathers_ref[...])
+def spectrum_kernel(chunk, self_ref, gathers_ref, table_ref, *refs):
+    outs, (held, table, products, sems) = refs[:-4], refs[-4:]
+    devices = len(outs)
+    length = gathers_ref.shape[1]
+    rows = table_ref.shape[0] // 2
+    copies = []
+    for step in range(length // chunk):
+        part = pl.ds(step * chunk, chunk)
+        copies.append(
+            (
+                pltpu.make_async_copy(gathers_ref.at[:, part], held.at[:, part], sems.at[0, step]),
+                pltpu.make_async_copy(table_ref.at[:, part], table.at[:, part], sems.at[1, step]),
+            )
+        )
+    for pair in copies:
+        for copy in pair:
+            copy.start()
     dot = functools.partial(
-        lax.dot_general, dimension_numbers=nt, preferred_element_type=jnp.float32
-    )
-    total = dot(high_ref[...], high) + (dot(high_ref[...], low) + dot(low_ref[...], high))
-    out_ref[...] = total.astype(jnp.bfloat16).reshape(out_ref.shape)
-
-
-def coefficient_kernel(kept_bins, slots, slice_ref, filters_ref, table_ref, out_ref):
+        lax.dot_general,
+        dimension_numbers=(((1,), (1,)), ((), ())),
+        preferred_element_type=jnp.float32,
+    )
+    total = jnp.zeros((rows, held.shape[0]), jnp.float32)
+    for step, pair in enumerate(copies):
+        for copy in pair:
+            copy.wait()
+        part = pl.ds(step * chunk, chunk)
+        high, low = split_array(held[:, part])
+        weights = table[:, part]
+        both = dot(weights, high)
+        total = total + both[:rows] + (both[rows:] + dot(weights[:rows], low))
+    products[...] = total.reshape(products.shape)
+    me = self_ref[0]
+    for r in range(devices):
+        outs[r][...] = products[me ^ r].astype(jnp.bfloat16)
+
+
+def prepare_kernel(
+    kept_bins, slots, slice_ref, after_ref, filters_ref, table_ref, operator_ref, out_ref, held_ref, sem
+):
+    copy = pltpu.make_async_copy(operator_ref, held_ref, sem)
+    copy.start()
     rows = out_ref.shape[1]
     offsets = filters_ref.shape[2]
     width = out_ref.shape[2]
@@ -88,20 +119,21 @@
     for offset in range(offsets):
         out_ref[offset] = total[:rows, offset : offset + 1] * scale
         out_ref[offsets + offset] = total[rows:, offset : offset + 1] * scale
-
-
-def predict_kernel(tile_ref, incoming_ref, operator_ref, out_ref, holder_ref, tiles_ref):
-    devices, group_rows, traces = incoming_ref.shape
+    copy.wait()
+
+
+def predict_kernel(devices, self_ref, tile_ref, *refs):
+    incoming, (operator_ref, out_ref, spectra) = refs[:devices], refs[devices:]
+    group_rows, traces = incoming[0].shape
     slots, _, receivers, _ = operator_ref.shape
     per_shot = receivers // traces
     shots = devices // per_shot
-    for k in range(devices):
-        holder_ref[tile_ref[k]] = k
+    me = self_ref[0]
+    for r in range(devices):
+        spectra[tile_ref[me ^ r]] = incoming[r][...].astype(jnp.float32)
     columns = []
     for q in range(per_shot):
-        parts = [
-            incoming_ref[holder_ref[s * per_shot + q]].astype(jnp.float32) for s in range(shots)
-        ]
+        parts = [spectra[s * per_shot + q] for s in range(shots)]
         columns.append(jnp.concatenate(parts, axis=0))
     spectrum = jnp.concatenate(columns, axis=1).astype(jnp.bfloat16)
     rows = shots * group_rows
@@ -119,28 +151,27 @@
         predicted = jnp.where(row_ids // 2 % slots == slot, product, predicted)
     for s in range(shots):
         for q in range(per_shot):
-            tiles_ref[s * per_shot + q] = predicted[
+            out_ref[s * per_shot + q] = predicted[
                 s * group_rows : (s + 1) * group_rows, q * traces : (q + 1) * traces
-            ]
-    lane_ids = lax.broadcasted_iota(jnp.int32, (group_rows, traces), 1)
-    for k in range(devices):
-        tile = tile_ref[k]
-        place = tile % per_shot
-        before = tiles_ref[jnp.maximum(tile - 1, 0)]
-        after = tiles_ref[jnp.minimum(tile + 1, devices - 1)]
-        first_lanes = jnp.where(place < per_shot - 1, REACH, 0)
-        last_lanes = jnp.where(place > 0, traces - REACH, traces)
-        halo = jnp.where(lane_ids < first_lanes, after, 0.0)
-        halo = jnp.where(lane_ids >= last_lanes, before, halo)
-        both = jnp.concatenate([tiles_ref[tile], halo], axis=1)
-        out_ref[k] = both.astype(jnp.bfloat16)
-
-
-def subtract_kernel(returned_ref, coefficient_ref, table_ref, gathers_ref, out_ref):
-    devices, group_rows, width = returned_ref.shape
+            ].astype(jnp.bfloat16)
+
+
+def subtract_kernel(per_shot, tile_ref, returned_ref, coefficient_ref, table_ref, gathers_ref, out_ref):
+    devices, tiles, group_rows, traces = returned_ref.shape
     rows = devices * group_rows
-    traces = gathers_ref.shape[0]
-    own = returned_ref[...].astype(jnp.float32).reshape(rows, width)
+    width = 2 * traces
+    tile = tile_ref[0]
+    place = tile % per_shot
+
+    def held(index):
+        return returned_ref[:, index].astype(jnp.float32).reshape(rows, traces)
+
+    lane_ids = lax.broadcasted_iota(jnp.int32, (rows, traces), 1)
+    first_lanes = jnp.where(place < per_shot - 1, REACH, 0)
+    last_lanes = jnp.where(place > 0, traces - REACH, traces)
+    halo = jnp.where(lane_ids < first_lanes, held(jnp.minimum(tile + 1, tiles - 1)), 0.0)
+    halo = jnp.where(lane_ids >= last_lanes, held(jnp.maximum(tile - 1, 0)), halo)
+    own = jnp.concatenate([held(tile), halo], axis=1)
     partner = swap_pairs(own)
     offsets = coefficient_ref.shape[0] // 2
     total = jnp.zeros((rows, traces), jnp.float32)
@@ -164,6 +195,14 @@
     return pl.BlockSpec(memory_space=pltpu.SMEM)
 
 
+def hbm_spec():
+    return pl.BlockSpec(memory_space=pltpu.HBM)
+
+
+def in_hbm(values):
+    return pltpu.with_memory_space_constraint(values, pltpu.HBM)
+
+
 def local(gathers, operator, filters, tile_of, slice_len):
     devices = lax.axis_size("freq")
     traces, length = gathers.shape
@@ -173,54 +212,79 @@
     group_rows = 2 * slots
     kept_bins = 5 * devices // 4
     offsets, lags = filters.shape[2], filters.shape[3]
+    chunk = length // 4
     params = pltpu.CompilerParams(vmem_limit_bytes=VMEM_LIMIT)
     table = row_tables(band_bins, length)
-    forward_high, forward_low = split_halves(table / math.sqrt(length))
+    forward_table = np.concatenate(split_halves(table / math.sqrt(length)), axis=0)
     back_high, back_low = split_halves(table)
     back_table = np.concatenate([back_high, back_high, back_low], axis=0)
+    me = lax.axis_index("freq").astype(jnp.int32)
+    place = me.reshape(1)
 
     with jax.named_scope("spectrum"):
         outgoing = pl.pallas_call(
-            spectrum_kernel,
-            out_shape=jax.ShapeDtypeStruct((devices, group_rows, traces), jnp.bfloat16),
-            in_specs=[vmem_spec()] * 3,
-            out_specs=vmem_spec(),
+            functools.partial(spectrum_kernel, chunk),
+            out_shape=[jax.ShapeDtypeStruct((group_rows, traces), jnp.bfloat16)] * devices,
+            in_specs=[smem_spec(), hbm_spec(), hbm_spec()],
+            out_specs=[vmem_spec()] * devices,
+            scratch_shapes=[
+                pltpu.VMEM((traces, length), jnp.float32),
+                pltpu.VMEM((2 * rows, length), jnp.bfloat16),
+                pltpu.VMEM((devices, group_rows, traces), jnp.float32),
+                pltpu.SemaphoreType.DMA((2, length // chunk)),
+            ],
             compiler_params=params,
             name="spectrum",
-        )(gathers, jnp.asarray(forward_high), jnp.asarray(forward_low))
-    incoming = lax.all_to_all(outgoing, "freq", split_axis=0, concat_axis=0, tiled=True)
-    with jax.named_scope("coefficients"):
-        coefficients = pl.pallas_call(
-            functools.partial(coefficient_kernel, kept_bins, slots),
-            out_shape=jax.ShapeDtypeStruct((2 * offsets, rows, traces), jnp.float32),
-            in_specs=[smem_spec(), vmem_spec(), vmem_spec()],
-            out_specs=vmem_spec(),
+        )(place, in_hbm(gathers), in_hbm(jnp.asarray(forward_table)))
+    incoming = [outgoing[0]]
+    for r in range(1, devices):
+        pairs = [(i, i ^ r) for i in range(devices)]
+        incoming.append(lax.ppermute(outgoing[r], "freq", pairs))
+    with jax.named_scope("prepare"):
+        coefficients, held = pl.pallas_call(
+            functools.partial(prepare_kernel, kept_bins, slots),
+            out_shape=[
+                jax.ShapeDtypeStruct((2 * offsets, rows, traces), jnp.float32),
+                pltpu.VMEM(operator.shape, operator.dtype),
+            ],
+            in_specs=[smem_spec(), pl.BlockSpec(memory_space=pl.ANY), vmem_spec(), vmem_spec(), hbm_spec()],
+            out_specs=[vmem_spec(), vmem_spec()],
+            scratch_shapes=[pltpu.SemaphoreType.DMA],
             compiler_params=params,
-            name="coefficients",
-        )(slice_len, filters, jnp.asarray(lag_tables(band_bins, lags, length)))
+            name="prepare",
+        )(
+            slice_len,
+            outgoing[0],
+            filters,
+            jnp.asarray(lag_tables(band_bins, lags, length)),
+            in_hbm(operator),
+        )
     with jax.named_scope("predict"):
         sending = pl.pallas_call(
-            predict_kernel,
-            out_shape=jax.ShapeDtypeStruct((devices, group_rows, 2 * traces), jnp.bfloat16),
-            in_specs=[smem_spec(), vmem_spec(), vmem_spec()],
+            functools.partial(predict_kernel, devices),
+            out_shape=jax.ShapeDtypeStruct((devices, group_rows, traces), jnp.bfloat16),
+            in_specs=[smem_spec(), smem_spec()] + [vmem_spec()] * (devices + 1),
             out_specs=vmem_spec(),
-            scratch_shapes=[
-                pltpu.SMEM((devices,), jnp.int32),
-                pltpu.VMEM((devices, group_rows, traces), jnp.float32),
-            ],
+            scratch_shapes=[pltpu.VMEM((devices, group_rows, traces), jnp.float32)],
             compiler_params=params,
             name="predict",
-        )(tile_of, incoming, operator)
-    returned = lax.all_to_all(sending, "freq", split_axis=0, concat_axis=0, tiled=True)
+        )(place, tile_of, *incoming, held)
+    returned = lax.all_gather(sending, "freq", axis=0, tiled=False)
     with jax.named_scope("subtract"):
         return pl.pallas_call(
-            subtract_kernel,
+            functools.partial(subtract_kernel, receivers // traces),
             out_shape=jax.ShapeDtypeStruct((traces, length), jnp.float32),
-            in_specs=[vmem_spec()] * 4,
+            in_specs=[smem_spec()] + [vmem_spec()] * 4,
             out_specs=vmem_spec(),
             compiler_params=params,
             name="subtract",
-        )(returned, coefficients, jnp.asarray(back_table), gathers)
+        )(
+            lax.dynamic_slice(tile_of, (me,), (1,)),
+            returned,
+            coefficients,
+            jnp.asarray(back_table),
+            gathers,
+        )
 
 
 def solution(mesh):

time: 37.1 us -> 58.3 us (1.57)
  starting transfers between devices: 3.5 us -> 23.2 us
  blocking collectives: 13.7 us -> 20.2 us
  waiting for transfers between devices: 5.41 us -> 0.04 us
  Pallas kernels: 6.9 us -> 11 us
  local copies, waits for them, and re-layouts: 7.18 us -> 3.59 us
    ppermute x0 -> x15, starting transfers between devices: none -> 23.2 us  [local(): incoming.append(lax.ppermute(outgoing[r], 'freq', pairs))]
    all_gather x0 -> x1, blocking collectives: none -> 20.2 us  [local(): returned = lax.all_gather(sending, 'freq', axis=0, tiled=False)]
    all_to_all x1 -> x0, blocking collectives: 13.7 us -> none  [local(): lax.all_to_all(outgoing, 'freq', split_axis=0, concat_axis=0, tiled=True)]
    all_to_all x1 -> x0, waiting for transfers between devices: 5.41 us -> none  [local(): lax.all_to_all(sending, 'freq', split_axis=0, concat_axis=0, tiled=True)]
    unnamed x21 -> x11, local copies, waits for them, and re-layouts: 7.18 us -> 2.34 us
    pallas_call x4, Pallas kernels: 6.9 us -> 11 us  [the longest x1 3.96 us: local(): pl.pallas_call(functools.partial(prepare_kernel, kept_bins, slots), out_s...]
    all_to_all x1 -> x0, starting transfers between devices: 3.5 us -> none  [local(): lax.all_to_all(sending, 'freq', split_axis=0, concat_axis=0, tiled=True)]
    dynamic_slice x0 -> x1, local copies, waits for them, and re-layouts: none -> 1.25 us  [local(): lax.dynamic_slice(tile_of, (me,), (1,))]
  transfers between devices with their start and end apart: 1 -> 15, of which waited for: 1 -> 0; matrix products, arithmetic and copies ran while one was open for 0% -> 3% of each run, Pallas kernels for 3% -> 7%
where the time goes in v2:
time: 58.3 us; the launch traced here: 58 us
  starting transfers between devices  23.2 us (40%)
  blocking collectives  20.2 us (35%)
  Pallas kernels  11 us (19%)
  local copies, waits for them, and re-layouts  3.59 us (6%)
    ppermute x15, starting transfers between devices, local(): incoming.append(lax.ppermute(outgoing[r], 'freq', pairs))  23.2 us
    all_gather x1, blocking collectives, local(): returned = lax.all_gather(sending, 'freq', axis=0, tiled=False)  20.2 us
    pallas_call x1, Pallas kernels, local(): pl.pallas_call(functools.partial(prepare_kernel, kept_bins, slots), out_s...  3.96 us
    pallas_call x1, Pallas kernels, local(): pl.pallas_call(functools.partial(predict_kernel, devices), out_shape=jax....  2.85 us
    unnamed x11, local copies, waits for them, and re-layouts  2.34 us
    pallas_call x1, Pallas kernels, local(): pl.pallas_call(functools.partial(subtract_kernel, receivers // traces), o...  2.22 us
    pallas_call x1, Pallas kernels, local(): pl.pallas_call(functools.partial(spectrum_kernel, chunk), out_shape=[jax....  1.93 us
    dynamic_slice x1, local copies, waits for them, and re-layouts, local(): lax.dynamic_slice(tile_of, (me,), (1,))  1.25 us
  transfers between devices with their start and end apart: 15, of which 0 were waited for; matrix products, arithmetic and copies ran while one was open for 3% of the time, Pallas kernels for 7%

profile of v2, /device:TPU:0, one launch (start us, length us, event | category | flops | bytes accessed | tf_op | source)
XLA Modules:
  0.0 58.0 jit_solution(6520743015179772118)
XLA Ops:
  0.0 1.9 %spectrum.1 = (bf16[4,128]{1,0:T(4,128)(2,1)S(1)}, bf16[4,128]{1,0:T(4,128)(2,1)S(1)}, bf16[4,128]{1,0:T(4,128)(2,1)S(1)}, bf16[4,128]{1,0:T(4,128)(2,1)S(1)}, b...) custom-call(s32[1]{0:T(128)} %bitcast.self_ref, ...), custom_call_target="tpu_custom_call" | custom-call | tf_op jit(solution)/shard_map/spectrum/spectrum/pallas_call | solution.py:225
  1.9 0.5 collective-permute-start
  2.5 2.6 %collective-permute-start.1 = (bf16[4,128]{1,0:T(4,128)(2,1)S(1)}, bf16[4,128]{1,0:T(4,128)(2,1)S(1)}, u32[]{:S(2)}, u32[]{:S(2)}) collective-permute-start(bf16[4,128]{1,0:T(4,128)(2,1)S(1)} %get-tuple-element.25), channel_id=1, source_target_pairs={{0,2},{1,3},{2,0},{3,1},{4,6},{5,7},{6,4},{7,5},{8,10},{9,11},{10,... | collective-permute-start | bytes 3080 | tf_op jit(solution)/shard_map/ppermute | solution.py:242
  5.1 2.3 %collective-permute-start.10 = (bf16[4,128]{1,0:T(4,128)(2,1)S(1)}, bf16[4,128]{1,0:T(4,128)(2,1)S(1)}, u32[]{:S(2)}, u32[]{:S(2)}) collective-permute-start(bf16[4,128]{1,0:T(4,128)(2,1)S(1)} %get-tuple-element.34), channel_id=1, source_target_pairs={{0,11},{1,10},{2,9},{3,8},{4,15},{5,14},{6,13},{7,12},{8,3},{9,2},... | collective-permute-start | bytes 3080 | tf_op jit(solution)/shard_map/ppermute | solution.py:242
  7.4 1.3 %collective-permute-start.11 = (bf16[4,128]{1,0:T(4,128)(2,1)S(1)}, bf16[4,128]{1,0:T(4,128)(2,1)S(1)}, u32[]{:S(2)}, u32[]{:S(2)}) collective-permute-start(bf16[4,128]{1,0:T(4,128)(2,1)S(1)} %get-tuple-element.35), channel_id=1, source_target_pairs={{0,12},{1,13},{2,14},{3,15},{4,8},{5,9},{6,10},{7,11},{8,4},{9,5},... | collective-permute-start | bytes 3080 | tf_op jit(solution)/shard_map/ppermute | solution.py:242
  8.7 2.1 %collective-permute-start.12 = (bf16[4,128]{1,0:T(4,128)(2,1)S(1)}, bf16[4,128]{1,0:T(4,128)(2,1)S(1)}, u32[]{:S(2)}, u32[]{:S(2)}) collective-permute-start(bf16[4,128]{1,0:T(4,128)(2,1)S(1)} %get-tuple-element.36), channel_id=1, source_target_pairs={{0,13},{1,12},{2,15},{3,14},{4,9},{5,8},{6,11},{7,10},{8,5},{9,4},... | collective-permute-start | bytes 3080 | tf_op jit(solution)/shard_map/ppermute | solution.py:242
  10.9 2.3 %collective-permute-start.13 = (bf16[4,128]{1,0:T(4,128)(2,1)S(1)}, bf16[4,128]{1,0:T(4,128)(2,1)S(1)}, u32[]{:S(2)}, u32[]{:S(2)}) collective-permute-start(bf16[4,128]{1,0:T(4,128)(2,1)S(1)} %get-tuple-element.37), channel_id=1, source_target_pairs={{0,14},{1,15},{2,12},{3,13},{4,10},{5,11},{6,8},{7,9},{8,6},{9,7},... | collective-permute-start | bytes 3080 | tf_op jit(solution)/shard_map/ppermute | solution.py:242
  13.2 0.0 collective-permute-done.1.refs_2_
  13.2 2.2 %collective-permute-start.14 = (bf16[4,128]{1,0:T(4,128)(2,1)S(1)}, bf16[4,128]{1,0:T(4,128)(2,1)S(1)}, u32[]{:S(2)}, u32[]{:S(2)}) collective-permute-start(bf16[4,128]{1,0:T(4,128)(2,1)S(1)} %get-tuple-element.38), channel_id=1, source_target_pairs={{0,15},{1,14},{2,13},{3,12},{4,11},{5,10},{6,9},{7,8},{8,7},{9,6},... | collective-permute-start | bytes 3080 | tf_op jit(solution)/shard_map/ppermute | solution.py:242
  15.4 1.5 %collective-permute-start.2 = (bf16[4,128]{1,0:T(4,128)(2,1)S(1)}, bf16[4,128]{1,0:T(4,128)(2,1)S(1)}, u32[]{:S(2)}, u32[]{:S(2)}) collective-permute-start(bf16[4,128]{1,0:T(4,128)(2,1)S(1)} %get-tuple-element.26), channel_id=1, source_target_pairs={{0,3},{1,2},{2,1},{3,0},{4,7},{5,6},{6,5},{7,4},{8,11},{9,10},{10,... | collective-permute-start | bytes 3080 | tf_op jit(solution)/shard_map/ppermute | solution.py:242
  16.8 1.5 %collective-permute-start.4 = (bf16[4,128]{1,0:T(4,128)(2,1)S(1)}, bf16[4,128]{1,0:T(4,128)(2,1)S(1)}, u32[]{:S(2)}, u32[]{:S(2)}) collective-permute-start(bf16[4,128]{1,0:T(4,128)(2,1)S(1)} %get-tuple-element.28), channel_id=1, source_target_pairs={{0,5},{1,4},{2,7},{3,6},{4,1},{5,0},{6,3},{7,2},{8,13},{9,12},{10,... | collective-permute-start | bytes 3080 | tf_op jit(solution)/shard_map/ppermute | solution.py:242
  18.4 0.5 collective-permute-start.5
  18.9 2.4 %collective-permute-start.6 = (bf16[4,128]{1,0:T(4,128)(2,1)S(1)}, bf16[4,128]{1,0:T(4,128)(2,1)S(1)}, u32[]{:S(2)}, u32[]{:S(2)}) collective-permute-start(bf16[4,128]{1,0:T(4,128)(2,1)S(1)} %get-tuple-element.30), channel_id=1, source_target_pairs={{0,7},{1,6},{2,5},{3,4},{4,3},{5,2},{6,1},{7,0},{8,15},{9,14},{10,... | collective-permute-start | bytes 3080 | tf_op jit(solution)/shard_map/ppermute | solution.py:242
  21.2 0.4 collective-permute-start.7
  21.6 2.0 %collective-permute-start.8 = (bf16[4,128]{1,0:T(4,128)(2,1)S(1)}, bf16[4,128]{1,0:T(4,128)(2,1)S(1)}, u32[]{:S(2)}, u32[]{:S(2)}) collective-permute-start(bf16[4,128]{1,0:T(4,128)(2,1)S(1)} %get-tuple-element.32), channel_id=1, source_target_pairs={{0,9},{1,8},{2,11},{3,10},{4,13},{5,12},{6,15},{7,14},{8,1},{9,0},... | collective-permute-start | bytes 3080 | tf_op jit(solution)/shard_map/ppermute | solution.py:242
  23.7 1.5 %collective-permute-start.9 = (bf16[4,128]{1,0:T(4,128)(2,1)S(1)}, bf16[4,128]{1,0:T(4,128)(2,1)S(1)}, u32[]{:S(2)}, u32[]{:S(2)}) collective-permute-start(bf16[4,128]{1,0:T(4,128)(2,1)S(1)} %get-tuple-element.33), channel_id=1, source_target_pairs={{0,10},{1,11},{2,8},{3,9},{4,14},{5,15},{6,12},{7,13},{8,2},{9,3},... | collective-permute-start | bytes 3080 | tf_op jit(solution)/shard_map/ppermute | solution.py:242
  25.2 0.7 %copy.10.filters_ref = f32[1,4,9,31]{3,2,1,0:T(8,128)S(1)} copy(f32[1,4,9,31]{3,1,2,0:T(4,128)} %param.10) | data formatting | bytes 8928 | tf_op args[2]
  25.9 1.2 %dynamic_slice.3.tile_ref = s32[1]{0:T(128)} dynamic-slice(s32[16]{0:T(128)} %tile_ref.1, s32[]{:T(128)S(6)} %select_n.3), dynamic_slice_sizes={1} | dynamic-slice | bytes 12 | tf_op jit(solution)/shard_map/subtract/dynamic_slice | solution.py:282
  27.2 0.9 %copy-done.2 = f32[4,128,31]{2,1,0:T(8,128)S(1)} copy-done((f32[4,128,31]{2,1,0:T(8,128)S(1)}, f32[4,128,31]{2,1,0:T(8,128)}, u32[]{:S(2)}) %copy-start.2) | copy-done | bytes 63512
  28.1 0.7 %copy-done.3 = s32[16]{0:T(128)S(1)} copy-done((s32[16]{0:T(128)S(1)}, s32[16]{0:T(128)}, u32[]{:S(2)}) %copy-start.3) | copy-done | bytes 88
  28.8 4.0 %prepare.1 = (f32[18,64,128]{2,1,0:T(8,128)S(1)}, bf16[2,2,1024,1024]{3,2,1,0:T(8,128)(2,1)S(1)}) custom-call(s32[16]{0:T(128)S(1)} %copy-done.3, bf16[4,128]{1,0:T(4,128)(2,1)S(1)} %get-tuple-element.23.after_ref.refs_0_, f32[1,4,9,31]{3,2,1,0:T(8,128)S(1)} %copy.10.filters_ref, f32[4,128,31]{2,1,0:T(8,128)S(1)} %copy-done.2, ...), custom_call_target="tpu_custom_call" | custom-call | tf_op jit(solution)/shard_map/prepare/prepare/pallas_call | solution.py:244
  32.8 2.8 %predict.1 = bf16[16,4,128]{2,1,0:T(4,128)(2,1)S(1)} custom-call(s32[1]{0:T(128)} %bitcast.self_ref, s32[16]{0:T(128)S(1)} %copy-done.4, bf16[4,128]{1,0:T(4,128)(2,1)S(1)} %get-tuple-element.23.after_ref.refs_0_, bf16[4,128]{1,0:T(4,128)(2,1)S(1)} %collective-permute-done.refs_1_, bf16[4,128]{1,0:T(4,128)(2,1)S(1)} %collective-permute-done.1.refs_2_, ...), custom_call_target="tpu_custom_call" | custom-call | tf_op jit(solution)/shard_map/predict/predict/pallas_call | solution.py:263
  35.6 20.2 %all-gather = bf16[256,4,128]{2,1,0:T(4,128)(2,1)S(1)} all-gather(bf16[16,4,128]{2,1,0:T(4,128)(2,1)S(1)} %predict.1), channel_id=2, replica_groups=mesh['survey'=2,'freq'=16] {'freq'}, dimensions={0}, use_global_device_ids=true | all-gather | bytes 278528 | tf_op jit(solution)/shard_map/all_gather | solution.py:272
  55.8 2.2 %subtract.1 = f32[128,2048]{1,0:T(8,128)} custom-call(s32[1]{0:T(128)} %dynamic_slice.3.tile_ref, bf16[16,16,4,128]{3,2,1,0:T(4,128)(2,1)S(1)} %bitcast.2, f32[18,64,128]{2,1,0:T(8,128)S(1)} %get-tuple-element.40.coefficient_ref, bf16[192,2048]{1,0:T(8,128)(2,1)S(1)} %copy-done.1, f32[128,2048]{1,0:T(8,128)S(1)} %copy-done), custom_call_target="tpu_custom_call" | custom-call | tf_op jit(solution)/shard_map/subtract/subtract/pallas_call | solution.py:274
  (23 shorter events, 0.1 us)
Async XLA Ops:
  0.0 32.8 %copy-start.4 = (s32[16]{0:T(128)S(1)}, s32[16]{0:T(128)}, u32[]{:S(2)}) copy-start(s32[16]{0:T(128)} %tile_ref.1) | copy-start | bytes 196
  1.9 8.9 %collective-permute-start = (bf16[4,128]{1,0:T(4,128)(2,1)S(1)}, bf16[4,128]{1,0:T(4,128)(2,1)S(1)}, u32[]{:S(2)}, u32[]{:S(2)}) collective-permute-start(bf16[4,128]{1,0:T(4,128)(2,1)S(1)} %get-tuple-element.24), channel_id=1, source_target_pairs={{0,1},{1,0},{2,3},{3,2},{4,5},{5,4},{6,7},{7,6},{8,9},{9,8},{10,11... | collective-permute-start | bytes 3080 | tf_op jit(solution)/shard_map/ppermute | solution.py:242
  2.5 10.7 %collective-permute-start.1 = (bf16[4,128]{1,0:T(4,128)(2,1)S(1)}, bf16[4,128]{1,0:T(4,128)(2,1)S(1)}, u32[]{:S(2)}, u32[]{:S(2)}) collective-permute-start(bf16[4,128]{1,0:T(4,128)(2,1)S(1)} %get-tuple-element.25), channel_id=1, source_target_pairs={{0,2},{1,3},{2,0},{3,1},{4,6},{5,7},{6,4},{7,5},{8,10},{9,11},{10,... | collective-permute-start | bytes 3080 | tf_op jit(solution)/shard_map/ppermute | solution.py:242
  5.1 10.3 %collective-permute-start.10 = (bf16[4,128]{1,0:T(4,128)(2,1)S(1)}, bf16[4,128]{1,0:T(4,128)(2,1)S(1)}, u32[]{:S(2)}, u32[]{:S(2)}) collective-permute-start(bf16[4,128]{1,0:T(4,128)(2,1)S(1)} %get-tuple-element.34), channel_id=1, source_target_pairs={{0,11},{1,10},{2,9},{3,8},{4,15},{5,14},{6,13},{7,12},{8,3},{9,2},... | collective-permute-start | bytes 3080 | tf_op jit(solution)/shard_map/ppermute | solution.py:242
  7.4 9.5 %collective-permute-start.11 = (bf16[4,128]{1,0:T(4,128)(2,1)S(1)}, bf16[4,128]{1,0:T(4,128)(2,1)S(1)}, u32[]{:S(2)}, u32[]{:S(2)}) collective-permute-start(bf16[4,128]{1,0:T(4,128)(2,1)S(1)} %get-tuple-element.35), channel_id=1, source_target_pairs={{0,12},{1,13},{2,14},{3,15},{4,8},{5,9},{6,10},{7,11},{8,4},{9,5},... | collective-permute-start | bytes 3080 | tf_op jit(solution)/shard_map/ppermute | solution.py:242
  8.7 8.1 %collective-permute-start.12 = (bf16[4,128]{1,0:T(4,128)(2,1)S(1)}, bf16[4,128]{1,0:T(4,128)(2,1)S(1)}, u32[]{:S(2)}, u32[]{:S(2)}) collective-permute-start(bf16[4,128]{1,0:T(4,128)(2,1)S(1)} %get-tuple-element.36), channel_id=1, source_target_pairs={{0,13},{1,12},{2,15},{3,14},{4,9},{5,8},{6,11},{7,10},{8,5},{9,4},... | collective-permute-start | bytes 3080 | tf_op jit(solution)/shard_map/ppermute | solution.py:242
  10.9 7.5 %collective-permute-start.13 = (bf16[4,128]{1,0:T(4,128)(2,1)S(1)}, bf16[4,128]{1,0:T(4,128)(2,1)S(1)}, u32[]{:S(2)}, u32[]{:S(2)}) collective-permute-start(bf16[4,128]{1,0:T(4,128)(2,1)S(1)} %get-tuple-element.37), channel_id=1, source_target_pairs={{0,14},{1,15},{2,12},{3,13},{4,10},{5,11},{6,8},{7,9},{8,6},{9,7},... | collective-permute-start | bytes 3080 | tf_op jit(solution)/shard_map/ppermute | solution.py:242
  13.2 5.7 %collective-permute-start.14 = (bf16[4,128]{1,0:T(4,128)(2,1)S(1)}, bf16[4,128]{1,0:T(4,128)(2,1)S(1)}, u32[]{:S(2)}, u32[]{:S(2)}) collective-permute-start(bf16[4,128]{1,0:T(4,128)(2,1)S(1)} %get-tuple-element.38), channel_id=1, source_target_pairs={{0,15},{1,14},{2,13},{3,12},{4,11},{5,10},{6,9},{7,8},{8,7},{9,6},... | collective-permute-start | bytes 3080 | tf_op jit(solution)/shard_map/ppermute | solution.py:242
  15.4 5.9 %collective-permute-start.2 = (bf16[4,128]{1,0:T(4,128)(2,1)S(1)}, bf16[4,128]{1,0:T(4,128)(2,1)S(1)}, u32[]{:S(2)}, u32[]{:S(2)}) collective-permute-start(bf16[4,128]{1,0:T(4,128)(2,1)S(1)} %get-tuple-element.26), channel_id=1, source_target_pairs={{0,3},{1,2},{2,1},{3,0},{4,7},{5,6},{6,5},{7,4},{8,11},{9,10},{10,... | collective-permute-start | bytes 3080 | tf_op jit(solution)/shard_map/ppermute | solution.py:242
  16.8 4.8 %collective-permute-start.3 = (bf16[4,128]{1,0:T(4,128)(2,1)S(1)}, bf16[4,128]{1,0:T(4,128)(2,1)S(1)}, u32[]{:S(2)}, u32[]{:S(2)}) collective-permute-start(bf16[4,128]{1,0:T(4,128)(2,1)S(1)} %get-tuple-element.27), channel_id=1, source_target_pairs={{0,4},{1,5},{2,6},{3,7},{4,0},{5,1},{6,2},{7,3},{8,12},{9,13},{10,... | collective-permute-start | bytes 3080 | tf_op jit(solution)/shard_map/ppermute | solution.py:242
  16.8 6.8 %collective-permute-start.4 = (bf16[4,128]{1,0:T(4,128)(2,1)S(1)}, bf16[4,128]{1,0:T(4,128)(2,1)S(1)}, u32[]{:S(2)}, u32[]{:S(2)}) collective-permute-start(bf16[4,128]{1,0:T(4,128)(2,1)S(1)} %get-tuple-element.28), channel_id=1, source_target_pairs={{0,5},{1,4},{2,7},{3,6},{4,1},{5,0},{6,3},{7,2},{8,13},{9,12},{10,... | collective-permute-start | bytes 3080 | tf_op jit(solution)/shard_map/ppermute | solution.py:242
  18.4 14.4 %collective-permute-start.5 = (bf16[4,128]{1,0:T(4,128)(2,1)S(1)}, bf16[4,128]{1,0:T(4,128)(2,1)S(1)}, u32[]{:S(2)}, u32[]{:S(2)}) collective-permute-start(bf16[4,128]{1,0:T(4,128)(2,1)S(1)} %get-tuple-element.29), channel_id=1, source_target_pairs={{0,6},{1,7},{2,4},{3,5},{4,2},{5,3},{6,0},{7,1},{8,14},{9,15},{10,... | collective-permute-start | bytes 3080 | tf_op jit(solution)/shard_map/ppermute | solution.py:242
  18.9 13.9 %collective-permute-start.6 = (bf16[4,128]{1,0:T(4,128)(2,1)S(1)}, bf16[4,128]{1,0:T(4,128)(2,1)S(1)}, u32[]{:S(2)}, u32[]{:S(2)}) collective-permute-start(bf16[4,128]{1,0:T(4,128)(2,1)S(1)} %get-tuple-element.30), channel_id=1, source_target_pairs={{0,7},{1,6},{2,5},{3,4},{4,3},{5,2},{6,1},{7,0},{8,15},{9,14},{10,... | collective-permute-start | bytes 3080 | tf_op jit(solution)/shard_map/ppermute | solution.py:242
  21.2 11.5 %collective-permute-start.7 = (bf16[4,128]{1,0:T(4,128)(2,1)S(1)}, bf16[4,128]{1,0:T(4,128)(2,1)S(1)}, u32[]{:S(2)}, u32[]{:S(2)}) collective-permute-start(bf16[4,128]{1,0:T(4,128)(2,1)S(1)} %get-tuple-element.31), channel_id=1, source_target_pairs={{0,8},{1,9},{2,10},{3,11},{4,12},{5,13},{6,14},{7,15},{8,0},{9,1},... | collective-permute-start | bytes 3080 | tf_op jit(solution)/shard_map/ppermute | solution.py:242
  21.6 11.1 %collective-permute-start.8 = (bf16[4,128]{1,0:T(4,128)(2,1)S(1)}, bf16[4,128]{1,0:T(4,128)(2,1)S(1)}, u32[]{:S(2)}, u32[]{:S(2)}) collective-permute-start(bf16[4,128]{1,0:T(4,128)(2,1)S(1)} %get-tuple-element.32), channel_id=1, source_target_pairs={{0,9},{1,8},{2,11},{3,10},{4,13},{5,12},{6,15},{7,14},{8,1},{9,0},... | collective-permute-start | bytes 3080 | tf_op jit(solution)/shard_map/ppermute | solution.py:242
  23.7 9.1 %collective-permute-start.9 = (bf16[4,128]{1,0:T(4,128)(2,1)S(1)}, bf16[4,128]{1,0:T(4,128)(2,1)S(1)}, u32[]{:S(2)}, u32[]{:S(2)}) collective-permute-start(bf16[4,128]{1,0:T(4,128)(2,1)S(1)} %get-tuple-element.33), channel_id=1, source_target_pairs={{0,10},{1,11},{2,8},{3,9},{4,14},{5,15},{6,12},{7,13},{8,2},{9,3},... | collective-permute-start | bytes 3080 | tf_op jit(solution)/shard_map/ppermute | solution.py:242
  27.1 0.9 %copy-start.2 = (f32[4,128,31]{2,1,0:T(8,128)S(1)}, f32[4,128,31]{2,1,0:T(8,128)}, u32[]{:S(2)}) copy-start(f32[4,128,31]{2,1,0:T(8,128)} %constant.15.clone.table_ref) | copy-start | bytes 190468
  28.1 0.7 %copy-start.3 = (s32[16]{0:T(128)S(1)}, s32[16]{0:T(128)}, u32[]{:S(2)}) copy-start(s32[16]{0:T(128)} %slice_ref.1) | copy-start | bytes 196
  28.8 27.1 %copy-start = (f32[128,2048]{1,0:T(8,128)S(1)}, f32[128,2048]{1,0:T(8,128)}, u32[]{:S(2)}) copy-start(f32[128,2048]{1,0:T(8,128)} %gathers_ref.3) | copy-start | bytes 3145732
  28.8 27.1 %copy-start.1 = (bf16[192,2048]{1,0:T(8,128)(2,1)S(1)}, bf16[192,2048]{1,0:T(8,128)(2,1)}, u32[]{:S(2)}) copy-start(bf16[192,2048]{1,0:T(8,128)(2,1)} %constant.16.clone.table_ref) | copy-start | bytes 2359300

commit v3 on v1

v3 whole, which is shorter than its diff:
```python
import functools
import math

import jax
import jax.numpy as jnp
import ml_dtypes
import numpy as np
from jax import lax
from jax.experimental import pallas as pl
from jax.experimental.pallas import tpu as pltpu
from jax.sharding import PartitionSpec as P

FIRST = 40
REACH = 4
COST = (10**11, 40_000_000)
VMEM_LIMIT = 32 * 1024 * 1024


def split_halves(values):
    values = values.astype(np.float32)
    high = values.astype(ml_dtypes.bfloat16)
    low = (values - high.astype(np.float32)).astype(ml_dtypes.bfloat16)
    return high, low


def row_tables(band_bins, length):
    bin_ids = FIRST + np.arange(band_bins)
    angles = 2.0 * np.pi / length * (bin_ids[:, None] * np.arange(length)[None, :] % length)
    return np.stack([np.cos(angles), -np.sin(angles)], axis=1).reshape(2 * band_bins, length)


def lag_tables(band_bins, lags, length):
    bin_ids = FIRST + np.arange(band_bins)
    lag_ids = np.arange(lags) - lags // 2
    angles = 2.0 * np.pi / length * (bin_ids[:, None] * lag_ids[None, :] % length)
    cosine, sine = np.cos(angles), np.sin(angles)
    weight = (bin_ids / (FIRST + band_bins))[:, None]
    real = np.stack([cosine, sine, -weight * sine, weight * cosine])
    imag = np.stack([sine, -cosine, weight * cosine, weight * sine])
    own = np.stack([real, real], axis=2).reshape(4, 2 * band_bins, lags)
    partner = np.stack([-imag, imag], axis=2).reshape(4, 2 * band_bins, lags)
    both = np.concatenate([own, partner], axis=1)
    return np.swapaxes(both, 0, 1).reshape(4 * band_bins, 4 * lags).astype(np.float32)


def split_array(values):
    high = values.astype(jnp.bfloat16)
    low = (values - high.astype(jnp.float32)).astype(jnp.bfloat16)
    return high, low


def swap_pairs(values):
    rows = values.shape[0]
    parity = lax.broadcasted_iota(jnp.int32, values.shape, 0) % 2
    return jnp.where(
        parity == 0, pltpu.roll(values, rows - 1, 0), pltpu.roll(values, 1, 0)
    )


def fill_coefficients(kept_bins, slots, counts, filters, table, out_ref):
    offsets, components, _ = filters.shape
    _, rows, width = out_ref.shape
    flat = jnp.concatenate([filters[:, part] for part in range(components)], axis=1)
    total = lax.dot_general(
        table[...],
        flat,
        (((1,), (1,)), ((), ())),
        precision=lax.Precision.HIGHEST,
        preferred_element_type=jnp.float32,
    )
    row_ids = lax.broadcasted_iota(jnp.int32, (rows, width), 0)
    group = row_ids // (2 * slots)
    slot = row_ids // 2 % slots
    count = jnp.zeros((rows, width), jnp.int32)
    for device in range(rows // (2 * slots)):
        count = jnp.where(group == device, counts[device], count)
    scale = jnp.where(slot < count, math.sqrt(2.0 / kept_bins), 0.0)
    for offset in range(offsets):
        out_ref[offset] = total[:rows, offset : offset + 1] * scale
        out_ref[offsets + offset] = total[rows:, offset : offset + 1] * scale


def spectrum_kernel(
    chunk,
    kept_bins,
    slots,
    slice_ref,
    filters_ref,
    lag_ref,
    gathers_ref,
    table_ref,
    out_ref,
    coefficient_ref,
    counts,
    filters,
    lags,
    held,
    table,
    small_sems,
    sems,
):
    length = gathers_ref.shape[1]
    rows = table_ref.shape[0] // 2
    pairs = ((slice_ref, counts), (filters_ref, filters), (lag_ref, lags))
    small = [
        pltpu.make_async_copy(source, target, small_sems.at[i])
        for i, (source, target) in enumerate(pairs)
    ]
    for copy in small:
        copy.start()
    copies = []
    for step in range(length // chunk):
        part = pl.ds(step * chunk, chunk)
        copies.append(
            (
                pltpu.make_async_copy(gathers_ref.at[:, part], held.at[:, part], sems.at[0, step]),
                pltpu.make_async_copy(table_ref.at[:, part], table.at[:, part], sems.at[1, step]),
            )
        )
    for pair in copies:
        for copy in pair:
            copy.start()
    for copy in small:
        copy.wait()
    fill_coefficients(kept_bins, slots, counts, filters, lags, coefficient_ref)
    dot = functools.partial(
        lax.dot_general,
        dimension_numbers=(((1,), (1,)), ((), ())),
        preferred_element_type=jnp.float32,
    )
    total = jnp.zeros((rows, held.shape[0]), jnp.float32)
    for step, pair in enumerate(copies):
        for copy in pair:
            copy.wait()
        part = pl.ds(step * chunk, chunk)
        high, low = split_array(held[:, part])
        weights = table[:, part]
        both = dot(weights, high)
        total = total + both[:rows] + (both[rows:] + dot(weights[:rows], low))
    out_ref[...] = total.astype(jnp.bfloat16).reshape(out_ref.shape)


def predict_kernel(tile_ref, incoming_ref, operator_ref, out_ref, spectra, tiles):
    devices, group_rows, traces = incoming_ref.shape
    slots, _, receivers, _ = operator_ref.shape
    per_shot = receivers // traces
    shots = devices // per_shot
    rows = shots * group_rows
    for k in range(devices):
        spectra[tile_ref[k]] = incoming_ref[k].astype(jnp.float32)
    columns = []
    for q in range(per_shot):
        parts = [spectra[s * per_shot + q] for s in range(shots)]
        columns.append(jnp.concatenate(parts, axis=0))
    spectrum = jnp.concatenate(columns, axis=1).astype(jnp.bfloat16)
    row_ids = lax.broadcasted_iota(jnp.int32, (rows, receivers), 0)
    dot = functools.partial(
        lax.dot_general,
        dimension_numbers=(((1,), (1,)), ((), ())),
        preferred_element_type=jnp.float32,
    )
    predicted = jnp.zeros((rows, receivers), jnp.float32)
    for slot in range(slots):
        by_real = dot(spectrum, operator_ref[slot, 0])
        by_imag = swap_pairs(dot(spectrum, operator_ref[slot, 1]))
        product = jnp.where(row_ids % 2 == 0, by_real - by_imag, by_real + by_imag)
        predicted = jnp.where(row_ids // 2 % slots == slot, product, predicted)
    for s in range(shots):
        for q in range(per_shot):
            tiles[s * per_shot + q] = predicted[
                s * group_rows : (s + 1) * group_rows, q * traces : (q + 1) * traces
            ]
    lane_ids = lax.broadcasted_iota(jnp.int32, (group_rows, traces), 1)
    for k in range(devices):
        tile = tile_ref[k]
        place = tile % per_shot
        before = tiles[jnp.maximum(tile - 1, 0)]
        after = tiles[jnp.minimum(tile + 1, devices - 1)]
        first_lanes = jnp.where(place < per_shot - 1, REACH, 0)
        last_lanes = jnp.where(place > 0, traces - REACH, traces)
        halo = jnp.where(lane_ids < first_lanes, after, 0.0)
        halo = jnp.where(lane_ids >= last_lanes, before, halo)
        out_ref[k] = jnp.concatenate([tiles[tile], halo], axis=1).astype(jnp.bfloat16)


def subtract_kernel(chunk, returned_ref, coefficient_ref, table_ref, gathers_ref, out_ref, result, sems):
    devices, group_rows, width = returned_ref.shape
    rows = devices * group_rows
    traces, length = gathers_ref.shape
    own = returned_ref[...].astype(jnp.float32).reshape(rows, width)
    partner = swap_pairs(own)
    offsets = coefficient_ref.shape[0] // 2
    total = jnp.zeros((rows, traces), jnp.float32)
    for offset in range(offsets):
        shift = (offsets // 2 - offset) % width
        moved = pltpu.roll(own, shift, 1)[:, :traces]
        moved_partner = pltpu.roll(partner, shift, 1)[:, :traces]
        total = total + coefficient_ref[offset] * moved
        total = total + coefficient_ref[offsets + offset] * moved_partner
    high, low = split_array(jnp.transpose(total))
    stacked = jnp.concatenate([high, low, high], axis=1)
    copies = []
    for step in range(length // chunk):
        part = pl.ds(step * chunk, chunk)
        response = jnp.dot(stacked, table_ref[:, part], preferred_element_type=jnp.float32)
        result[:, part] = gathers_ref[:, part] - response
        copy = pltpu.make_async_copy(result.at[:, part], out_ref.at[:, part], sems.at[step])
        copy.start()
        copies.append(copy)
    for copy in copies:
        copy.wait()


def vmem_spec():
    return pl.BlockSpec(memory_space=pltpu.VMEM)


def hbm_spec():
    return pl.BlockSpec(memory_space=pltpu.HBM)


def in_hbm(values):
    return pltpu.with_memory_space_constraint(values, pltpu.HBM)


def local(gathers, operator, filters, tile_of, slice_len):
    devices = lax.axis_size("freq")
    traces, length = gathers.shape
    slots, _, receivers, _ = operator.shape
    band_bins = slots * devices
    rows = 2 * band_bins
    group_rows = 2 * slots
    kept_bins = 5 * devices // 4
    offsets, lags = filters.shape[2], filters.shape[3]
    chunk = length // 4
    params = pltpu.CompilerParams(vmem_limit_bytes=VMEM_LIMIT)
    table = row_tables(band_bins, length)
    forward_table = np.concatenate(split_halves(table / math.sqrt(length)), axis=0)
    back_high, back_low = split_halves(table)
    back_table = np.concatenate([back_high, back_high, back_low], axis=0)
    tables = lag_tables(band_bins, lags, length)
    with jax.named_scope("spectrum"):
        outgoing, coefficients = pl.pallas_call(
            functools.partial(spectrum_kernel, chunk, kept_bins, slots),
            out_shape=[
                jax.ShapeDtypeStruct((devices, group_rows, traces), jnp.bfloat16),
                jax.ShapeDtypeStruct((2 * offsets, rows, traces), jnp.float32),
            ],
            in_specs=[hbm_spec()] * 5,
            out_specs=[vmem_spec()] * 2,
            scratch_shapes=[
                pltpu.SMEM(slice_len.shape, jnp.int32),
                pltpu.VMEM((offsets, filters.shape[1], lags), jnp.float32),
                pltpu.VMEM(tables.shape, jnp.float32),
                pltpu.VMEM((traces, length), jnp.float32),
                pltpu.VMEM((2 * rows, length), jnp.bfloat16),
                pltpu.SemaphoreType.DMA((3,)),
                pltpu.SemaphoreType.DMA((2, length // chunk)),
            ],
            compiler_params=params,
            cost_estimate=pl.CostEstimate(flops=COST[0], bytes_accessed=COST[1], transcendentals=0),
            name="spectrum",
        )(
            in_hbm(slice_len),
            in_hbm(jnp.transpose(filters[0], (1, 0, 2))),
            in_hbm(jnp.asarray(tables)),
            in_hbm(gathers),
            in_hbm(jnp.asarray(forward_table)),
        )
    incoming = lax.all_to_all(outgoing, "freq", split_axis=0, concat_axis=0, tiled=True)
    with jax.named_scope("predict"):
        sending = pl.pallas_call(
            predict_kernel,
            out_shape=jax.ShapeDtypeStruct((devices, group_rows, 2 * traces), jnp.bfloat16),
            in_specs=[pl.BlockSpec(memory_space=pltpu.SMEM), vmem_spec(), vmem_spec()],
            out_specs=vmem_spec(),
            scratch_shapes=[pltpu.VMEM((devices, group_rows, traces), jnp.float32)] * 2,
            compiler_params=params,
            name="predict",
        )(tile_of, incoming, operator)
    returned = lax.all_to_all(sending, "freq", split_axis=0, concat_axis=0, tiled=True)
    with jax.named_scope("subtract"):
        return pl.pallas_call(
            functools.partial(subtract_kernel, chunk),
            out_shape=jax.ShapeDtypeStruct((traces, length), jnp.float32),
            in_specs=[vmem_spec()] * 4,
            out_specs=hbm_spec(),
            scratch_shapes=[
                pltpu.VMEM((traces, length), jnp.float32),
                pltpu.SemaphoreType.DMA((length // chunk,)),
            ],
            compiler_params=params,
            name="subtract",
        )(returned, coefficients, jnp.asarray(back_table), gathers)


def solution(mesh):
    placed = (
        P(("survey", "freq"), None),
        P(("survey", "freq"), None, None, None),
        P(("survey", "freq"), None, None, None),
        P("survey"),
        P("survey"),
    )
    return jax.shard_map(
        local, mesh=mesh, in_specs=placed, out_specs=P(("survey", "freq"), None), check_vma=False
    )
```

time: 37.1 us -> 30.6 us (0.82)
  blocking collectives: 13.7 us -> 23 us
  local copies, waits for them, and re-layouts: 7.18 us -> 0.02 us
  waiting for transfers between devices: 5.41 us -> 0 us
  starting transfers between devices: 3.5 us -> 0 us
  Pallas kernels: 6.9 us -> 7.33 us
    all_to_all x0 -> x1, blocking collectives: none -> 9.2 us  [local(): lax.all_to_all(sending, 'freq', split_axis=0, concat_axis=0, tiled=True)]
    unnamed x21 -> x8, local copies, waits for them, and re-layouts: 7.18 us -> 0.02 us
    all_to_all x1 -> x0, waiting for transfers between devices: 5.41 us -> none  [local(): lax.all_to_all(sending, 'freq', split_axis=0, concat_axis=0, tiled=True)]
    all_to_all x1 -> x0, starting transfers between devices: 3.5 us -> none  [local(): lax.all_to_all(sending, 'freq', split_axis=0, concat_axis=0, tiled=True)]
    pallas_call x3 -> x2, Pallas kernels: 3.38 us -> 4.43 us  [the longest x1 2.93 us: local(): pl.pallas_call(functools.partial(spectrum_kernel, chunk, kept_bins, slots...]
    pallas_call x1, Pallas kernels: 3.51 us -> 2.9 us  [local(): pl.pallas_call(predict_kernel, out_shape=jax.ShapeDtypeStruct((devices, g...]
  transfers between devices with their start and end apart: 1 -> 0, of which waited for: 1 -> 0; matrix products, arithmetic and copies ran while one was open for 0% -> 0% of each run, Pallas kernels for 3% -> 0%
where the time goes in v3:
time: 30.6 us; the launch traced here: 30.4 us
  blocking collectives  23 us (75%)
  Pallas kernels  7.33 us (24%)
    all_to_all x1, blocking collectives, local(): lax.all_to_all(outgoing, 'freq', split_axis=0, concat_axis=0, tiled=True)  13.8 us
    all_to_all x1, blocking collectives, local(): lax.all_to_all(sending, 'freq', split_axis=0, concat_axis=0, tiled=True)  9.2 us
    pallas_call x1, Pallas kernels, local(): pl.pallas_call(functools.partial(spectrum_kernel, chunk, kept_bins, slots...  2.93 us
    pallas_call x1, Pallas kernels, local(): pl.pallas_call(predict_kernel, out_shape=jax.ShapeDtypeStruct((devices, g...  2.9 us
    pallas_call x1, Pallas kernels, local(): pl.pallas_call(functools.partial(subtract_kernel, chunk), out_shape=jax.S...  1.5 us

profile of v3, /device:TPU:0, one launch (start us, length us, event | category | flops | bytes accessed | tf_op | source)
XLA Modules:
  0.0 30.4 jit_solution(3738410256749971107)
XLA Ops:
  0.0 0.0 copy-start
  0.0 0.0 copy-start.3
  0.0 2.9 %spectrum.1 = (bf16[16,4,128]{2,1,0:T(4,128)(2,1)S(1)}, f32[18,64,128]{2,1,0:T(8,128)S(1)}) custom-call(s32[16]{0:T(128)} %slice_ref.1, f32[9,4,31]{2,1,0:T(4,128)} %bitcast.3, f32[128,124]{1,0:T(8,128)} %constant.6.clone.lag_ref, f32[128,2048]{1,0:T(8,128)} %gathers_ref.3, bf16[128,2048]{1,0:T(8,128)(2,1)} %constant.7.clone.table_ref), custom_call_target="tpu_custom_call" | custom-call | flops 99999997952 | bytes 40000000 | tf_op jit(solution)/shard_map/spectrum/spectrum/pallas_call | solution.py:243
  2.9 0.0 copy-start.1
  3.0 0.0 copy-start.2
  3.0 13.8 %all_to_all.10.incoming_ref = bf16[16,4,128]{2,1,0:T(4,128)(2,1)S(1)} all-to-all(bf16[16,4,128]{2,1,0:T(4,128)(2,1)S(1)} %get-tuple-element.7), channel_id=1, replica_groups=mesh['survey'=2,'freq'=16] {'freq'}, dimensions={0} | all-to-all | bytes 32768 | tf_op jit(solution)/shard_map/all_to_all | solution.py:270
  16.8 0.0 copy-done
  16.8 0.0 copy-done.3
  16.8 2.9 %predict.1 = bf16[16,4,256]{2,1,0:T(4,128)(2,1)S(1)} custom-call(s32[16]{0:T(128)S(1)} %copy-done.3, bf16[16,4,128]{2,1,0:T(4,128)(2,1)S(1)} %all_to_all.10.incoming_ref, bf16[2,2,1024,1024]{3,2,1,0:T(8,128)(2,1)S(1)} %copy-done), custom_call_target="tpu_custom_call" | custom-call | tf_op jit(solution)/shard_map/predict/predict/pallas_call | solution.py:272
  19.7 9.2 %all_to_all.11.returned_ref = bf16[16,4,256]{2,1,0:T(4,128)(2,1)S(1)} all-to-all(bf16[16,4,256]{2,1,0:T(4,128)(2,1)S(1)} %predict.1), channel_id=1, replica_groups=mesh['survey'=2,'freq'=16] {'freq'}, dimensions={0} | all-to-all | bytes 65536 | tf_op jit(solution)/shard_map/all_to_all | solution.py:281
  28.9 0.0 copy-done.1
  28.9 0.0 copy-done.2
  28.9 1.5 %subtract.1 = f32[128,2048]{1,0:T(8,128)} custom-call(bf16[16,4,256]{2,1,0:T(4,128)(2,1)S(1)} %all_to_all.11.returned_ref, f32[18,64,128]{2,1,0:T(8,128)S(1)} %get-tuple-element.8.coefficient_ref, bf16[192,2048]{1,0:T(8,128)(2,1)S(1)} %copy-done.2, f32[128,2048]{1,0:T(8,128)S(1)} %copy-done.1), custom_call_target="tpu_custom_call" | custom-call | tf_op jit(solution)/shard_map/subtract/subtract/pallas_call | solution.py:283
Async XLA Ops:
  0.0 16.8 %copy-start = (bf16[2,2,1024,1024]{3,2,1,0:T(8,128)(2,1)S(1)}, bf16[2,2,1024,1024]{3,2,1,0:T(8,128)(2,1)}, u32[]{:S(2)}) copy-start(bf16[2,2,1024,1024]{3,2,1,0:T(8,128)(2,1)} %operator_ref.1) | copy-start | bytes 25165828
  0.0 16.8 %copy-start.3 = (s32[16]{0:T(128)S(1)}, s32[16]{0:T(128)}, u32[]{:S(2)}) copy-start(s32[16]{0:T(128)} %tile_ref.1) | copy-start | bytes 196
  2.9 26.0 %copy-start.1 = (f32[128,2048]{1,0:T(8,128)S(1)}, f32[128,2048]{1,0:T(8,128)}, u32[]{:S(2)}) copy-start(f32[128,2048]{1,0:T(8,128)} %gathers_ref.3) | copy-start | bytes 3145732
  3.0 25.9 %copy-start.2 = (bf16[192,2048]{1,0:T(8,128)(2,1)S(1)}, bf16[192,2048]{1,0:T(8,128)(2,1)}, u32[]{:S(2)}) copy-start(bf16[192,2048]{1,0:T(8,128)(2,1)} %constant.8.clone.table_ref) | copy-start | bytes 2359300

commit v4 on v3

v4 whole, which is shorter than its diff:
```python
import functools
import math

import jax
import jax.numpy as jnp
import ml_dtypes
import numpy as np
from jax import lax
from jax.experimental import pallas as pl
from jax.experimental.pallas import tpu as pltpu
from jax.sharding import PartitionSpec as P

FIRST = 40
REACH = 4
COST = (10**11, 40_000_000)
VMEM_LIMIT = 32 * 1024 * 1024


def split_halves(values):
    values = values.astype(np.float32)
    high = values.astype(ml_dtypes.bfloat16)
    low = (values - high.astype(np.float32)).astype(ml_dtypes.bfloat16)
    return high, low


def row_tables(band_bins, length):
    bin_ids = FIRST + np.arange(band_bins)
    angles = 2.0 * np.pi / length * (bin_ids[:, None] * np.arange(length)[None, :] % length)
    return np.stack([np.cos(angles), -np.sin(angles)], axis=1).reshape(2 * band_bins, length)


def lag_tables(band_bins, lags, length):
    bin_ids = FIRST + np.arange(band_bins)
    lag_ids = np.arange(lags) - lags // 2
    angles = 2.0 * np.pi / length * (bin_ids[:, None] * lag_ids[None, :] % length)
    cosine, sine = np.cos(angles), np.sin(angles)
    weight = (bin_ids / (FIRST + band_bins))[:, None]
    real = np.stack([cosine, sine, -weight * sine, weight * cosine])
    imag = np.stack([sine, -cosine, weight * cosine, weight * sine])
    own = np.stack([real, real], axis=2).reshape(4, 2 * band_bins, lags)
    partner = np.stack([-imag, imag], axis=2).reshape(4, 2 * band_bins, lags)
    both = np.concatenate([own, partner], axis=1)
    return np.swapaxes(both, 1, 2).reshape(4 * lags, 4 * band_bins).astype(np.float32)


def split_array(values):
    high = values.astype(jnp.bfloat16)
    low = (values - high.astype(jnp.float32)).astype(jnp.bfloat16)
    return high, low


def swap_pairs(values):
    rows = values.shape[0]
    parity = lax.broadcasted_iota(jnp.int32, values.shape, 0) % 2
    return jnp.where(
        parity == 0, pltpu.roll(values, rows - 1, 0), pltpu.roll(values, 1, 0)
    )


def filter_lanes(kept_bins, slots, slice_ref, filters_ref, lag_ref):
    _, components, _ = filters_ref.shape
    lanes = lag_ref.shape[1]
    rows = lanes // 2
    flat = jnp.concatenate([filters_ref[:, part] for part in range(components)], axis=1)
    total = jnp.dot(
        flat, lag_ref[...], precision=lax.Precision.HIGHEST, preferred_element_type=jnp.float32
    )
    lane_ids = lax.broadcasted_iota(jnp.int32, (1, lanes), 1) % rows
    group = lane_ids // (2 * slots)
    slot = lane_ids // 2 % slots
    count = jnp.zeros((1, lanes), jnp.int32)
    for device in range(rows // (2 * slots)):
        count = jnp.where(group == device, slice_ref[device], count)
    return total * jnp.where(slot < count, math.sqrt(2.0 / kept_bins), 0.0)


def spectrum_kernel(chunk, gathers_ref, table_ref, out_ref, held, table, sems):
    length = gathers_ref.shape[1]
    rows = table_ref.shape[0] // 2
    copies = []
    for step in range(length // chunk):
        part = pl.ds(step * chunk, chunk)
        copies.append(
            (
                pltpu.make_async_copy(gathers_ref.at[:, part], held.at[:, part], sems.at[0, step]),
                pltpu.make_async_copy(table_ref.at[:, part], table.at[:, part], sems.at[1, step]),
            )
        )
    for pair in copies:
        for copy in pair:
            copy.start()
    dot = functools.partial(
        lax.dot_general,
        dimension_numbers=(((1,), (1,)), ((), ())),
        preferred_element_type=jnp.float32,
    )
    total = jnp.zeros((rows, held.shape[0]), jnp.float32)
    for step, pair in enumerate(copies):
        for copy in pair:
            copy.wait()
        part = pl.ds(step * chunk, chunk)
        high, low = split_array(held[:, part])
        weights = table[:, part]
        both = dot(weights, high)
        total = total + both[:rows] + (both[rows:] + dot(weights[:rows], low))
    out_ref[...] = total.astype(jnp.bfloat16).reshape(out_ref.shape)


def predict_kernel(
    kept_bins,
    tile_ref,
    slice_ref,
    filters_ref,
    lag_ref,
    incoming_ref,
    operator_ref,
    out_ref,
    coefficient_ref,
    holder,
):
    devices, group_rows, traces = incoming_ref.shape
    slots, _, receivers, _ = operator_ref.shape
    per_shot = receivers // traces
    shots = devices // per_shot
    rows = shots * group_rows
    for k in range(devices):
        holder[tile_ref[k]] = k
    columns = []
    for q in range(per_shot):
        parts = [
            incoming_ref[holder[s * per_shot + q]].astype(jnp.float32) for s in range(shots)
        ]
        columns.append(jnp.concatenate(parts, axis=0))
    spectrum = jnp.concatenate(columns, axis=1).astype(jnp.bfloat16)
    row_ids = lax.broadcasted_iota(jnp.int32, (rows, receivers), 0)
    dot = functools.partial(
        lax.dot_general,
        dimension_numbers=(((1,), (1,)), ((), ())),
        preferred_element_type=jnp.float32,
    )
    predicted = jnp.zeros((rows, receivers), jnp.float32)
    for slot in range(slots):
        by_real = dot(spectrum, operator_ref[slot, 0])
        by_imag = swap_pairs(dot(spectrum, operator_ref[slot, 1]))
        product = jnp.where(row_ids % 2 == 0, by_real - by_imag, by_real + by_imag)
        predicted = jnp.where(row_ids // 2 % slots == slot, product, predicted)
    lane_ids = lax.broadcasted_iota(jnp.int32, (rows, receivers), 1) % traces
    edge = jnp.zeros((rows, traces), jnp.float32)
    after = jnp.concatenate([predicted[:, traces:], edge], axis=1)
    before = jnp.concatenate([edge, predicted[:, :-traces]], axis=1)
    halo = jnp.where(lane_ids < REACH, after, jnp.where(lane_ids >= traces - REACH, before, 0.0))
    for s in range(shots):
        for q in range(per_shot):
            where = (slice(s * group_rows, (s + 1) * group_rows), slice(q * traces, (q + 1) * traces))
            both = jnp.concatenate([predicted[where], halo[where]], axis=1)
            out_ref[holder[s * per_shot + q]] = both.astype(jnp.bfloat16)
    coefficient_ref[...] = filter_lanes(kept_bins, slots, slice_ref, filters_ref, lag_ref)


def subtract_kernel(
    chunk, returned_ref, coefficient_ref, table_ref, gathers_ref, out_ref, spread, result, sems
):
    devices, group_rows, _ = returned_ref.shape
    rows = devices * group_rows
    traces, length = gathers_ref.shape
    offsets = coefficient_ref.shape[0]
    own = returned_ref[...].astype(jnp.float32).reshape(rows, 2 * traces)
    both = jnp.concatenate([own, swap_pairs(own)], axis=0)
    halo = jnp.transpose(both[:, traces:])
    spread[0:8] = halo[traces - 8 :]
    spread[8 : 8 + traces] = jnp.transpose(both[:, :traces])
    spread[8 + traces : 16 + traces] = halo[:8]
    total = jnp.zeros((traces, 2 * rows), jnp.float32)
    for offset in range(offsets):
        first = 8 + offset - offsets // 2
        total = total + spread[first : first + traces] * coefficient_ref[offset : offset + 1]
    total = total + pltpu.roll(total, rows, 1)
    high = total.astype(jnp.bfloat16).astype(jnp.float32)
    lane_ids = lax.broadcasted_iota(jnp.int32, total.shape, 1)
    mixed = jnp.where(lane_ids < rows, high, total - high)
    stacked = jnp.concatenate([mixed, high[:, :rows]], axis=1).astype(jnp.bfloat16)
    copies = []
    for step in range(length // chunk):
        part = pl.ds(step * chunk, chunk)
        response = jnp.dot(stacked, table_ref[:, part], preferred_element_type=jnp.float32)
        result[:, part] = gathers_ref[:, part] - response
        copy = pltpu.make_async_copy(result.at[:, part], out_ref.at[:, part], sems.at[step])
        copy.start()
        copies.append(copy)
    for copy in copies:
        copy.wait()


def vmem_spec():
    return pl.BlockSpec(memory_space=pltpu.VMEM)


def smem_spec():
    return pl.BlockSpec(memory_space=pltpu.SMEM)


def hbm_spec():
    return pl.BlockSpec(memory_space=pltpu.HBM)


def in_hbm(values):
    return pltpu.with_memory_space_constraint(values, pltpu.HBM)


def local(gathers, operator, filters, tile_of, slice_len):
    devices = lax.axis_size("freq")
    traces, length = gathers.shape
    slots, _, receivers, _ = operator.shape
    band_bins = slots * devices
    rows = 2 * band_bins
    group_rows = 2 * slots
    kept_bins = 5 * devices // 4
    offsets, lags = filters.shape[2], filters.shape[3]
    chunk = length // 4
    params = pltpu.CompilerParams(vmem_limit_bytes=VMEM_LIMIT)
    table = row_tables(band_bins, length)
    forward_table = np.concatenate(split_halves(table / math.sqrt(length)), axis=0)
    back_high, back_low = split_halves(table)
    back_table = np.concatenate([back_high, back_high, back_low], axis=0)
    tables = lag_tables(band_bins, lags, length)
    with jax.named_scope("spectrum"):
        outgoing = pl.pallas_call(
            functools.partial(spectrum_kernel, chunk),
            out_shape=jax.ShapeDtypeStruct((devices, group_rows, traces), jnp.bfloat16),
            in_specs=[hbm_spec()] * 2,
            out_specs=vmem_spec(),
            scratch_shapes=[
                pltpu.VMEM((traces, length), jnp.float32),
                pltpu.VMEM((2 * rows, length), jnp.bfloat16),
                pltpu.SemaphoreType.DMA((2, length // chunk)),
            ],
            compiler_params=params,
            cost_estimate=pl.CostEstimate(flops=COST[0], bytes_accessed=COST[1], transcendentals=0),
            name="spectrum",
        )(in_hbm(gathers), in_hbm(jnp.asarray(forward_table)))
    incoming = lax.all_to_all(outgoing, "freq", split_axis=0, concat_axis=0, tiled=True)
    with jax.named_scope("predict"):
        sending, coefficients = pl.pallas_call(
            functools.partial(predict_kernel, kept_bins),
            out_shape=[
                jax.ShapeDtypeStruct((devices, group_rows, 2 * traces), jnp.bfloat16),
                jax.ShapeDtypeStruct((offsets, 2 * rows), jnp.float32),
            ],
            in_specs=[smem_spec()] * 2 + [vmem_spec()] * 4,
            out_specs=[vmem_spec()] * 2,
            scratch_shapes=[pltpu.SMEM((devices,), jnp.int32)],
            compiler_params=params,
            name="predict",
        )(
            tile_of,
            slice_len,
            jnp.transpose(filters[0], (1, 0, 2)),
            jnp.asarray(tables),
            incoming,
            operator,
        )
    returned = lax.all_to_all(sending, "freq", split_axis=0, concat_axis=0, tiled=True)
    with jax.named_scope("subtract"):
        return pl.pallas_call(
            functools.partial(subtract_kernel, length // 8),
            out_shape=jax.ShapeDtypeStruct((traces, length), jnp.float32),
            in_specs=[vmem_spec()] * 4,
            out_specs=hbm_spec(),
            scratch_shapes=[
                pltpu.VMEM((traces + 16, 2 * rows), jnp.float32),
                pltpu.VMEM((traces, length), jnp.float32),
                pltpu.SemaphoreType.DMA((8,)),
            ],
            compiler_params=params,
            name="subtract",
        )(returned, coefficients, jnp.asarray(back_table), gathers)


def solution(mesh):
    placed = (
        P(("survey", "freq"), None),
        P(("survey", "freq"), None, None, None),
        P(("survey", "freq"), None, None, None),
        P("survey"),
        P("survey"),
    )
    return jax.shard_map(
        local, mesh=mesh, in_specs=placed, out_specs=P(("survey", "freq"), None), check_vma=False
    )
```

time: 30.6 us -> 29.8 us (0.974)
  Pallas kernels: 7.33 us -> 6.39 us
    pallas_call x3, Pallas kernels: 7.33 us -> 6.39 us  [the longest x1 2.91 us: local(): pl.pallas_call(functools.partial(predict_kernel, kept_bins), out_shape=[j...]
where the time goes in v4:
time: 29.8 us; the launch traced here: 29.7 us
  blocking collectives  23.2 us (78%)
  Pallas kernels  6.39 us (21%)
    all_to_all x1, blocking collectives, local(): lax.all_to_all(outgoing, 'freq', split_axis=0, concat_axis=0, tiled=True)  14 us
    all_to_all x1, blocking collectives, local(): lax.all_to_all(sending, 'freq', split_axis=0, concat_axis=0, tiled=True)  9.2 us
    pallas_call x1, Pallas kernels, local(): pl.pallas_call(functools.partial(predict_kernel, kept_bins), out_shape=[j...  2.91 us
    pallas_call x1, Pallas kernels, local(): pl.pallas_call(functools.partial(spectrum_kernel, chunk), out_shape=jax.S...  2.07 us
    pallas_call x1, Pallas kernels, local(): pl.pallas_call(functools.partial(subtract_kernel, length // 8), out_shape...  1.41 us

profile of v4, /device:TPU:0, one launch (start us, length us, event | category | flops | bytes accessed | tf_op | source)
XLA Modules:
  0.0 29.7 jit_solution(5307347640840164273)
XLA Ops:
  0.0 0.0 copy-start.3
  0.0 0.0 copy-start.6
  0.0 0.0 copy-start.5
  0.0 0.0 copy-start.4
  0.0 0.0 copy-start
  0.0 2.1 %spectrum.1 = bf16[16,4,128]{2,1,0:T(4,128)(2,1)S(1)} custom-call(f32[128,2048]{1,0:T(8,128)} %gathers_ref.3, bf16[128,2048]{1,0:T(8,128)(2,1)} %constant.6.clone.table_ref), custom_call_target="tpu_custom_call" | custom-call | flops 99999997952 | bytes 40000000 | tf_op jit(solution)/shard_map/spectrum/spectrum/pallas_call | solution.py:227
  2.1 0.0 copy-start.1
  2.1 0.0 copy-start.2
  2.1 14.0 %all_to_all.10.incoming_ref = bf16[16,4,128]{2,1,0:T(4,128)(2,1)S(1)} all-to-all(bf16[16,4,128]{2,1,0:T(4,128)(2,1)S(1)} %spectrum.1), channel_id=1, replica_groups=mesh['survey'=2,'freq'=16] {'freq'}, dimensions={0} | all-to-all | bytes 32768 | tf_op jit(solution)/shard_map/all_to_all | solution.py:241
  16.1 0.0 copy-done.3
  16.1 0.0 copy-done.6
  16.1 0.0 copy-done.5
  16.1 0.0 copy-done.4
  16.1 0.0 copy-done
  16.1 2.9 %predict.1 = (bf16[16,4,256]{2,1,0:T(4,128)(2,1)S(1)}, f32[9,128]{1,0:T(8,128)S(1)}) custom-call(s32[16]{0:T(128)S(1)} %copy-done.5, s32[16]{0:T(128)S(1)} %copy-done.6, f32[9,4,31]{2,1,0:T(4,128)S(1)} %bitcast.3, f32[124,128]{1,0:T(8,128)S(1)} %copy-done.3, bf16[16,4,128]{2,1,0:T(4,128)(2,1)S(1)} %all_to_all.10.incoming_ref, ...), custom_call_target="tpu_custom_call" | custom-call | tf_op jit(solution)/shard_map/predict/predict/pallas_call | solution.py:243
  19.0 9.2 %all_to_all.11.returned_ref = bf16[16,4,256]{2,1,0:T(4,128)(2,1)S(1)} all-to-all(bf16[16,4,256]{2,1,0:T(4,128)(2,1)S(1)} %get-tuple-element.7), channel_id=1, replica_groups=mesh['survey'=2,'freq'=16] {'freq'}, dimensions={0} | all-to-all | bytes 65536 | tf_op jit(solution)/shard_map/all_to_all | solution.py:262
  28.2 0.0 copy-done.1
  28.2 0.0 copy-done.2
  28.2 1.4 %subtract.1 = f32[128,2048]{1,0:T(8,128)} custom-call(bf16[16,4,256]{2,1,0:T(4,128)(2,1)S(1)} %all_to_all.11.returned_ref, f32[9,128]{1,0:T(8,128)S(1)} %get-tuple-element.8.coefficient_ref, bf16[192,2048]{1,0:T(8,128)(2,1)S(1)} %copy-done.2, f32[128,2048]{1,0:T(8,128)S(1)} %copy-done.1), custom_call_target="tpu_custom_call" | custom-call | tf_op jit(solution)/shard_map/subtract/subtract/pallas_call | solution.py:264
Async XLA Ops:
  0.0 16.1 %copy-start.3 = (f32[124,128]{1,0:T(8,128)S(1)}, f32[124,128]{1,0:T(8,128)}, u32[]{:S(2)}) copy-start(f32[124,128]{1,0:T(8,128)} %constant.7.clone.lag_ref) | copy-start | bytes 190468
  0.0 16.1 %copy-start.6 = (s32[16]{0:T(128)S(1)}, s32[16]{0:T(128)}, u32[]{:S(2)}) copy-start(s32[16]{0:T(128)} %slice_ref.1) | copy-start | bytes 196
  0.0 16.1 %copy-start.5 = (s32[16]{0:T(128)S(1)}, s32[16]{0:T(128)}, u32[]{:S(2)}) copy-start(s32[16]{0:T(128)} %tile_ref.1) | copy-start | bytes 196
  0.0 16.1 %copy-start.4 = (f32[1,4,9,31]{3,1,2,0:T(4,128)S(1)}, f32[1,4,9,31]{3,1,2,0:T(4,128)}, u32[]{:S(2)}) copy-start(f32[1,4,9,31]{3,1,2,0:T(4,128)} %param.10) | copy-start | bytes 13396
  0.0 16.1 %copy-start = (bf16[2,2,1024,1024]{3,2,1,0:T(8,128)(2,1)S(1)}, bf16[2,2,1024,1024]{3,2,1,0:T(8,128)(2,1)}, u32[]{:S(2)}) copy-start(bf16[2,2,1024,1024]{3,2,1,0:T(8,128)(2,1)} %operator_ref.1) | copy-start | bytes 25165828
  2.1 26.1 %copy-start.1 = (f32[128,2048]{1,0:T(8,128)S(1)}, f32[128,2048]{1,0:T(8,128)}, u32[]{:S(2)}) copy-start(f32[128,2048]{1,0:T(8,128)} %gathers_ref.3) | copy-start | bytes 3145732
  2.1 26.1 %copy-start.2 = (bf16[192,2048]{1,0:T(8,128)(2,1)S(1)}, bf16[192,2048]{1,0:T(8,128)(2,1)}, u32[]{:S(2)}) copy-start(bf16[192,2048]{1,0:T(8,128)(2,1)} %constant.8.clone.table_ref) | copy-start | bytes 2359300

commit v5 on v4

--- a/solution.py
+++ b/solution.py
@@ -131,19 +131,20 @@
             incoming_ref[holder[s * per_shot + q]].astype(jnp.float32) for s in range(shots)
         ]
         columns.append(jnp.concatenate(parts, axis=0))
-    spectrum = jnp.concatenate(columns, axis=1).astype(jnp.bfloat16)
+    spectrum = jnp.concatenate(columns, axis=1)
     row_ids = lax.broadcasted_iota(jnp.int32, (rows, receivers), 0)
-    dot = functools.partial(
-        lax.dot_general,
-        dimension_numbers=(((1,), (1,)), ((), ())),
-        preferred_element_type=jnp.float32,
-    )
-    predicted = jnp.zeros((rows, receivers), jnp.float32)
+    partner = swap_pairs(spectrum)
+    partner = jnp.where(row_ids % 2 == 0, -partner, partner)
+    sides = [jnp.transpose(spectrum), jnp.transpose(partner)]
+    column_ids = lax.broadcasted_iota(jnp.int32, (receivers, rows), 1)
+    turned = jnp.zeros((receivers, rows), jnp.float32)
     for slot in range(slots):
-        by_real = dot(spectrum, operator_ref[slot, 0])
-        by_imag = swap_pairs(dot(spectrum, operator_ref[slot, 1]))
-        product = jnp.where(row_ids % 2 == 0, by_real - by_imag, by_real + by_imag)
-        predicted = jnp.where(row_ids // 2 % slots == slot, product, predicted)
+        for part in range(2):
+            side = jnp.where(column_ids // 2 % slots == slot, sides[part], 0.0).astype(jnp.bfloat16)
+            turned = turned + jnp.dot(
+                operator_ref[slot, part], side, preferred_element_type=jnp.float32
+            )
+    predicted = jnp.transpose(turned)
     lane_ids = lax.broadcasted_iota(jnp.int32, (rows, receivers), 1) % traces
     edge = jnp.zeros((rows, traces), jnp.float32)
     after = jnp.concatenate([predicted[:, traces:], edge], axis=1)
@@ -216,7 +217,7 @@
     group_rows = 2 * slots
     kept_bins = 5 * devices // 4
     offsets, lags = filters.shape[2], filters.shape[3]
-    chunk = length // 4
+    chunk = length // 8
     params = pltpu.CompilerParams(vmem_limit_bytes=VMEM_LIMIT)
     table = row_tables(band_bins, length)
     forward_table = np.concatenate(split_halves(table / math.sqrt(length)), axis=0)
@@ -262,14 +263,14 @@
     returned = lax.all_to_all(sending, "freq", split_axis=0, concat_axis=0, tiled=True)
     with jax.named_scope("subtract"):
         return pl.pallas_call(
-            functools.partial(subtract_kernel, length // 8),
+            functools.partial(subtract_kernel, length // 4),
             out_shape=jax.ShapeDtypeStruct((traces, length), jnp.float32),
             in_specs=[vmem_spec()] * 4,
             out_specs=hbm_spec(),
             scratch_shapes=[
                 pltpu.VMEM((traces + 16, 2 * rows), jnp.float32),
                 pltpu.VMEM((traces, length), jnp.float32),
-                pltpu.SemaphoreType.DMA((8,)),
+                pltpu.SemaphoreType.DMA((4,)),
             ],
             compiler_params=params,
             name="subtract",

time: 29.8 us -> 30.1 us (1.010)
  no operation moved by 1% of the time
where the time goes in v5:
time: 30.1 us; the launch traced here: 29.8 us
  blocking collectives  23.2 us (77%)
  Pallas kernels  6.59 us (22%)
    all_to_all x1, blocking collectives, local(): lax.all_to_all(outgoing, 'freq', split_axis=0, concat_axis=0, tiled=True)  14 us
    all_to_all x1, blocking collectives, local(): lax.all_to_all(sending, 'freq', split_axis=0, concat_axis=0, tiled=True)  9.2 us
    pallas_call x1, Pallas kernels, local(): pl.pallas_call(functools.partial(predict_kernel, kept_bins), out_shape=[j...  3.07 us
    pallas_call x1, Pallas kernels, local(): pl.pallas_call(functools.partial(spectrum_kernel, chunk), out_shape=jax.S...  2.15 us
    pallas_call x1, Pallas kernels, local(): pl.pallas_call(functools.partial(subtract_kernel, length // 4), out_shape...  1.36 us

profile of v5, /device:TPU:0, one launch (start us, length us, event | category | flops | bytes accessed | tf_op | source)
XLA Modules:
  0.0 29.8 jit_solution(4176749992912978616)
XLA Ops:
  0.0 0.0 copy-start.3
  0.0 0.0 copy-start.6
  0.0 0.0 copy-start.5
  0.0 0.0 copy-start.4
  0.0 0.0 copy-start
  0.0 2.1 %spectrum.1 = bf16[16,4,128]{2,1,0:T(4,128)(2,1)S(1)} custom-call(f32[128,2048]{1,0:T(8,128)} %gathers_ref.3, bf16[128,2048]{1,0:T(8,128)(2,1)} %constant.6.clone.table_ref), custom_call_target="tpu_custom_call" | custom-call | flops 99999997952 | bytes 40000000 | tf_op jit(solution)/shard_map/spectrum/spectrum/pallas_call | solution.py:228
  2.2 0.0 copy-start.1
  2.2 0.0 copy-start.2
  2.2 14.0 %all_to_all.10.incoming_ref = bf16[16,4,128]{2,1,0:T(4,128)(2,1)S(1)} all-to-all(bf16[16,4,128]{2,1,0:T(4,128)(2,1)S(1)} %spectrum.1), channel_id=1, replica_groups=mesh['survey'=2,'freq'=16] {'freq'}, dimensions={0} | all-to-all | bytes 32768 | tf_op jit(solution)/shard_map/all_to_all | solution.py:242
  16.2 0.0 copy-done.3
  16.2 0.0 copy-done.6
  16.2 0.0 copy-done.5
  16.2 0.0 copy-done.4
  16.2 0.0 copy-done
  16.2 3.1 %predict.1 = (bf16[16,4,256]{2,1,0:T(4,128)(2,1)S(1)}, f32[9,128]{1,0:T(8,128)S(1)}) custom-call(s32[16]{0:T(128)S(1)} %copy-done.5, s32[16]{0:T(128)S(1)} %copy-done.6, f32[9,4,31]{2,1,0:T(4,128)S(1)} %bitcast.3, f32[124,128]{1,0:T(8,128)S(1)} %copy-done.3, bf16[16,4,128]{2,1,0:T(4,128)(2,1)S(1)} %all_to_all.10.incoming_ref, ...), custom_call_target="tpu_custom_call" | custom-call | tf_op jit(solution)/shard_map/predict/predict/pallas_call | solution.py:244
  19.3 9.2 %all_to_all.11.returned_ref = bf16[16,4,256]{2,1,0:T(4,128)(2,1)S(1)} all-to-all(bf16[16,4,256]{2,1,0:T(4,128)(2,1)S(1)} %get-tuple-element.7), channel_id=1, replica_groups=mesh['survey'=2,'freq'=16] {'freq'}, dimensions={0} | all-to-all | bytes 65536 | tf_op jit(solution)/shard_map/all_to_all | solution.py:263
  28.5 0.0 copy-done.1
  28.5 0.0 copy-done.2
  28.5 1.4 %subtract.1 = f32[128,2048]{1,0:T(8,128)} custom-call(bf16[16,4,256]{2,1,0:T(4,128)(2,1)S(1)} %all_to_all.11.returned_ref, f32[9,128]{1,0:T(8,128)S(1)} %get-tuple-element.8.coefficient_ref, bf16[192,2048]{1,0:T(8,128)(2,1)S(1)} %copy-done.2, f32[128,2048]{1,0:T(8,128)S(1)} %copy-done.1), custom_call_target="tpu_custom_call" | custom-call | tf_op jit(solution)/shard_map/subtract/subtract/pallas_call | solution.py:265
Async XLA Ops:
  0.0 16.2 %copy-start.3 = (f32[124,128]{1,0:T(8,128)S(1)}, f32[124,128]{1,0:T(8,128)}, u32[]{:S(2)}) copy-start(f32[124,128]{1,0:T(8,128)} %constant.7.clone.lag_ref) | copy-start | bytes 190468
  0.0 16.2 %copy-start.6 = (s32[16]{0:T(128)S(1)}, s32[16]{0:T(128)}, u32[]{:S(2)}) copy-start(s32[16]{0:T(128)} %slice_ref.1) | copy-start | bytes 196
  0.0 16.2 %copy-start.5 = (s32[16]{0:T(128)S(1)}, s32[16]{0:T(128)}, u32[]{:S(2)}) copy-start(s32[16]{0:T(128)} %tile_ref.1) | copy-start | bytes 196
  0.0 16.2 %copy-start.4 = (f32[1,4,9,31]{3,1,2,0:T(4,128)S(1)}, f32[1,4,9,31]{3,1,2,0:T(4,128)}, u32[]{:S(2)}) copy-start(f32[1,4,9,31]{3,1,2,0:T(4,128)} %param.10) | copy-start | bytes 13396
  0.0 16.2 %copy-start = (bf16[2,2,1024,1024]{3,2,1,0:T(8,128)(2,1)S(1)}, bf16[2,2,1024,1024]{3,2,1,0:T(8,128)(2,1)}, u32[]{:S(2)}) copy-start(bf16[2,2,1024,1024]{3,2,1,0:T(8,128)(2,1)} %operator_ref.1) | copy-start | bytes 25165828
  2.2 26.3 %copy-start.1 = (f32[128,2048]{1,0:T(8,128)S(1)}, f32[128,2048]{1,0:T(8,128)}, u32[]{:S(2)}) copy-start(f32[128,2048]{1,0:T(8,128)} %gathers_ref.3) | copy-start | bytes 3145732
  2.2 26.3 %copy-start.2 = (bf16[192,2048]{1,0:T(8,128)(2,1)S(1)}, bf16[192,2048]{1,0:T(8,128)(2,1)}, u32[]{:S(2)}) copy-start(bf16[192,2048]{1,0:T(8,128)(2,1)} %constant.8.clone.table_ref) | copy-start | bytes 2359300

commit v6 on v4

--- a/solution.py
+++ b/solution.py
@@ -23,14 +23,18 @@
     return high, low
 
 
-def row_tables(band_bins, length):
-    bin_ids = FIRST + np.arange(band_bins)
+def bins_in_order(band_bins, slots):
+    return FIRST + np.arange(band_bins).reshape(-1, slots)[::-1].reshape(-1)
+
+
+def row_tables(band_bins, slots, length):
+    bin_ids = bins_in_order(band_bins, slots)
     angles = 2.0 * np.pi / length * (bin_ids[:, None] * np.arange(length)[None, :] % length)
     return np.stack([np.cos(angles), -np.sin(angles)], axis=1).reshape(2 * band_bins, length)
 
 
-def lag_tables(band_bins, lags, length):
-    bin_ids = FIRST + np.arange(band_bins)
+def lag_tables(band_bins, slots, lags, length):
+    bin_ids = bins_in_order(band_bins, slots)
     lag_ids = np.arange(lags) - lags // 2
     angles = 2.0 * np.pi / length * (bin_ids[:, None] * lag_ids[None, :] % length)
     cosine, sine = np.cos(angles), np.sin(angles)
@@ -69,8 +73,9 @@
     group = lane_ids // (2 * slots)
     slot = lane_ids // 2 % slots
     count = jnp.zeros((1, lanes), jnp.int32)
-    for device in range(rows // (2 * slots)):
-        count = jnp.where(group == device, slice_ref[device], count)
+    devices = rows // (2 * slots)
+    for device in range(devices):
+        count = jnp.where(group == devices - 1 - device, slice_ref[device], count)
     return total * jnp.where(slot < count, math.sqrt(2.0 / kept_bins), 0.0)
 
 
@@ -124,7 +129,7 @@
     shots = devices // per_shot
     rows = shots * group_rows
     for k in range(devices):
-        holder[tile_ref[k]] = k
+        holder[tile_ref[k]] = devices - 1 - k
     columns = []
     for q in range(per_shot):
         parts = [
@@ -207,6 +212,11 @@
     return pltpu.with_memory_space_constraint(values, pltpu.HBM)
 
 
+def exchange(chunks):
+    order = list(range(chunks.shape[0]))[::-1]
+    return lax.all_to_all(chunks, "freq", 0, 0, axis_index_groups=[order], tiled=True)
+
+
 def local(gathers, operator, filters, tile_of, slice_len):
     devices = lax.axis_size("freq")
     traces, length = gathers.shape
@@ -218,11 +228,11 @@
     offsets, lags = filters.shape[2], filters.shape[3]
     chunk = length // 4
     params = pltpu.CompilerParams(vmem_limit_bytes=VMEM_LIMIT)
-    table = row_tables(band_bins, length)
+    table = row_tables(band_bins, slots, length)
     forward_table = np.concatenate(split_halves(table / math.sqrt(length)), axis=0)
     back_high, back_low = split_halves(table)
     back_table = np.concatenate([back_high, back_high, back_low], axis=0)
-    tables = lag_tables(band_bins, lags, length)
+    tables = lag_tables(band_bins, slots, lags, length)
     with jax.named_scope("spectrum"):
         outgoing = pl.pallas_call(
             functools.partial(spectrum_kernel, chunk),
@@ -238,7 +248,7 @@
             cost_estimate=pl.CostEstimate(flops=COST[0], bytes_accessed=COST[1], transcendentals=0),
             name="spectrum",
         )(in_hbm(gathers), in_hbm(jnp.asarray(forward_table)))
-    incoming = lax.all_to_all(outgoing, "freq", split_axis=0, concat_axis=0, tiled=True)
+    incoming = exchange(outgoing)
     with jax.named_scope("predict"):
         sending, coefficients = pl.pallas_call(
             functools.partial(predict_kernel, kept_bins),
@@ -259,17 +269,17 @@
             incoming,
             operator,
         )
-    returned = lax.all_to_all(sending, "freq", split_axis=0, concat_axis=0, tiled=True)
+    returned = exchange(sending)
     with jax.named_scope("subtract"):
         return pl.pallas_call(
-            functools.partial(subtract_kernel, length // 8),
+            functools.partial(subtract_kernel, length // 4),
             out_shape=jax.ShapeDtypeStruct((traces, length), jnp.float32),
             in_specs=[vmem_spec()] * 4,
             out_specs=hbm_spec(),
             scratch_shapes=[
                 pltpu.VMEM((traces + 16, 2 * rows), jnp.float32),
                 pltpu.VMEM((traces, length), jnp.float32),
-                pltpu.SemaphoreType.DMA((8,)),
+                pltpu.SemaphoreType.DMA((4,)),
             ],
             compiler_params=params,
             name="subtract",

time: 29.8 us -> 25.8 us (0.87)
  blocking collectives: 23.2 us -> 19.2 us
    all_to_all x2, blocking collectives: 23.2 us -> 19.2 us  [exchange(): lax.all_to_all(chunks, 'freq', 0, 0, axis_index_groups=[order], tiled=True)]
where the time goes in v6:
time: 25.8 us; the launch traced here: 25.6 us
  blocking collectives  19.2 us (74%)
  Pallas kernels  6.34 us (25%)
    all_to_all x2, blocking collectives, exchange(): lax.all_to_all(chunks, 'freq', 0, 0, axis_index_groups=[order], tiled=True)  19.2 us
    pallas_call x1, Pallas kernels, local(): pl.pallas_call(functools.partial(predict_kernel, kept_bins), out_shape=[j...  2.92 us
    pallas_call x1, Pallas kernels, local(): pl.pallas_call(functools.partial(spectrum_kernel, chunk), out_shape=jax.S...  2.07 us
    pallas_call x1, Pallas kernels, local(): pl.pallas_call(functools.partial(subtract_kernel, length // 4), out_shape...  1.36 us

profile of v6, /device:TPU:0, one launch (start us, length us, event | category | flops | bytes accessed | tf_op | source)
XLA Modules:
  0.0 25.6 jit_solution(15526437902886599030)
XLA Ops:
  0.0 0.0 copy-start.3
  0.0 0.0 copy-start.6
  0.0 0.0 copy-start.5
  0.0 0.0 copy-start.4
  0.0 0.0 copy-start
  0.0 2.1 %spectrum.1 = bf16[16,4,128]{2,1,0:T(4,128)(2,1)S(1)} custom-call(f32[128,2048]{1,0:T(8,128)} %gathers_ref.3, bf16[128,2048]{1,0:T(8,128)(2,1)} %constant.6.clone.table_ref), custom_call_target="tpu_custom_call" | custom-call | flops 99999997952 | bytes 40000000 | tf_op jit(solution)/shard_map/spectrum/spectrum/pallas_call | solution.py:237
  2.1 0.0 copy-start.1
  2.1 0.0 copy-start.2
  2.1 10.6 %all_to_all.10.incoming_ref = bf16[16,4,128]{2,1,0:T(4,128)(2,1)S(1)} all-to-all(bf16[16,4,128]{2,1,0:T(4,128)(2,1)S(1)} %spectrum.1), channel_id=1, replica_groups={{15,14,13,12,11,10,9,8,7,6,5,4,3,2,1,0},{31,30,29,28,27,26,25,24,23,22,..., dimensions={0} | all-to-all | bytes 32768 | tf_op jit(solution)/shard_map/all_to_all | solution.py:217
  12.7 0.0 copy-done.3
  12.7 0.0 copy-done.6
  12.7 0.0 copy-done.5
  12.7 0.0 copy-done.4
  12.7 0.0 copy-done
  12.7 2.9 %predict.1 = (bf16[16,4,256]{2,1,0:T(4,128)(2,1)S(1)}, f32[9,128]{1,0:T(8,128)S(1)}) custom-call(s32[16]{0:T(128)S(1)} %copy-done.5, s32[16]{0:T(128)S(1)} %copy-done.6, f32[9,4,31]{2,1,0:T(4,128)S(1)} %bitcast.3, f32[124,128]{1,0:T(8,128)S(1)} %copy-done.3, bf16[16,4,128]{2,1,0:T(4,128)(2,1)S(1)} %all_to_all.10.incoming_ref, ...), custom_call_target="tpu_custom_call" | custom-call | tf_op jit(solution)/shard_map/predict/predict/pallas_call | solution.py:253
  15.7 8.6 %all_to_all.11.returned_ref = bf16[16,4,256]{2,1,0:T(4,128)(2,1)S(1)} all-to-all(bf16[16,4,256]{2,1,0:T(4,128)(2,1)S(1)} %get-tuple-element.7), channel_id=1, replica_groups={{15,14,13,12,11,10,9,8,7,6,5,4,3,2,1,0},{31,30,29,28,27,26,25,24,23,22,..., dimensions={0} | all-to-all | bytes 65536 | tf_op jit(solution)/shard_map/all_to_all | solution.py:217
  24.3 0.0 copy-done.1
  24.3 0.0 copy-done.2
  24.3 1.4 %subtract.1 = f32[128,2048]{1,0:T(8,128)} custom-call(bf16[16,4,256]{2,1,0:T(4,128)(2,1)S(1)} %all_to_all.11.returned_ref, f32[9,128]{1,0:T(8,128)S(1)} %get-tuple-element.8.coefficient_ref, bf16[192,2048]{1,0:T(8,128)(2,1)S(1)} %copy-done.2, f32[128,2048]{1,0:T(8,128)S(1)} %copy-done.1), custom_call_target="tpu_custom_call" | custom-call | tf_op jit(solution)/shard_map/subtract/subtract/pallas_call | solution.py:274
Async XLA Ops:
  0.0 12.7 %copy-start.3 = (f32[124,128]{1,0:T(8,128)S(1)}, f32[124,128]{1,0:T(8,128)}, u32[]{:S(2)}) copy-start(f32[124,128]{1,0:T(8,128)} %constant.7.clone.lag_ref) | copy-start | bytes 190468
  0.0 12.7 %copy-start.6 = (s32[16]{0:T(128)S(1)}, s32[16]{0:T(128)}, u32[]{:S(2)}) copy-start(s32[16]{0:T(128)} %slice_ref.1) | copy-start | bytes 196
  0.0 12.7 %copy-start.5 = (s32[16]{0:T(128)S(1)}, s32[16]{0:T(128)}, u32[]{:S(2)}) copy-start(s32[16]{0:T(128)} %tile_ref.1) | copy-start | bytes 196
  0.0 12.7 %copy-start.4 = (f32[1,4,9,31]{3,1,2,0:T(4,128)S(1)}, f32[1,4,9,31]{3,1,2,0:T(4,128)}, u32[]{:S(2)}) copy-start(f32[1,4,9,31]{3,1,2,0:T(4,128)} %param.10) | copy-start | bytes 13396
  0.0 12.7 %copy-start = (bf16[2,2,1024,1024]{3,2,1,0:T(8,128)(2,1)S(1)}, bf16[2,2,1024,1024]{3,2,1,0:T(8,128)(2,1)}, u32[]{:S(2)}) copy-start(bf16[2,2,1024,1024]{3,2,1,0:T(8,128)(2,1)} %operator_ref.1) | copy-start | bytes 25165828
  2.1 22.2 %copy-start.1 = (f32[128,2048]{1,0:T(8,128)S(1)}, f32[128,2048]{1,0:T(8,128)}, u32[]{:S(2)}) copy-start(f32[128,2048]{1,0:T(8,128)} %gathers_ref.3) | copy-start | bytes 3145732
  2.1 22.2 %copy-start.2 = (bf16[192,2048]{1,0:T(8,128)(2,1)S(1)}, bf16[192,2048]{1,0:T(8,128)(2,1)}, u32[]{:S(2)}) copy-start(bf16[192,2048]{1,0:T(8,128)(2,1)} %constant.8.clone.table_ref) | copy-start | bytes 2359300

commit v7 on v6

--- a/solution.py
+++ b/solution.py
@@ -12,6 +12,7 @@
 
 FIRST = 40
 REACH = 4
+SPAN = 256
 COST = (10**11, 40_000_000)
 VMEM_LIMIT = 32 * 1024 * 1024
 
@@ -137,29 +138,43 @@
         ]
         columns.append(jnp.concatenate(parts, axis=0))
     spectrum = jnp.concatenate(columns, axis=1).astype(jnp.bfloat16)
-    row_ids = lax.broadcasted_iota(jnp.int32, (rows, receivers), 0)
+    coefficient_ref[...] = filter_lanes(kept_bins, slots, slice_ref, filters_ref, lag_ref)
+    span = SPAN
+    row_ids = lax.broadcasted_iota(jnp.int32, (rows, span), 0)
+    lane_ids = lax.broadcasted_iota(jnp.int32, (rows, traces), 1)
     dot = functools.partial(
         lax.dot_general,
         dimension_numbers=(((1,), (1,)), ((), ())),
         preferred_element_type=jnp.float32,
     )
-    predicted = jnp.zeros((rows, receivers), jnp.float32)
-    for slot in range(slots):
-        by_real = dot(spectrum, operator_ref[slot, 0])
-        by_imag = swap_pairs(dot(spectrum, operator_ref[slot, 1]))
-        product = jnp.where(row_ids % 2 == 0, by_real - by_imag, by_real + by_imag)
-        predicted = jnp.where(row_ids // 2 % slots == slot, product, predicted)
-    lane_ids = lax.broadcasted_iota(jnp.int32, (rows, receivers), 1) % traces
     edge = jnp.zeros((rows, traces), jnp.float32)
-    after = jnp.concatenate([predicted[:, traces:], edge], axis=1)
-    before = jnp.concatenate([edge, predicted[:, :-traces]], axis=1)
-    halo = jnp.where(lane_ids < REACH, after, jnp.where(lane_ids >= traces - REACH, before, 0.0))
-    for s in range(shots):
-        for q in range(per_shot):
-            where = (slice(s * group_rows, (s + 1) * group_rows), slice(q * traces, (q + 1) * traces))
-            both = jnp.concatenate([predicted[where], halo[where]], axis=1)
-            out_ref[holder[s * per_shot + q]] = both.astype(jnp.bfloat16)
-    coefficient_ref[...] = filter_lanes(kept_bins, slots, slice_ref, filters_ref, lag_ref)
+    predicted = [edge]
+
+    def cut(q):
+        before, here, after = predicted[q : q + 3]
+        halo = jnp.where(
+            lane_ids < REACH, after, jnp.where(lane_ids >= traces - REACH, before, 0.0)
+        )
+        both = jnp.concatenate([here, halo], axis=1)
+        for s in range(shots):
+            piece = both[s * group_rows : (s + 1) * group_rows]
+            out_ref[holder[s * per_shot + q]] = piece.astype(jnp.bfloat16)
+
+    done = 0
+    for first in range(0, receivers, span):
+        where = pl.ds(first, span)
+        block = jnp.zeros((rows, span), jnp.float32)
+        for slot in range(slots):
+            by_real = dot(spectrum, operator_ref[slot, 0, where])
+            by_imag = swap_pairs(dot(spectrum, operator_ref[slot, 1, where]))
+            product = jnp.where(row_ids % 2 == 0, by_real - by_imag, by_real + by_imag)
+            block = jnp.where(row_ids // 2 % slots == slot, product, block)
+        predicted.extend(block[:, i : i + traces] for i in range(0, span, traces))
+        while done + 3 <= len(predicted):
+            cut(done)
+            done += 1
+    predicted.append(edge)
+    cut(done)
 
 
 def subtract_kernel(
@@ -226,7 +241,7 @@
     group_rows = 2 * slots
     kept_bins = 5 * devices // 4
     offsets, lags = filters.shape[2], filters.shape[3]
-    chunk = length // 4
+    chunk = length // 2
     params = pltpu.CompilerParams(vmem_limit_bytes=VMEM_LIMIT)
     table = row_tables(band_bins, slots, length)
     forward_table = np.concatenate(split_halves(table / math.sqrt(length)), axis=0)

time: 25.8 us -> 25.9 us (level)
  no operation moved by 1% of the time
where the time goes in v7:
time: 25.9 us; the launch traced here: 25.7 us
  blocking collectives  19.2 us (74%)
  Pallas kernels  6.42 us (25%)
    all_to_all x2, blocking collectives, exchange(): lax.all_to_all(chunks, 'freq', 0, 0, axis_index_groups=[order], tiled=True)  19.2 us
    pallas_call x1, Pallas kernels, local(): pl.pallas_call(functools.partial(predict_kernel, kept_bins), out_shape=[j...  2.94 us
    pallas_call x1, Pallas kernels, local(): pl.pallas_call(functools.partial(spectrum_kernel, chunk), out_shape=jax.S...  2.12 us
    pallas_call x1, Pallas kernels, local(): pl.pallas_call(functools.partial(subtract_kernel, length // 4), out_shape...  1.36 us

profile of v7, /device:TPU:0, one launch (start us, length us, event | category | flops | bytes accessed | tf_op | source)
XLA Modules:
  0.0 25.7 jit_solution(17167263489223728796)
XLA Ops:
  0.0 0.0 copy-start.3
  0.0 0.0 copy-start.6
  0.0 0.0 copy-start.5
  0.0 0.0 copy-start.4
  0.0 0.0 copy-start
  0.0 2.1 %spectrum.1 = bf16[16,4,128]{2,1,0:T(4,128)(2,1)S(1)} custom-call(f32[128,2048]{1,0:T(8,128)} %gathers_ref.3, bf16[128,2048]{1,0:T(8,128)(2,1)} %constant.6.clone.table_ref), custom_call_target="tpu_custom_call" | custom-call | flops 99999997952 | bytes 40000000 | tf_op jit(solution)/shard_map/spectrum/spectrum/pallas_call | solution.py:252
  2.1 0.0 copy-start.1
  2.1 0.0 copy-start.2
  2.2 10.6 %all_to_all.10.incoming_ref = bf16[16,4,128]{2,1,0:T(4,128)(2,1)S(1)} all-to-all(bf16[16,4,128]{2,1,0:T(4,128)(2,1)S(1)} %spectrum.1), channel_id=1, replica_groups={{15,14,13,12,11,10,9,8,7,6,5,4,3,2,1,0},{31,30,29,28,27,26,25,24,23,22,..., dimensions={0} | all-to-all | bytes 32768 | tf_op jit(solution)/shard_map/all_to_all | solution.py:232
  12.8 0.0 copy-done.3
  12.8 0.0 copy-done.6
  12.8 0.0 copy-done.5
  12.8 0.0 copy-done.4
  12.8 0.0 copy-done
  12.8 2.9 %predict.1 = (bf16[16,4,256]{2,1,0:T(4,128)(2,1)S(1)}, f32[9,128]{1,0:T(8,128)S(1)}) custom-call(s32[16]{0:T(128)S(1)} %copy-done.5, s32[16]{0:T(128)S(1)} %copy-done.6, f32[9,4,31]{2,1,0:T(4,128)S(1)} %bitcast.3, f32[124,128]{1,0:T(8,128)S(1)} %copy-done.3, bf16[16,4,128]{2,1,0:T(4,128)(2,1)S(1)} %all_to_all.10.incoming_ref, ...), custom_call_target="tpu_custom_call" | custom-call | tf_op jit(solution)/shard_map/predict/predict/pallas_call | solution.py:268
  15.7 8.6 %all_to_all.11.returned_ref = bf16[16,4,256]{2,1,0:T(4,128)(2,1)S(1)} all-to-all(bf16[16,4,256]{2,1,0:T(4,128)(2,1)S(1)} %get-tuple-element.7), channel_id=1, replica_groups={{15,14,13,12,11,10,9,8,7,6,5,4,3,2,1,0},{31,30,29,28,27,26,25,24,23,22,..., dimensions={0} | all-to-all | bytes 65536 | tf_op jit(solution)/shard_map/all_to_all | solution.py:232
  24.3 0.0 copy-done.1
  24.3 0.0 copy-done.2
  24.3 1.4 %subtract.1 = f32[128,2048]{1,0:T(8,128)} custom-call(bf16[16,4,256]{2,1,0:T(4,128)(2,1)S(1)} %all_to_all.11.returned_ref, f32[9,128]{1,0:T(8,128)S(1)} %get-tuple-element.8.coefficient_ref, bf16[192,2048]{1,0:T(8,128)(2,1)S(1)} %copy-done.2, f32[128,2048]{1,0:T(8,128)S(1)} %copy-done.1), custom_call_target="tpu_custom_call" | custom-call | tf_op jit(solution)/shard_map/subtract/subtract/pallas_call | solution.py:289
Async XLA Ops:
  0.0 12.8 %copy-start.3 = (f32[124,128]{1,0:T(8,128)S(1)}, f32[124,128]{1,0:T(8,128)}, u32[]{:S(2)}) copy-start(f32[124,128]{1,0:T(8,128)} %constant.7.clone.lag_ref) | copy-start | bytes 190468
  0.0 12.8 %copy-start.6 = (s32[16]{0:T(128)S(1)}, s32[16]{0:T(128)}, u32[]{:S(2)}) copy-start(s32[16]{0:T(128)} %slice_ref.1) | copy-start | bytes 196
  0.0 12.8 %copy-start.5 = (s32[16]{0:T(128)S(1)}, s32[16]{0:T(128)}, u32[]{:S(2)}) copy-start(s32[16]{0:T(128)} %tile_ref.1) | copy-start | bytes 196
  0.0 12.8 %copy-start.4 = (f32[1,4,9,31]{3,1,2,0:T(4,128)S(1)}, f32[1,4,9,31]{3,1,2,0:T(4,128)}, u32[]{:S(2)}) copy-start(f32[1,4,9,31]{3,1,2,0:T(4,128)} %param.10) | copy-start | bytes 13396
  0.0 12.8 %copy-start = (bf16[2,2,1024,1024]{3,2,1,0:T(8,128)(2,1)S(1)}, bf16[2,2,1024,1024]{3,2,1,0:T(8,128)(2,1)}, u32[]{:S(2)}) copy-start(bf16[2,2,1024,1024]{3,2,1,0:T(8,128)(2,1)} %operator_ref.1) | copy-start | bytes 25165828
  2.1 22.2 %copy-start.1 = (f32[128,2048]{1,0:T(8,128)S(1)}, f32[128,2048]{1,0:T(8,128)}, u32[]{:S(2)}) copy-start(f32[128,2048]{1,0:T(8,128)} %gathers_ref.3) | copy-start | bytes 3145732
  2.1 22.2 %copy-start.2 = (bf16[192,2048]{1,0:T(8,128)(2,1)S(1)}, bf16[192,2048]{1,0:T(8,128)(2,1)}, u32[]{:S(2)}) copy-start(bf16[192,2048]{1,0:T(8,128)(2,1)} %constant.8.clone.table_ref) | copy-start | bytes 2359300

commit v8 on v6

--- a/solution.py
+++ b/solution.py
@@ -108,7 +108,7 @@
         weights = table[:, part]
         both = dot(weights, high)
         total = total + both[:rows] + (both[rows:] + dot(weights[:rows], low))
-    out_ref[...] = total.astype(jnp.bfloat16).reshape(out_ref.shape)
+    out_ref[...] = total.astype(jnp.bfloat16).astype(out_ref.dtype).reshape(out_ref.shape)
 
 
 def predict_kernel(
@@ -157,7 +157,7 @@
     for s in range(shots):
         for q in range(per_shot):
             where = (slice(s * group_rows, (s + 1) * group_rows), slice(q * traces, (q + 1) * traces))
-            both = jnp.concatenate([predicted[where], halo[where]], axis=1)
+            both = jnp.concatenate([predicted[where], halo[where]], axis=0)
             out_ref[holder[s * per_shot + q]] = both.astype(jnp.bfloat16)
     coefficient_ref[...] = filter_lanes(kept_bins, slots, slice_ref, filters_ref, lag_ref)
 
@@ -166,14 +166,16 @@
     chunk, returned_ref, coefficient_ref, table_ref, gathers_ref, out_ref, spread, result, sems
 ):
     devices, group_rows, _ = returned_ref.shape
+    group_rows = group_rows // 2
     rows = devices * group_rows
     traces, length = gathers_ref.shape
     offsets = coefficient_ref.shape[0]
-    own = returned_ref[...].astype(jnp.float32).reshape(rows, 2 * traces)
-    both = jnp.concatenate([own, swap_pairs(own)], axis=0)
-    halo = jnp.transpose(both[:, traces:])
+    came = returned_ref[...].astype(jnp.float32)
+    own = came[:, :group_rows].reshape(rows, traces)
+    edges = came[:, group_rows:].reshape(rows, traces)
+    halo = jnp.transpose(jnp.concatenate([edges, swap_pairs(edges)], axis=0))
     spread[0:8] = halo[traces - 8 :]
-    spread[8 : 8 + traces] = jnp.transpose(both[:, :traces])
+    spread[8 : 8 + traces] = jnp.transpose(jnp.concatenate([own, swap_pairs(own)], axis=0))
     spread[8 + traces : 16 + traces] = halo[:8]
     total = jnp.zeros((traces, 2 * rows), jnp.float32)
     for offset in range(offsets):
@@ -226,7 +228,7 @@
     group_rows = 2 * slots
     kept_bins = 5 * devices // 4
     offsets, lags = filters.shape[2], filters.shape[3]
-    chunk = length // 4
+    chunk = length
     params = pltpu.CompilerParams(vmem_limit_bytes=VMEM_LIMIT)
     table = row_tables(band_bins, slots, length)
     forward_table = np.concatenate(split_halves(table / math.sqrt(length)), axis=0)
@@ -236,7 +238,7 @@
     with jax.named_scope("spectrum"):
         outgoing = pl.pallas_call(
             functools.partial(spectrum_kernel, chunk),
-            out_shape=jax.ShapeDtypeStruct((devices, group_rows, traces), jnp.bfloat16),
+            out_shape=jax.ShapeDtypeStruct((devices, group_rows, traces), jnp.float32),
             in_specs=[hbm_spec()] * 2,
             out_specs=vmem_spec(),
             scratch_shapes=[
@@ -253,7 +255,7 @@
         sending, coefficients = pl.pallas_call(
             functools.partial(predict_kernel, kept_bins),
             out_shape=[
-                jax.ShapeDtypeStruct((devices, group_rows, 2 * traces), jnp.bfloat16),
+                jax.ShapeDtypeStruct((devices, 2 * group_rows, traces), jnp.bfloat16),
                 jax.ShapeDtypeStruct((offsets, 2 * rows), jnp.float32),
             ],
             in_specs=[smem_spec()] * 2 + [vmem_spec()] * 4,

time: 25.8 us -> 25.8 us (level)
  no operation moved by 1% of the time
where the time goes in v8:
time: 25.8 us; the launch traced here: 25.6 us
  blocking collectives  19.3 us (75%)
  Pallas kernels  6.25 us (24%)
    all_to_all x2, blocking collectives, exchange(): lax.all_to_all(chunks, 'freq', 0, 0, axis_index_groups=[order], tiled=True)  19.3 us
    pallas_call x1, Pallas kernels, local(): pl.pallas_call(functools.partial(predict_kernel, kept_bins), out_shape=[j...  2.92 us
    pallas_call x1, Pallas kernels, local(): pl.pallas_call(functools.partial(spectrum_kernel, chunk), out_shape=jax.S...  1.98 us
    pallas_call x1, Pallas kernels, local(): pl.pallas_call(functools.partial(subtract_kernel, length // 4), out_shape...  1.36 us

profile of v8, /device:TPU:0, one launch (start us, length us, event | category | flops | bytes accessed | tf_op | source)
XLA Modules:
  0.0 25.6 jit_solution(793957083138332040)
XLA Ops:
  0.0 0.0 copy-start.3
  0.0 0.0 copy-start.6
  0.0 0.0 copy-start.5
  0.0 0.0 copy-start.4
  0.0 0.0 copy-start
  0.0 2.0 %spectrum.1 = f32[16,4,128]{2,1,0:T(4,128)S(1)} custom-call(f32[128,2048]{1,0:T(8,128)} %gathers_ref.3, bf16[128,2048]{1,0:T(8,128)(2,1)} %constant.6.clone.table_ref), custom_call_target="tpu_custom_call" | custom-call | flops 99999997952 | bytes 40000000 | tf_op jit(solution)/shard_map/spectrum/spectrum/pallas_call | solution.py:239
  2.0 0.0 copy-start.1
  2.0 0.0 copy-start.2
  2.0 10.7 %all_to_all.10.incoming_ref = f32[16,4,128]{2,1,0:T(4,128)S(1)} all-to-all(f32[16,4,128]{2,1,0:T(4,128)S(1)} %spectrum.1), channel_id=1, replica_groups={{15,14,13,12,11,10,9,8,7,6,5,4,3,2,1,0},{31,30,29,28,27,26,25,24,23,22,..., dimensions={0} | all-to-all | bytes 65536 | tf_op jit(solution)/shard_map/all_to_all | solution.py:219
  12.8 0.0 copy-done.3
  12.8 0.0 copy-done.6
  12.8 0.0 copy-done.5
  12.8 0.0 copy-done.4
  12.8 0.0 copy-done
  12.8 2.9 %predict.1 = (bf16[16,8,128]{2,1,0:T(8,128)(2,1)S(1)}, f32[9,128]{1,0:T(8,128)S(1)}) custom-call(s32[16]{0:T(128)S(1)} %copy-done.5, s32[16]{0:T(128)S(1)} %copy-done.6, f32[9,4,31]{2,1,0:T(4,128)S(1)} %bitcast.3, f32[124,128]{1,0:T(8,128)S(1)} %copy-done.3, f32[16,4,128]{2,1,0:T(4,128)S(1)} %all_to_all.10.incoming_ref, bf16[2,2,1024,1024]{3,2,1,0:T(8,128)(2,1)S(1)} %copy-done), custom_call_target="tpu_custom_call" | custom-call | tf_op jit(solution)/shard_map/predict/predict/pallas_call | solution.py:255
  15.7 8.5 %all_to_all.11.returned_ref = bf16[16,8,128]{2,1,0:T(8,128)(2,1)S(1)} all-to-all(bf16[16,8,128]{2,1,0:T(8,128)(2,1)S(1)} %get-tuple-element.7), channel_id=1, replica_groups={{15,14,13,12,11,10,9,8,7,6,5,4,3,2,1,0},{31,30,29,28,27,26,25,24,23,22,..., dimensions={0} | all-to-all | bytes 65536 | tf_op jit(solution)/shard_map/all_to_all | solution.py:219
  24.2 0.0 copy-done.1
  24.2 0.0 copy-done.2
  24.3 1.4 %subtract.1 = f32[128,2048]{1,0:T(8,128)} custom-call(bf16[16,8,128]{2,1,0:T(8,128)(2,1)S(1)} %all_to_all.11.returned_ref, f32[9,128]{1,0:T(8,128)S(1)} %get-tuple-element.8.coefficient_ref, bf16[192,2048]{1,0:T(8,128)(2,1)S(1)} %copy-done.2, f32[128,2048]{1,0:T(8,128)S(1)} %copy-done.1), custom_call_target="tpu_custom_call" | custom-call | tf_op jit(solution)/shard_map/subtract/subtract/pallas_call | solution.py:276
Async XLA Ops:
  0.0 12.8 %copy-start.3 = (f32[124,128]{1,0:T(8,128)S(1)}, f32[124,128]{1,0:T(8,128)}, u32[]{:S(2)}) copy-start(f32[124,128]{1,0:T(8,128)} %constant.7.clone.lag_ref) | copy-start | bytes 190468
  0.0 12.8 %copy-start.6 = (s32[16]{0:T(128)S(1)}, s32[16]{0:T(128)}, u32[]{:S(2)}) copy-start(s32[16]{0:T(128)} %slice_ref.1) | copy-start | bytes 196
  0.0 12.8 %copy-start.5 = (s32[16]{0:T(128)S(1)}, s32[16]{0:T(128)}, u32[]{:S(2)}) copy-start(s32[16]{0:T(128)} %tile_ref.1) | copy-start | bytes 196
  0.0 12.8 %copy-start.4 = (f32[1,4,9,31]{3,1,2,0:T(4,128)S(1)}, f32[1,4,9,31]{3,1,2,0:T(4,128)}, u32[]{:S(2)}) copy-start(f32[1,4,9,31]{3,1,2,0:T(4,128)} %param.10) | copy-start | bytes 13396
  0.0 12.8 %copy-start = (bf16[2,2,1024,1024]{3,2,1,0:T(8,128)(2,1)S(1)}, bf16[2,2,1024,1024]{3,2,1,0:T(8,128)(2,1)}, u32[]{:S(2)}) copy-start(bf16[2,2,1024,1024]{3,2,1,0:T(8,128)(2,1)} %operator_ref.1) | copy-start | bytes 25165828
  2.0 22.2 %copy-start.1 = (f32[128,2048]{1,0:T(8,128)S(1)}, f32[128,2048]{1,0:T(8,128)}, u32[]{:S(2)}) copy-start(f32[128,2048]{1,0:T(8,128)} %gathers_ref.3) | copy-start | bytes 3145732
  2.0 22.2 %copy-start.2 = (bf16[192,2048]{1,0:T(8,128)(2,1)S(1)}, bf16[192,2048]{1,0:T(8,128)(2,1)}, u32[]{:S(2)}) copy-start(bf16[192,2048]{1,0:T(8,128)(2,1)} %constant.8.clone.table_ref) | copy-start | bytes 2359300

commit v9 on v8

--- a/solution.py
+++ b/solution.py
@@ -23,8 +23,13 @@
     return high, low
 
 
+def exchange_order(devices):
+    return [device ^ 1 for device in range(devices)][::-1]
+
+
 def bins_in_order(band_bins, slots):
-    return FIRST + np.arange(band_bins).reshape(-1, slots)[::-1].reshape(-1)
+    groups = FIRST + np.arange(band_bins).reshape(-1, slots)
+    return groups[exchange_order(band_bins // slots)].reshape(-1)
 
 
 def row_tables(band_bins, slots, length):
@@ -74,8 +79,8 @@
     slot = lane_ids // 2 % slots
     count = jnp.zeros((1, lanes), jnp.int32)
     devices = rows // (2 * slots)
-    for device in range(devices):
-        count = jnp.where(group == devices - 1 - device, slice_ref[device], count)
+    for place, device in enumerate(exchange_order(devices)):
+        count = jnp.where(group == place, slice_ref[device], count)
     return total * jnp.where(slot < count, math.sqrt(2.0 / kept_bins), 0.0)
 
 
@@ -128,8 +133,8 @@
     per_shot = receivers // traces
     shots = devices // per_shot
     rows = shots * group_rows
-    for k in range(devices):
-        holder[tile_ref[k]] = devices - 1 - k
+    for place, device in enumerate(exchange_order(devices)):
+        holder[tile_ref[device]] = place
     columns = []
     for q in range(per_shot):
         parts = [
@@ -215,8 +220,8 @@
 
 
 def exchange(chunks):
-    order = list(range(chunks.shape[0]))[::-1]
-    return lax.all_to_all(chunks, "freq", 0, 0, axis_index_groups=[order], tiled=True)
+    groups = [exchange_order(chunks.shape[0])]
+    return lax.all_to_all(chunks, "freq", 0, 0, axis_index_groups=groups, tiled=True)
 
 
 def local(gathers, operator, filters, tile_of, slice_len):

time: 25.8 us -> 27 us (1.047)
  blocking collectives: 19.3 us -> 20.5 us
    all_to_all x2, blocking collectives: 19.3 us -> 20.5 us  [exchange(): lax.all_to_all(chunks, 'freq', 0, 0, axis_index_groups=groups, tiled=True)]
where the time goes in v9:
time: 27 us; the launch traced here: 26.8 us
  blocking collectives  20.5 us (76%)
  Pallas kernels  6.26 us (23%)
    all_to_all x2, blocking collectives, exchange(): lax.all_to_all(chunks, 'freq', 0, 0, axis_index_groups=groups, tiled=True)  20.5 us
    pallas_call x1, Pallas kernels, local(): pl.pallas_call(functools.partial(predict_kernel, kept_bins), out_shape=[j...  2.92 us
    pallas_call x1, Pallas kernels, local(): pl.pallas_call(functools.partial(spectrum_kernel, chunk), out_shape=jax.S...  1.98 us
    pallas_call x1, Pallas kernels, local(): pl.pallas_call(functools.partial(subtract_kernel, length // 4), out_shape...  1.36 us

profile of v9, /device:TPU:0, one launch (start us, length us, event | category | flops | bytes accessed | tf_op | source)
XLA Modules:
  0.0 26.8 jit_solution(16047021106636976923)
XLA Ops:
  0.0 0.0 copy-start.3
  0.0 0.0 copy-start.6
  0.0 0.0 copy-start.5
  0.0 0.0 copy-start.4
  0.0 0.0 copy-start
  0.0 2.0 %spectrum.1 = f32[16,4,128]{2,1,0:T(4,128)S(1)} custom-call(f32[128,2048]{1,0:T(8,128)} %gathers_ref.3, bf16[128,2048]{1,0:T(8,128)(2,1)} %constant.6.clone.table_ref), custom_call_target="tpu_custom_call" | custom-call | flops 99999997952 | bytes 40000000 | tf_op jit(solution)/shard_map/spectrum/spectrum/pallas_call | solution.py:244
  2.0 0.0 copy-start.1
  2.0 0.0 copy-start.2
  2.0 11.3 %all_to_all.10.incoming_ref = f32[16,4,128]{2,1,0:T(4,128)S(1)} all-to-all(f32[16,4,128]{2,1,0:T(4,128)S(1)} %spectrum.1), channel_id=1, replica_groups={{14,15,12,13,10,11,8,9,6,7,4,5,2,3,0,1},{30,31,28,29,26,27,24,25,22,23,..., dimensions={0} | all-to-all | bytes 65536 | tf_op jit(solution)/shard_map/all_to_all | solution.py:224
  13.3 0.0 copy-done.3
  13.3 0.0 copy-done.6
  13.3 0.0 copy-done.5
  13.3 0.0 copy-done.4
  13.3 0.0 copy-done
  13.3 2.9 %predict.1 = (bf16[16,8,128]{2,1,0:T(8,128)(2,1)S(1)}, f32[9,128]{1,0:T(8,128)S(1)}) custom-call(s32[16]{0:T(128)S(1)} %copy-done.5, s32[16]{0:T(128)S(1)} %copy-done.6, f32[9,4,31]{2,1,0:T(4,128)S(1)} %bitcast.3, f32[124,128]{1,0:T(8,128)S(1)} %copy-done.3, f32[16,4,128]{2,1,0:T(4,128)S(1)} %all_to_all.10.incoming_ref, bf16[2,2,1024,1024]{3,2,1,0:T(8,128)(2,1)S(1)} %copy-done), custom_call_target="tpu_custom_call" | custom-call | tf_op jit(solution)/shard_map/predict/predict/pallas_call | solution.py:260
  16.2 9.2 %all_to_all.11.returned_ref = bf16[16,8,128]{2,1,0:T(8,128)(2,1)S(1)} all-to-all(bf16[16,8,128]{2,1,0:T(8,128)(2,1)S(1)} %get-tuple-element.7), channel_id=1, replica_groups={{14,15,12,13,10,11,8,9,6,7,4,5,2,3,0,1},{30,31,28,29,26,27,24,25,22,23,..., dimensions={0} | all-to-all | bytes 65536 | tf_op jit(solution)/shard_map/all_to_all | solution.py:224
  25.4 0.0 copy-done.1
  25.4 0.0 copy-done.2
  25.4 1.4 %subtract.1 = f32[128,2048]{1,0:T(8,128)} custom-call(bf16[16,8,128]{2,1,0:T(8,128)(2,1)S(1)} %all_to_all.11.returned_ref, f32[9,128]{1,0:T(8,128)S(1)} %get-tuple-element.8.coefficient_ref, bf16[192,2048]{1,0:T(8,128)(2,1)S(1)} %copy-done.2, f32[128,2048]{1,0:T(8,128)S(1)} %copy-done.1), custom_call_target="tpu_custom_call" | custom-call | tf_op jit(solution)/shard_map/subtract/subtract/pallas_call | solution.py:281
Async XLA Ops:
  0.0 13.3 %copy-start.3 = (f32[124,128]{1,0:T(8,128)S(1)}, f32[124,128]{1,0:T(8,128)}, u32[]{:S(2)}) copy-start(f32[124,128]{1,0:T(8,128)} %constant.7.clone.lag_ref) | copy-start | bytes 190468
  0.0 13.3 %copy-start.6 = (s32[16]{0:T(128)S(1)}, s32[16]{0:T(128)}, u32[]{:S(2)}) copy-start(s32[16]{0:T(128)} %slice_ref.1) | copy-start | bytes 196
  0.0 13.3 %copy-start.5 = (s32[16]{0:T(128)S(1)}, s32[16]{0:T(128)}, u32[]{:S(2)}) copy-start(s32[16]{0:T(128)} %tile_ref.1) | copy-start | bytes 196
  0.0 13.3 %copy-start.4 = (f32[1,4,9,31]{3,1,2,0:T(4,128)S(1)}, f32[1,4,9,31]{3,1,2,0:T(4,128)}, u32[]{:S(2)}) copy-start(f32[1,4,9,31]{3,1,2,0:T(4,128)} %param.10) | copy-start | bytes 13396
  0.0 13.3 %copy-start = (bf16[2,2,1024,1024]{3,2,1,0:T(8,128)(2,1)S(1)}, bf16[2,2,1024,1024]{3,2,1,0:T(8,128)(2,1)}, u32[]{:S(2)}) copy-start(bf16[2,2,1024,1024]{3,2,1,0:T(8,128)(2,1)} %operator_ref.1) | copy-start | bytes 25165828
  2.0 23.4 %copy-start.1 = (f32[128,2048]{1,0:T(8,128)S(1)}, f32[128,2048]{1,0:T(8,128)}, u32[]{:S(2)}) copy-start(f32[128,2048]{1,0:T(8,128)} %gathers_ref.3) | copy-start | bytes 3145732
  2.0 23.4 %copy-start.2 = (bf16[192,2048]{1,0:T(8,128)(2,1)S(1)}, bf16[192,2048]{1,0:T(8,128)(2,1)}, u32[]{:S(2)}) copy-start(bf16[192,2048]{1,0:T(8,128)(2,1)} %constant.8.clone.table_ref) | copy-start | bytes 2359300

commit v10 on v8

--- a/solution.py
+++ b/solution.py
@@ -23,18 +23,26 @@
     return high, low
 
 
-def bins_in_order(band_bins, slots):
-    return FIRST + np.arange(band_bins).reshape(-1, slots)[::-1].reshape(-1)
-
-
-def row_tables(band_bins, slots, length):
-    bin_ids = bins_in_order(band_bins, slots)
+def order_out(devices):
+    return list(range(devices))[::-1]
+
+
+def order_back(devices):
+    return [devices - 1] + list(range(devices - 1))
+
+
+def bins_in_order(order, slots):
+    return (FIRST + np.array(order)[:, None] * slots + np.arange(slots)).reshape(-1)
+
+
+def row_tables(bin_ids, length):
+    band_bins = len(bin_ids)
     angles = 2.0 * np.pi / length * (bin_ids[:, None] * np.arange(length)[None, :] % length)
     return np.stack([np.cos(angles), -np.sin(angles)], axis=1).reshape(2 * band_bins, length)
 
 
-def lag_tables(band_bins, slots, lags, length):
-    bin_ids = bins_in_order(band_bins, slots)
+def lag_tables(bin_ids, lags, length):
+    band_bins = len(bin_ids)
     lag_ids = np.arange(lags) - lags // 2
     angles = 2.0 * np.pi / length * (bin_ids[:, None] * lag_ids[None, :] % length)
     cosine, sine = np.cos(angles), np.sin(angles)
@@ -74,8 +82,8 @@
     slot = lane_ids // 2 % slots
     count = jnp.zeros((1, lanes), jnp.int32)
     devices = rows // (2 * slots)
-    for device in range(devices):
-        count = jnp.where(group == devices - 1 - device, slice_ref[device], count)
+    for place, device in enumerate(order_back(devices)):
+        count = jnp.where(group == place, slice_ref[device], count)
     return total * jnp.where(slot < count, math.sqrt(2.0 / kept_bins), 0.0)
 
 
@@ -128,12 +136,14 @@
     per_shot = receivers // traces
     shots = devices // per_shot
     rows = shots * group_rows
-    for k in range(devices):
-        holder[tile_ref[k]] = devices - 1 - k
+    for place, device in enumerate(order_out(devices)):
+        holder[0, tile_ref[device]] = place
+    for place, device in enumerate(order_back(devices)):
+        holder[1, tile_ref[device]] = place
     columns = []
     for q in range(per_shot):
         parts = [
-            incoming_ref[holder[s * per_shot + q]].astype(jnp.float32) for s in range(shots)
+            incoming_ref[holder[0, s * per_shot + q]].astype(jnp.float32) for s in range(shots)
         ]
         columns.append(jnp.concatenate(parts, axis=0))
     spectrum = jnp.concatenate(columns, axis=1).astype(jnp.bfloat16)
@@ -158,7 +168,7 @@
         for q in range(per_shot):
             where = (slice(s * group_rows, (s + 1) * group_rows), slice(q * traces, (q + 1) * traces))
             both = jnp.concatenate([predicted[where], halo[where]], axis=0)
-            out_ref[holder[s * per_shot + q]] = both.astype(jnp.bfloat16)
+            out_ref[holder[1, s * per_shot + q]] = both.astype(jnp.bfloat16)
     coefficient_ref[...] = filter_lanes(kept_bins, slots, slice_ref, filters_ref, lag_ref)
 
 
@@ -214,8 +224,7 @@
     return pltpu.with_memory_space_constraint(values, pltpu.HBM)
 
 
-def exchange(chunks):
-    order = list(range(chunks.shape[0]))[::-1]
+def exchange(chunks, order):
     return lax.all_to_all(chunks, "freq", 0, 0, axis_index_groups=[order], tiled=True)
 
 
@@ -230,11 +239,13 @@
     offsets, lags = filters.shape[2], filters.shape[3]
     chunk = length
     params = pltpu.CompilerParams(vmem_limit_bytes=VMEM_LIMIT)
-    table = row_tables(band_bins, slots, length)
-    forward_table = np.concatenate(split_halves(table / math.sqrt(length)), axis=0)
-    back_high, back_low = split_halves(table)
+    bins_out = bins_in_order(order_out(devices), slots)
+    bins_back = bins_in_order(order_back(devices), slots)
+    forward = row_tables(bins_out, length) / math.sqrt(length)
+    forward_table = np.concatenate(split_halves(forward), axis=0)
+    back_high, back_low = split_halves(row_tables(bins_back, length))
     back_table = np.concatenate([back_high, back_high, back_low], axis=0)
-    tables = lag_tables(band_bins, slots, lags, length)
+    tables = lag_tables(bins_back, lags, length)
     with jax.named_scope("spectrum"):
         outgoing = pl.pallas_call(
             functools.partial(spectrum_kernel, chunk),
@@ -250,7 +261,7 @@
             cost_estimate=pl.CostEstimate(flops=COST[0], bytes_accessed=COST[1], transcendentals=0),
             name="spectrum",
         )(in_hbm(gathers), in_hbm(jnp.asarray(forward_table)))
-    incoming = exchange(outgoing)
+    incoming = exchange(outgoing, order_out(devices))
     with jax.named_scope("predict"):
         sending, coefficients = pl.pallas_call(
             functools.partial(predict_kernel, kept_bins),
@@ -260,7 +271,7 @@
             ],
             in_specs=[smem_spec()] * 2 + [vmem_spec()] * 4,
             out_specs=[vmem_spec()] * 2,
-            scratch_shapes=[pltpu.SMEM((devices,), jnp.int32)],
+            scratch_shapes=[pltpu.SMEM((2, devices), jnp.int32)],
             compiler_params=params,
             name="predict",
         )(
@@ -271,7 +282,7 @@
             incoming,
             operator,
         )
-    returned = exchange(sending)
+    returned = exchange(sending, order_back(devices))
     with jax.named_scope("subtract"):
         return pl.pallas_call(
             functools.partial(subtract_kernel, length // 4),

time: 25.8 us -> 25.9 us (level)
  no operation moved by 1% of the time
where the time goes in v10:
time: 25.9 us; the launch traced here: 25.7 us
  blocking collectives  19.4 us (75%)
  Pallas kernels  6.26 us (24%)
    all_to_all x2, blocking collectives, exchange(): lax.all_to_all(chunks, 'freq', 0, 0, axis_index_groups=[order], tiled=True)  19.4 us
    pallas_call x1, Pallas kernels, local(): pl.pallas_call(functools.partial(predict_kernel, kept_bins), out_shape=[j...  2.92 us
    pallas_call x1, Pallas kernels, local(): pl.pallas_call(functools.partial(spectrum_kernel, chunk), out_shape=jax.S...  1.98 us
    pallas_call x1, Pallas kernels, local(): pl.pallas_call(functools.partial(subtract_kernel, length // 4), out_shape...  1.36 us

profile of v10, /device:TPU:0, one launch (start us, length us, event | category | flops | bytes accessed | tf_op | source)
XLA Modules:
  0.0 25.7 jit_solution(1074178993893645586)
XLA Ops:
  0.0 0.0 copy-start.3
  0.0 0.0 copy-start.6
  0.0 0.0 copy-start.5
  0.0 0.0 copy-start.4
  0.0 0.0 copy-start
  0.0 2.0 %spectrum.1 = f32[16,4,128]{2,1,0:T(4,128)S(1)} custom-call(f32[128,2048]{1,0:T(8,128)} %gathers_ref.3, bf16[128,2048]{1,0:T(8,128)(2,1)} %constant.6.clone.table_ref), custom_call_target="tpu_custom_call" | custom-call | flops 99999997952 | bytes 40000000 | tf_op jit(solution)/shard_map/spectrum/spectrum/pallas_call | solution.py:250
  2.0 0.0 copy-start.1
  2.0 0.0 copy-start.2
  2.0 10.7 %all_to_all.10.incoming_ref = f32[16,4,128]{2,1,0:T(4,128)S(1)} all-to-all(f32[16,4,128]{2,1,0:T(4,128)S(1)} %spectrum.1), channel_id=1, replica_groups={{15,14,13,12,11,10,9,8,7,6,5,4,3,2,1,0},{31,30,29,28,27,26,25,24,23,22,..., dimensions={0} | all-to-all | bytes 65536 | tf_op jit(solution)/shard_map/all_to_all | solution.py:228
  12.8 0.0 copy-done.3
  12.8 0.0 copy-done.6
  12.8 0.0 copy-done.5
  12.8 0.0 copy-done.4
  12.8 0.0 copy-done
  12.8 2.9 %predict.1 = (bf16[16,8,128]{2,1,0:T(8,128)(2,1)S(1)}, f32[9,128]{1,0:T(8,128)S(1)}) custom-call(s32[16]{0:T(128)S(1)} %copy-done.5, s32[16]{0:T(128)S(1)} %copy-done.6, f32[9,4,31]{2,1,0:T(4,128)S(1)} %bitcast.3, f32[124,128]{1,0:T(8,128)S(1)} %copy-done.3, f32[16,4,128]{2,1,0:T(4,128)S(1)} %all_to_all.10.incoming_ref, bf16[2,2,1024,1024]{3,2,1,0:T(8,128)(2,1)S(1)} %copy-done), custom_call_target="tpu_custom_call" | custom-call | tf_op jit(solution)/shard_map/predict/predict/pallas_call | solution.py:266
  15.7 8.6 %all_to_all.11.returned_ref = bf16[16,8,128]{2,1,0:T(8,128)(2,1)S(1)} all-to-all(bf16[16,8,128]{2,1,0:T(8,128)(2,1)S(1)} %get-tuple-element.7), channel_id=1, replica_groups={{15,0,1,2,3,4,5,6,7,8,9,10,11,12,13,14},{31,16,17,18,19,20,21,22,23,24,..., dimensions={0} | all-to-all | bytes 65536 | tf_op jit(solution)/shard_map/all_to_all | solution.py:228
  24.4 0.0 copy-done.1
  24.4 0.0 copy-done.2
  24.4 1.4 %subtract.1 = f32[128,2048]{1,0:T(8,128)} custom-call(bf16[16,8,128]{2,1,0:T(8,128)(2,1)S(1)} %all_to_all.11.returned_ref, f32[9,128]{1,0:T(8,128)S(1)} %get-tuple-element.8.coefficient_ref, bf16[192,2048]{1,0:T(8,128)(2,1)S(1)} %copy-done.2, f32[128,2048]{1,0:T(8,128)S(1)} %copy-done.1), custom_call_target="tpu_custom_call" | custom-call | tf_op jit(solution)/shard_map/subtract/subtract/pallas_call | solution.py:287
Async XLA Ops:
  0.0 12.8 %copy-start.3 = (f32[124,128]{1,0:T(8,128)S(1)}, f32[124,128]{1,0:T(8,128)}, u32[]{:S(2)}) copy-start(f32[124,128]{1,0:T(8,128)} %constant.7.clone.lag_ref) | copy-start | bytes 190468
  0.0 12.8 %copy-start.6 = (s32[16]{0:T(128)S(1)}, s32[16]{0:T(128)}, u32[]{:S(2)}) copy-start(s32[16]{0:T(128)} %slice_ref.1) | copy-start | bytes 196
  0.0 12.8 %copy-start.5 = (s32[16]{0:T(128)S(1)}, s32[16]{0:T(128)}, u32[]{:S(2)}) copy-start(s32[16]{0:T(128)} %tile_ref.1) | copy-start | bytes 196
  0.0 12.8 %copy-start.4 = (f32[1,4,9,31]{3,1,2,0:T(4,128)S(1)}, f32[1,4,9,31]{3,1,2,0:T(4,128)}, u32[]{:S(2)}) copy-start(f32[1,4,9,31]{3,1,2,0:T(4,128)} %param.10) | copy-start | bytes 13396
  0.0 12.8 %copy-start = (bf16[2,2,1024,1024]{3,2,1,0:T(8,128)(2,1)S(1)}, bf16[2,2,1024,1024]{3,2,1,0:T(8,128)(2,1)}, u32[]{:S(2)}) copy-start(bf16[2,2,1024,1024]{3,2,1,0:T(8,128)(2,1)} %operator_ref.1) | copy-start | bytes 25165828
  2.0 22.4 %copy-start.1 = (f32[128,2048]{1,0:T(8,128)S(1)}, f32[128,2048]{1,0:T(8,128)}, u32[]{:S(2)}) copy-start(f32[128,2048]{1,0:T(8,128)} %gathers_ref.3) | copy-start | bytes 3145732
  2.0 22.3 %copy-start.2 = (bf16[192,2048]{1,0:T(8,128)(2,1)S(1)}, bf16[192,2048]{1,0:T(8,128)(2,1)}, u32[]{:S(2)}) copy-start(bf16[192,2048]{1,0:T(8,128)(2,1)} %constant.8.clone.table_ref) | copy-start | bytes 2359300

commit v11 on v8

--- a/solution.py
+++ b/solution.py
@@ -12,6 +12,7 @@
 
 FIRST = 40
 REACH = 4
+SPAN = 256
 COST = (10**11, 40_000_000)
 VMEM_LIMIT = 32 * 1024 * 1024
 
@@ -136,19 +137,33 @@
             incoming_ref[holder[s * per_shot + q]].astype(jnp.float32) for s in range(shots)
         ]
         columns.append(jnp.concatenate(parts, axis=0))
-    spectrum = jnp.concatenate(columns, axis=1).astype(jnp.bfloat16)
+    spectrum = jnp.concatenate(columns, axis=1)
     row_ids = lax.broadcasted_iota(jnp.int32, (rows, receivers), 0)
-    dot = functools.partial(
-        lax.dot_general,
-        dimension_numbers=(((1,), (1,)), ((), ())),
-        preferred_element_type=jnp.float32,
-    )
-    predicted = jnp.zeros((rows, receivers), jnp.float32)
-    for slot in range(slots):
-        by_real = dot(spectrum, operator_ref[slot, 0])
-        by_imag = swap_pairs(dot(spectrum, operator_ref[slot, 1]))
-        product = jnp.where(row_ids % 2 == 0, by_real - by_imag, by_real + by_imag)
-        predicted = jnp.where(row_ids // 2 % slots == slot, product, predicted)
+    partner = swap_pairs(spectrum)
+    partner = jnp.where(row_ids % 2 == 0, -partner, partner)
+    flat = [spectrum.astype(jnp.bfloat16), partner.astype(jnp.bfloat16)]
+    turned = [jnp.transpose(side).astype(jnp.bfloat16) for side in (spectrum, partner)]
+    block_ids = lax.broadcasted_iota(jnp.int32, (rows, SPAN), 0)
+    blocks = []
+    for first in range(0, receivers, SPAN):
+        where = pl.ds(first, SPAN)
+        block = jnp.zeros((rows, SPAN), jnp.float32)
+        for slot in range(slots):
+            real, imag = operator_ref[slot, 0, where], operator_ref[slot, 1, where]
+            if slot % 2:
+                product = jnp.dot(real, turned[0], preferred_element_type=jnp.float32)
+                product += jnp.dot(imag, turned[1], preferred_element_type=jnp.float32)
+                product = jnp.transpose(product)
+            else:
+                dot = functools.partial(
+                    lax.dot_general,
+                    dimension_numbers=(((1,), (1,)), ((), ())),
+                    preferred_element_type=jnp.float32,
+                )
+                product = dot(flat[0], real) + dot(flat[1], imag)
+            block = jnp.where(block_ids // 2 % slots == slot, product, block)
+        blocks.append(block)
+    predicted = jnp.concatenate(blocks, axis=1)
     lane_ids = lax.broadcasted_iota(jnp.int32, (rows, receivers), 1) % traces
     edge = jnp.zeros((rows, traces), jnp.float32)
     after = jnp.concatenate([predicted[:, traces:], edge], axis=1)

time: 25.8 us -> 25.9 us (level)
  no operation moved by 1% of the time
where the time goes in v11:
time: 25.9 us; the launch traced here: 25.7 us
  blocking collectives  19.3 us (75%)
  Pallas kernels  6.32 us (24%)
    all_to_all x2, blocking collectives, exchange(): lax.all_to_all(chunks, 'freq', 0, 0, axis_index_groups=[order], tiled=True)  19.3 us
    pallas_call x1, Pallas kernels, local(): pl.pallas_call(functools.partial(predict_kernel, kept_bins), out_shape=[j...  2.98 us
    pallas_call x1, Pallas kernels, local(): pl.pallas_call(functools.partial(spectrum_kernel, chunk), out_shape=jax.S...  1.98 us
    pallas_call x1, Pallas kernels, local(): pl.pallas_call(functools.partial(subtract_kernel, length // 4), out_shape...  1.36 us

profile of v11, /device:TPU:0, one launch (start us, length us, event | category | flops | bytes accessed | tf_op | source)
XLA Modules:
  0.0 25.7 jit_solution(12466425195017353758)
XLA Ops:
  0.0 0.0 copy-start.3
  0.0 0.0 copy-start.6
  0.0 0.0 copy-start.5
  0.0 0.0 copy-start.4
  0.0 0.0 copy-start
  0.0 2.0 %spectrum.1 = f32[16,4,128]{2,1,0:T(4,128)S(1)} custom-call(f32[128,2048]{1,0:T(8,128)} %gathers_ref.3, bf16[128,2048]{1,0:T(8,128)(2,1)} %constant.6.clone.table_ref), custom_call_target="tpu_custom_call" | custom-call | flops 99999997952 | bytes 40000000 | tf_op jit(solution)/shard_map/spectrum/spectrum/pallas_call | solution.py:254
  2.0 0.0 copy-start.1
  2.0 0.0 copy-start.2
  2.0 10.7 %all_to_all.10.incoming_ref = f32[16,4,128]{2,1,0:T(4,128)S(1)} all-to-all(f32[16,4,128]{2,1,0:T(4,128)S(1)} %spectrum.1), channel_id=1, replica_groups={{15,14,13,12,11,10,9,8,7,6,5,4,3,2,1,0},{31,30,29,28,27,26,25,24,23,22,..., dimensions={0} | all-to-all | bytes 65536 | tf_op jit(solution)/shard_map/all_to_all | solution.py:234
  12.8 0.0 copy-done.3
  12.8 0.0 copy-done.6
  12.8 0.0 copy-done.5
  12.8 0.0 copy-done.4
  12.8 0.0 copy-done
  12.8 3.0 %predict.1 = (bf16[16,8,128]{2,1,0:T(8,128)(2,1)S(1)}, f32[9,128]{1,0:T(8,128)S(1)}) custom-call(s32[16]{0:T(128)S(1)} %copy-done.5, s32[16]{0:T(128)S(1)} %copy-done.6, f32[9,4,31]{2,1,0:T(4,128)S(1)} %bitcast.3, f32[124,128]{1,0:T(8,128)S(1)} %copy-done.3, f32[16,4,128]{2,1,0:T(4,128)S(1)} %all_to_all.10.incoming_ref, bf16[2,2,1024,1024]{3,2,1,0:T(8,128)(2,1)S(1)} %copy-done), custom_call_target="tpu_custom_call" | custom-call | tf_op jit(solution)/shard_map/predict/predict/pallas_call | solution.py:270
  15.8 8.5 %all_to_all.11.returned_ref = bf16[16,8,128]{2,1,0:T(8,128)(2,1)S(1)} all-to-all(bf16[16,8,128]{2,1,0:T(8,128)(2,1)S(1)} %get-tuple-element.7), channel_id=1, replica_groups={{15,14,13,12,11,10,9,8,7,6,5,4,3,2,1,0},{31,30,29,28,27,26,25,24,23,22,..., dimensions={0} | all-to-all | bytes 65536 | tf_op jit(solution)/shard_map/all_to_all | solution.py:234
  24.3 0.0 copy-done.1
  24.3 0.0 copy-done.2
  24.3 1.4 %subtract.1 = f32[128,2048]{1,0:T(8,128)} custom-call(bf16[16,8,128]{2,1,0:T(8,128)(2,1)S(1)} %all_to_all.11.returned_ref, f32[9,128]{1,0:T(8,128)S(1)} %get-tuple-element.8.coefficient_ref, bf16[192,2048]{1,0:T(8,128)(2,1)S(1)} %copy-done.2, f32[128,2048]{1,0:T(8,128)S(1)} %copy-done.1), custom_call_target="tpu_custom_call" | custom-call | tf_op jit(solution)/shard_map/subtract/subtract/pallas_call | solution.py:291
Async XLA Ops:
  0.0 12.8 %copy-start.3 = (f32[124,128]{1,0:T(8,128)S(1)}, f32[124,128]{1,0:T(8,128)}, u32[]{:S(2)}) copy-start(f32[124,128]{1,0:T(8,128)} %constant.7.clone.lag_ref) | copy-start | bytes 190468
  0.0 12.8 %copy-start.6 = (s32[16]{0:T(128)S(1)}, s32[16]{0:T(128)}, u32[]{:S(2)}) copy-start(s32[16]{0:T(128)} %slice_ref.1) | copy-start | bytes 196
  0.0 12.8 %copy-start.5 = (s32[16]{0:T(128)S(1)}, s32[16]{0:T(128)}, u32[]{:S(2)}) copy-start(s32[16]{0:T(128)} %tile_ref.1) | copy-start | bytes 196
  0.0 12.8 %copy-start.4 = (f32[1,4,9,31]{3,1,2,0:T(4,128)S(1)}, f32[1,4,9,31]{3,1,2,0:T(4,128)}, u32[]{:S(2)}) copy-start(f32[1,4,9,31]{3,1,2,0:T(4,128)} %param.10) | copy-start | bytes 13396
  0.0 12.8 %copy-start = (bf16[2,2,1024,1024]{3,2,1,0:T(8,128)(2,1)S(1)}, bf16[2,2,1024,1024]{3,2,1,0:T(8,128)(2,1)}, u32[]{:S(2)}) copy-start(bf16[2,2,1024,1024]{3,2,1,0:T(8,128)(2,1)} %operator_ref.1) | copy-start | bytes 25165828
  2.0 22.3 %copy-start.1 = (f32[128,2048]{1,0:T(8,128)S(1)}, f32[128,2048]{1,0:T(8,128)}, u32[]{:S(2)}) copy-start(f32[128,2048]{1,0:T(8,128)} %gathers_ref.3) | copy-start | bytes 3145732
  2.0 22.3 %copy-start.2 = (bf16[192,2048]{1,0:T(8,128)(2,1)S(1)}, bf16[192,2048]{1,0:T(8,128)(2,1)}, u32[]{:S(2)}) copy-start(bf16[192,2048]{1,0:T(8,128)(2,1)} %constant.8.clone.table_ref) | copy-start | bytes 2359300

commit v12 on v8

--- a/solution.py
+++ b/solution.py
@@ -12,6 +12,7 @@
 
 FIRST = 40
 REACH = 4
+SPAN = 256
 COST = (10**11, 40_000_000)
 VMEM_LIMIT = 32 * 1024 * 1024
 
@@ -82,32 +83,30 @@
 def spectrum_kernel(chunk, gathers_ref, table_ref, out_ref, held, table, sems):
     length = gathers_ref.shape[1]
     rows = table_ref.shape[0] // 2
-    copies = []
-    for step in range(length // chunk):
-        part = pl.ds(step * chunk, chunk)
-        copies.append(
-            (
-                pltpu.make_async_copy(gathers_ref.at[:, part], held.at[:, part], sems.at[0, step]),
-                pltpu.make_async_copy(table_ref.at[:, part], table.at[:, part], sems.at[1, step]),
-            )
-        )
-    for pair in copies:
-        for copy in pair:
-            copy.start()
+    copies = [
+        pltpu.make_async_copy(gathers_ref, held, sems.at[0]),
+        pltpu.make_async_copy(table_ref, table, sems.at[1]),
+    ]
+    for copy in copies:
+        copy.start()
+    for copy in copies:
+        copy.wait()
     dot = functools.partial(
         lax.dot_general,
         dimension_numbers=(((1,), (1,)), ((), ())),
         preferred_element_type=jnp.float32,
     )
-    total = jnp.zeros((rows, held.shape[0]), jnp.float32)
-    for step, pair in enumerate(copies):
-        for copy in pair:
-            copy.wait()
-        part = pl.ds(step * chunk, chunk)
+
+    def add(step, total):
+        part = pl.ds(pl.multiple_of(step * chunk, chunk), chunk)
         high, low = split_array(held[:, part])
         weights = table[:, part]
         both = dot(weights, high)
-        total = total + both[:rows] + (both[rows:] + dot(weights[:rows], low))
+        return total + both[:rows] + (both[rows:] + dot(weights[:rows], low))
+
+    total = lax.fori_loop(
+        0, length // chunk, add, jnp.zeros((rows, held.shape[0]), jnp.float32)
+    )
     out_ref[...] = total.astype(jnp.bfloat16).astype(out_ref.dtype).reshape(out_ref.shape)
 
 
@@ -122,6 +121,7 @@
     out_ref,
     coefficient_ref,
     holder,
+    blocks,
 ):
     devices, group_rows, traces = incoming_ref.shape
     slots, _, receivers, _ = operator_ref.shape
@@ -137,18 +137,25 @@
         ]
         columns.append(jnp.concatenate(parts, axis=0))
     spectrum = jnp.concatenate(columns, axis=1).astype(jnp.bfloat16)
-    row_ids = lax.broadcasted_iota(jnp.int32, (rows, receivers), 0)
+    row_ids = lax.broadcasted_iota(jnp.int32, (rows, SPAN), 0)
     dot = functools.partial(
         lax.dot_general,
         dimension_numbers=(((1,), (1,)), ((), ())),
         preferred_element_type=jnp.float32,
     )
-    predicted = jnp.zeros((rows, receivers), jnp.float32)
-    for slot in range(slots):
-        by_real = dot(spectrum, operator_ref[slot, 0])
-        by_imag = swap_pairs(dot(spectrum, operator_ref[slot, 1]))
-        product = jnp.where(row_ids % 2 == 0, by_real - by_imag, by_real + by_imag)
-        predicted = jnp.where(row_ids // 2 % slots == slot, product, predicted)
+
+    @pl.loop(0, receivers // SPAN)
+    def _(index):
+        where = pl.ds(pl.multiple_of(index * SPAN, SPAN), SPAN)
+        block = jnp.zeros((rows, SPAN), jnp.float32)
+        for slot in range(slots):
+            by_real = dot(spectrum, operator_ref[slot, 0, where])
+            by_imag = swap_pairs(dot(spectrum, operator_ref[slot, 1, where]))
+            product = jnp.where(row_ids % 2 == 0, by_real - by_imag, by_real + by_imag)
+            block = jnp.where(row_ids // 2 % slots == slot, product, block)
+        blocks[index] = block
+
+    predicted = jnp.concatenate([blocks[i] for i in range(receivers // SPAN)], axis=1)
     lane_ids = lax.broadcasted_iota(jnp.int32, (rows, receivers), 1) % traces
     edge = jnp.zeros((rows, traces), jnp.float32)
     after = jnp.concatenate([predicted[:, traces:], edge], axis=1)
@@ -186,16 +193,20 @@
     lane_ids = lax.broadcasted_iota(jnp.int32, total.shape, 1)
     mixed = jnp.where(lane_ids < rows, high, total - high)
     stacked = jnp.concatenate([mixed, high[:, :rows]], axis=1).astype(jnp.bfloat16)
-    copies = []
-    for step in range(length // chunk):
-        part = pl.ds(step * chunk, chunk)
+
+    def copy_out(step):
+        part = pl.ds(pl.multiple_of(step * chunk, chunk), chunk)
+        return pltpu.make_async_copy(result.at[:, part], out_ref.at[:, part], sems.at[step])
+
+    @pl.loop(0, length // chunk)
+    def _(step):
+        part = pl.ds(pl.multiple_of(step * chunk, chunk), chunk)
         response = jnp.dot(stacked, table_ref[:, part], preferred_element_type=jnp.float32)
         result[:, part] = gathers_ref[:, part] - response
-        copy = pltpu.make_async_copy(result.at[:, part], out_ref.at[:, part], sems.at[step])
-        copy.start()
-        copies.append(copy)
-    for copy in copies:
-        copy.wait()
+        copy_out(step).start()
+
+    for step in range(length // chunk):
+        copy_out(step).wait()
 
 
 def vmem_spec():
@@ -228,7 +239,7 @@
     group_rows = 2 * slots
     kept_bins = 5 * devices // 4
     offsets, lags = filters.shape[2], filters.shape[3]
-    chunk = length
+    chunk = length // 4
     params = pltpu.CompilerParams(vmem_limit_bytes=VMEM_LIMIT)
     table = row_tables(band_bins, slots, length)
     forward_table = np.concatenate(split_halves(table / math.sqrt(length)), axis=0)
@@ -244,7 +255,7 @@
             scratch_shapes=[
                 pltpu.VMEM((traces, length), jnp.float32),
                 pltpu.VMEM((2 * rows, length), jnp.bfloat16),
-                pltpu.SemaphoreType.DMA((2, length // chunk)),
+                pltpu.SemaphoreType.DMA((2,)),
             ],
             compiler_params=params,
             cost_estimate=pl.CostEstimate(flops=COST[0], bytes_accessed=COST[1], transcendentals=0),
@@ -260,7 +271,12 @@
             ],
             in_specs=[smem_spec()] * 2 + [vmem_spec()] * 4,
             out_specs=[vmem_spec()] * 2,
-            scratch_shapes=[pltpu.SMEM((devices,), jnp.int32)],
+            scratch_shapes=[
+                pltpu.SMEM((devices,), jnp.int32),
+                pltpu.VMEM(
+                    (receivers // SPAN, devices * traces // receivers * group_rows, SPAN), jnp.float32
+                ),
+            ],
             compiler_params=params,
             name="predict",
         )(

time: 25.8 us -> 27.1 us (1.050)
  Pallas kernels: 6.25 us -> 7.56 us
    pallas_call x1, Pallas kernels: 2.92 us -> 3.45 us  [local(): pl.pallas_call(functools.partial(predict_kernel, kept_bins), out_shape=[j...]
    pallas_call x1, Pallas kernels: 1.98 us -> 2.42 us  [local(): pl.pallas_call(functools.partial(spectrum_kernel, chunk), out_shape=jax.S...]
    pallas_call x1, Pallas kernels: 1.36 us -> 1.69 us  [local(): pl.pallas_call(functools.partial(subtract_kernel, length // 4), out_shape...]
where the time goes in v12:
time: 27.1 us; the launch traced here: 26.9 us
  blocking collectives  19.3 us (71%)
  Pallas kernels  7.56 us (28%)
    all_to_all x2, blocking collectives, exchange(): lax.all_to_all(chunks, 'freq', 0, 0, axis_index_groups=[order], tiled=True)  19.3 us
    pallas_call x1, Pallas kernels, local(): pl.pallas_call(functools.partial(predict_kernel, kept_bins), out_shape=[j...  3.45 us
    pallas_call x1, Pallas kernels, local(): pl.pallas_call(functools.partial(spectrum_kernel, chunk), out_shape=jax.S...  2.42 us
    pallas_call x1, Pallas kernels, local(): pl.pallas_call(functools.partial(subtract_kernel, length // 4), out_shape...  1.69 us

profile of v12, /device:TPU:0, one launch (start us, length us, event | category | flops | bytes accessed | tf_op | source)
XLA Modules:
  0.0 26.9 jit_solution(7530500756739779439)
XLA Ops:
  0.0 0.0 copy-start.3
  0.0 0.0 copy-start.6
  0.0 0.0 copy-start.5
  0.0 0.0 copy-start.4
  0.0 0.0 copy-start
  0.0 2.4 %spectrum.1 = f32[16,4,128]{2,1,0:T(4,128)S(1)} custom-call(f32[128,2048]{1,0:T(8,128)} %gathers_ref.3, bf16[128,2048]{1,0:T(8,128)(2,1)} %constant.6.clone.table_ref), custom_call_target="tpu_custom_call" | custom-call | flops 99999997952 | bytes 40000000 | tf_op jit(solution)/shard_map/spectrum/spectrum/pallas_call | solution.py:250
  2.4 0.0 copy-start.1
  2.5 0.0 copy-start.2
  2.5 10.7 %all_to_all.10.incoming_ref = f32[16,4,128]{2,1,0:T(4,128)S(1)} all-to-all(f32[16,4,128]{2,1,0:T(4,128)S(1)} %spectrum.1), channel_id=1, replica_groups={{15,14,13,12,11,10,9,8,7,6,5,4,3,2,1,0},{31,30,29,28,27,26,25,24,23,22,..., dimensions={0} | all-to-all | bytes 65536 | tf_op jit(solution)/shard_map/all_to_all | solution.py:230
  13.2 0.0 copy-done.3
  13.2 0.0 copy-done.6
  13.2 0.0 copy-done.5
  13.2 0.0 copy-done.4
  13.2 0.0 copy-done
  13.2 3.5 %predict.1 = (bf16[16,8,128]{2,1,0:T(8,128)(2,1)S(1)}, f32[9,128]{1,0:T(8,128)S(1)}) custom-call(s32[16]{0:T(128)S(1)} %copy-done.5, s32[16]{0:T(128)S(1)} %copy-done.6, f32[9,4,31]{2,1,0:T(4,128)S(1)} %bitcast.3, f32[124,128]{1,0:T(8,128)S(1)} %copy-done.3, f32[16,4,128]{2,1,0:T(4,128)S(1)} %all_to_all.10.incoming_ref, bf16[2,2,1024,1024]{3,2,1,0:T(8,128)(2,1)S(1)} %copy-done), custom_call_target="tpu_custom_call" | custom-call | tf_op jit(solution)/shard_map/predict/predict/pallas_call | solution.py:266
  16.7 8.5 %all_to_all.11.returned_ref = bf16[16,8,128]{2,1,0:T(8,128)(2,1)S(1)} all-to-all(bf16[16,8,128]{2,1,0:T(8,128)(2,1)S(1)} %get-tuple-element.7), channel_id=1, replica_groups={{15,14,13,12,11,10,9,8,7,6,5,4,3,2,1,0},{31,30,29,28,27,26,25,24,23,22,..., dimensions={0} | all-to-all | bytes 65536 | tf_op jit(solution)/shard_map/all_to_all | solution.py:230
  25.2 0.0 copy-done.1
  25.2 0.0 copy-done.2
  25.2 1.7 %subtract.1 = f32[128,2048]{1,0:T(8,128)} custom-call(bf16[16,8,128]{2,1,0:T(8,128)(2,1)S(1)} %all_to_all.11.returned_ref, f32[9,128]{1,0:T(8,128)S(1)} %get-tuple-element.8.coefficient_ref, bf16[192,2048]{1,0:T(8,128)(2,1)S(1)} %copy-done.2, f32[128,2048]{1,0:T(8,128)S(1)} %copy-done.1), custom_call_target="tpu_custom_call" | custom-call | tf_op jit(solution)/shard_map/subtract/subtract/pallas_call | solution.py:292
Async XLA Ops:
  0.0 13.2 %copy-start.3 = (f32[124,128]{1,0:T(8,128)S(1)}, f32[124,128]{1,0:T(8,128)}, u32[]{:S(2)}) copy-start(f32[124,128]{1,0:T(8,128)} %constant.7.clone.lag_ref) | copy-start | bytes 190468
  0.0 13.2 %copy-start.6 = (s32[16]{0:T(128)S(1)}, s32[16]{0:T(128)}, u32[]{:S(2)}) copy-start(s32[16]{0:T(128)} %slice_ref.1) | copy-start | bytes 196
  0.0 13.2 %copy-start.5 = (s32[16]{0:T(128)S(1)}, s32[16]{0:T(128)}, u32[]{:S(2)}) copy-start(s32[16]{0:T(128)} %tile_ref.1) | copy-start | bytes 196
  0.0 13.2 %copy-start.4 = (f32[1,4,9,31]{3,1,2,0:T(4,128)S(1)}, f32[1,4,9,31]{3,1,2,0:T(4,128)}, u32[]{:S(2)}) copy-start(f32[1,4,9,31]{3,1,2,0:T(4,128)} %param.10) | copy-start | bytes 13396
  0.0 13.2 %copy-start = (bf16[2,2,1024,1024]{3,2,1,0:T(8,128)(2,1)S(1)}, bf16[2,2,1024,1024]{3,2,1,0:T(8,128)(2,1)}, u32[]{:S(2)}) copy-start(bf16[2,2,1024,1024]{3,2,1,0:T(8,128)(2,1)} %operator_ref.1) | copy-start | bytes 25165828
  2.4 22.8 %copy-start.1 = (f32[128,2048]{1,0:T(8,128)S(1)}, f32[128,2048]{1,0:T(8,128)}, u32[]{:S(2)}) copy-start(f32[128,2048]{1,0:T(8,128)} %gathers_ref.3) | copy-start | bytes 3145732
  2.5 22.8 %copy-start.2 = (bf16[192,2048]{1,0:T(8,128)(2,1)S(1)}, bf16[192,2048]{1,0:T(8,128)(2,1)}, u32[]{:S(2)}) copy-start(bf16[192,2048]{1,0:T(8,128)(2,1)} %constant.8.clone.table_ref) | copy-start | bytes 2359300

commit v13 on v8

--- a/solution.py
+++ b/solution.py
@@ -23,18 +23,18 @@
     return high, low
 
 
-def bins_in_order(band_bins, slots):
-    return FIRST + np.arange(band_bins).reshape(-1, slots)[::-1].reshape(-1)
-
-
-def row_tables(band_bins, slots, length):
-    bin_ids = bins_in_order(band_bins, slots)
-    angles = 2.0 * np.pi / length * (bin_ids[:, None] * np.arange(length)[None, :] % length)
-    return np.stack([np.cos(angles), -np.sin(angles)], axis=1).reshape(2 * band_bins, length)
-
-
-def lag_tables(band_bins, slots, lags, length):
-    bin_ids = bins_in_order(band_bins, slots)
+def bins_by_parity(devices, slots):
+    groups = FIRST + np.arange(devices * slots).reshape(devices, slots)[::-1]
+    return np.stack([groups[:, groups[0] % 2 == parity].reshape(-1) for parity in range(2)])
+
+
+def half_tables(bin_ids, length):
+    angles = 2.0 * np.pi / length * (bin_ids[:, None] * np.arange(length // 2)[None, :] % length)
+    return np.stack([np.cos(angles), -np.sin(angles)], axis=1).reshape(-1, length // 2)
+
+
+def lag_tables(bin_ids, lags, length):
+    band_bins = len(bin_ids)
     lag_ids = np.arange(lags) - lags // 2
     angles = 2.0 * np.pi / length * (bin_ids[:, None] * lag_ids[None, :] % length)
     cosine, sine = np.cos(angles), np.sin(angles)
@@ -70,8 +70,10 @@
         flat, lag_ref[...], precision=lax.Precision.HIGHEST, preferred_element_type=jnp.float32
     )
     lane_ids = lax.broadcasted_iota(jnp.int32, (1, lanes), 1) % rows
-    group = lane_ids // (2 * slots)
-    slot = lane_ids // 2 % slots
+    parity = lane_ids // (rows // 2)
+    place = lane_ids % (rows // 2)
+    group = place // slots
+    slot = place % slots // 2 * 2 + (parity + FIRST) % 2
     count = jnp.zeros((1, lanes), jnp.int32)
     devices = rows // (2 * slots)
     for device in range(devices):
@@ -79,36 +81,37 @@
     return total * jnp.where(slot < count, math.sqrt(2.0 / kept_bins), 0.0)
 
 
-def spectrum_kernel(chunk, gathers_ref, table_ref, out_ref, held, table, sems):
-    length = gathers_ref.shape[1]
+def spectrum_kernel(gathers_ref, table_ref, out_ref, held, table, sems):
+    traces, length = gathers_ref.shape
     rows = table_ref.shape[0] // 2
-    copies = []
-    for step in range(length // chunk):
-        part = pl.ds(step * chunk, chunk)
-        copies.append(
-            (
-                pltpu.make_async_copy(gathers_ref.at[:, part], held.at[:, part], sems.at[0, step]),
-                pltpu.make_async_copy(table_ref.at[:, part], table.at[:, part], sems.at[1, step]),
-            )
-        )
-    for pair in copies:
-        for copy in pair:
-            copy.start()
+    devices, group_rows, _ = out_ref.shape
+    copies = [
+        pltpu.make_async_copy(gathers_ref, held, sems.at[0]),
+        pltpu.make_async_copy(table_ref, table, sems.at[1]),
+    ]
+    for copy in copies:
+        copy.start()
+    for copy in copies:
+        copy.wait()
     dot = functools.partial(
         lax.dot_general,
         dimension_numbers=(((1,), (1,)), ((), ())),
         preferred_element_type=jnp.float32,
     )
-    total = jnp.zeros((rows, held.shape[0]), jnp.float32)
-    for step, pair in enumerate(copies):
-        for copy in pair:
-            copy.wait()
-        part = pl.ds(step * chunk, chunk)
-        high, low = split_array(held[:, part])
-        weights = table[:, part]
+    early, late = held[:, : length // 2], held[:, length // 2 :]
+    pieces = []
+    for parity, folded in enumerate((early + late, early - late)):
+        high, low = split_array(folded)
+        weights = table[parity * rows : (parity + 1) * rows]
         both = dot(weights, high)
-        total = total + both[:rows] + (both[rows:] + dot(weights[:rows], low))
-    out_ref[...] = total.astype(jnp.bfloat16).astype(out_ref.dtype).reshape(out_ref.shape)
+        total = both[: rows // 2] + (both[rows // 2 :] + dot(weights[: rows // 2], low))
+        total = total.astype(jnp.bfloat16).astype(out_ref.dtype)
+        pieces.append(total.reshape(devices, group_rows // 2, traces))
+    out_ref[...] = jnp.concatenate(pieces, axis=1)
+
+
+def place_of(slot, slots):
+    return (slot + FIRST) % 2 * (slots // 2) + slot // 2
 
 
 def predict_kernel(
@@ -148,7 +151,7 @@
         by_real = dot(spectrum, operator_ref[slot, 0])
         by_imag = swap_pairs(dot(spectrum, operator_ref[slot, 1]))
         product = jnp.where(row_ids % 2 == 0, by_real - by_imag, by_real + by_imag)
-        predicted = jnp.where(row_ids // 2 % slots == slot, product, predicted)
+        predicted = jnp.where(row_ids // 2 % slots == place_of(slot, slots), product, predicted)
     lane_ids = lax.broadcasted_iota(jnp.int32, (rows, receivers), 1) % traces
     edge = jnp.zeros((rows, traces), jnp.float32)
     after = jnp.concatenate([predicted[:, traces:], edge], axis=1)
@@ -171,8 +174,13 @@
     traces, length = gathers_ref.shape
     offsets = coefficient_ref.shape[0]
     came = returned_ref[...].astype(jnp.float32)
-    own = came[:, :group_rows].reshape(rows, traces)
-    edges = came[:, group_rows:].reshape(rows, traces)
+
+    def by_parity(first):
+        middle, last = first + group_rows // 2, first + group_rows
+        parts = (came[:, first:middle], came[:, middle:last])
+        return jnp.concatenate([part.reshape(rows // 2, traces) for part in parts], axis=0)
+
+    own, edges = by_parity(0), by_parity(group_rows)
     halo = jnp.transpose(jnp.concatenate([edges, swap_pairs(edges)], axis=0))
     spread[0:8] = halo[traces - 8 :]
     spread[8 : 8 + traces] = jnp.transpose(jnp.concatenate([own, swap_pairs(own)], axis=0))
@@ -183,17 +191,23 @@
         total = total + spread[first : first + traces] * coefficient_ref[offset : offset + 1]
     total = total + pltpu.roll(total, rows, 1)
     high = total.astype(jnp.bfloat16).astype(jnp.float32)
-    lane_ids = lax.broadcasted_iota(jnp.int32, total.shape, 1)
-    mixed = jnp.where(lane_ids < rows, high, total - high)
-    stacked = jnp.concatenate([mixed, high[:, :rows]], axis=1).astype(jnp.bfloat16)
+    low = pltpu.roll(total - high, rows // 2, 1)
+    block = lax.broadcasted_iota(jnp.int32, total.shape, 1) // (rows // 2)
+    even = jnp.where(block == 1, low, high).astype(jnp.bfloat16)
+    odd = jnp.where(block == 2, low, high).astype(jnp.bfloat16)
     copies = []
-    for step in range(length // chunk):
+    for step in range(length // 2 // chunk):
         part = pl.ds(step * chunk, chunk)
-        response = jnp.dot(stacked, table_ref[:, part], preferred_element_type=jnp.float32)
-        result[:, part] = gathers_ref[:, part] - response
-        copy = pltpu.make_async_copy(result.at[:, part], out_ref.at[:, part], sems.at[step])
-        copy.start()
-        copies.append(copy)
+        even_part = jnp.dot(even, table_ref[0, :, part], preferred_element_type=jnp.float32)
+        odd_part = jnp.dot(odd, table_ref[1, :, part], preferred_element_type=jnp.float32)
+        for later, response in enumerate((even_part + odd_part, even_part - odd_part)):
+            where = pl.ds(later * (length // 2) + step * chunk, chunk)
+            result[:, where] = gathers_ref[:, where] - response
+            copy = pltpu.make_async_copy(
+                result.at[:, where], out_ref.at[:, where], sems.at[2 * step + later]
+            )
+            copy.start()
+            copies.append(copy)
     for copy in copies:
         copy.wait()
 
@@ -228,23 +242,30 @@
     group_rows = 2 * slots
     kept_bins = 5 * devices // 4
     offsets, lags = filters.shape[2], filters.shape[3]
-    chunk = length
+    chunk = length // 4
     params = pltpu.CompilerParams(vmem_limit_bytes=VMEM_LIMIT)
-    table = row_tables(band_bins, slots, length)
-    forward_table = np.concatenate(split_halves(table / math.sqrt(length)), axis=0)
-    back_high, back_low = split_halves(table)
-    back_table = np.concatenate([back_high, back_high, back_low], axis=0)
-    tables = lag_tables(band_bins, slots, lags, length)
+    bins = bins_by_parity(devices, slots)
+    halves = [half_tables(ids, length) for ids in bins]
+    forward_table = np.concatenate([
+        half for table in halves for half in split_halves(table / math.sqrt(length))
+    ])
+    blank = np.zeros((rows // 2, length // 2), ml_dtypes.bfloat16)
+    (even_high, even_low), (odd_high, odd_low) = [split_halves(table) for table in halves]
+    back_table = np.stack([
+        np.concatenate([even_high, even_high, even_low, blank]),
+        np.concatenate([blank, odd_high, odd_high, odd_low]),
+    ])
+    tables = lag_tables(bins.reshape(-1), lags, length)
     with jax.named_scope("spectrum"):
         outgoing = pl.pallas_call(
-            functools.partial(spectrum_kernel, chunk),
+            spectrum_kernel,
             out_shape=jax.ShapeDtypeStruct((devices, group_rows, traces), jnp.float32),
             in_specs=[hbm_spec()] * 2,
             out_specs=vmem_spec(),
             scratch_shapes=[
                 pltpu.VMEM((traces, length), jnp.float32),
-                pltpu.VMEM((2 * rows, length), jnp.bfloat16),
-                pltpu.SemaphoreType.DMA((2, length // chunk)),
+                pltpu.VMEM((2 * rows, length // 2), jnp.bfloat16),
+                pltpu.SemaphoreType.DMA((2,)),
             ],
             compiler_params=params,
             cost_estimate=pl.CostEstimate(flops=COST[0], bytes_accessed=COST[1], transcendentals=0),
@@ -274,7 +295,7 @@
     returned = exchange(sending)
     with jax.named_scope("subtract"):
         return pl.pallas_call(
-            functools.partial(subtract_kernel, length // 4),
+            functools.partial(subtract_kernel, chunk),
             out_shape=jax.ShapeDtypeStruct((traces, length), jnp.float32),
             in_specs=[vmem_spec()] * 4,
             out_specs=hbm_spec(),

time: 25.8 us -> 25.9 us (level)
  no operation moved by 1% of the time
where the time goes in v13:
time: 25.9 us; the launch traced here: 25.7 us
  blocking collectives  19.3 us (75%)
  Pallas kernels  6.33 us (24%)
    all_to_all x2, blocking collectives, exchange(): lax.all_to_all(chunks, 'freq', 0, 0, axis_index_groups=[order], tiled=True)  19.3 us
    pallas_call x1, Pallas kernels, local(): pl.pallas_call(functools.partial(predict_kernel, kept_bins), out_shape=[j...  2.92 us
    pallas_call x1, Pallas kernels, local(): pl.pallas_call(spectrum_kernel, out_shape=jax.ShapeDtypeStruct((devices,...  1.92 us
    pallas_call x1, Pallas kernels, local(): pl.pallas_call(functools.partial(subtract_kernel, chunk), out_shape=jax.S...  1.49 us

profile of v13, /device:TPU:0, one launch (start us, length us, event | category | flops | bytes accessed | tf_op | source)
XLA Modules:
  0.0 25.7 jit_solution(53659578010009714)
XLA Ops:
  0.0 0.0 copy-start.3
  0.0 0.0 copy-start.6
  0.0 0.0 copy-start.5
  0.0 0.0 copy-start.4
  0.0 0.0 copy-start
  0.0 1.9 %spectrum.1 = f32[16,4,128]{2,1,0:T(4,128)S(1)} custom-call(f32[128,2048]{1,0:T(8,128)} %gathers_ref.3, bf16[128,1024]{1,0:T(8,128)(2,1)} %constant.6.clone.table_ref), custom_call_target="tpu_custom_call" | custom-call | flops 99999997952 | bytes 40000000 | tf_op jit(solution)/shard_map/spectrum/spectrum/pallas_call | solution.py:260
  1.9 0.0 copy-start.1
  2.0 0.0 copy-start.2
  2.0 10.7 %all_to_all.10.incoming_ref = f32[16,4,128]{2,1,0:T(4,128)S(1)} all-to-all(f32[16,4,128]{2,1,0:T(4,128)S(1)} %spectrum.1), channel_id=1, replica_groups={{15,14,13,12,11,10,9,8,7,6,5,4,3,2,1,0},{31,30,29,28,27,26,25,24,23,22,..., dimensions={0} | all-to-all | bytes 65536 | tf_op jit(solution)/shard_map/all_to_all | solution.py:233
  12.7 0.0 copy-done.3
  12.7 0.0 copy-done.6
  12.7 0.0 copy-done.5
  12.7 0.0 copy-done.4
  12.7 0.0 copy-done
  12.7 2.9 %predict.1 = (bf16[16,8,128]{2,1,0:T(8,128)(2,1)S(1)}, f32[9,128]{1,0:T(8,128)S(1)}) custom-call(s32[16]{0:T(128)S(1)} %copy-done.5, s32[16]{0:T(128)S(1)} %copy-done.6, f32[9,4,31]{2,1,0:T(4,128)S(1)} %bitcast.3, f32[124,128]{1,0:T(8,128)S(1)} %copy-done.3, f32[16,4,128]{2,1,0:T(4,128)S(1)} %all_to_all.10.incoming_ref, bf16[2,2,1024,1024]{3,2,1,0:T(8,128)(2,1)S(1)} %copy-done), custom_call_target="tpu_custom_call" | custom-call | tf_op jit(solution)/shard_map/predict/predict/pallas_call | solution.py:276
  15.6 8.5 %all_to_all.11.returned_ref = bf16[16,8,128]{2,1,0:T(8,128)(2,1)S(1)} all-to-all(bf16[16,8,128]{2,1,0:T(8,128)(2,1)S(1)} %get-tuple-element.7), channel_id=1, replica_groups={{15,14,13,12,11,10,9,8,7,6,5,4,3,2,1,0},{31,30,29,28,27,26,25,24,23,22,..., dimensions={0} | all-to-all | bytes 65536 | tf_op jit(solution)/shard_map/all_to_all | solution.py:233
  24.2 0.0 copy-done.1
  24.2 0.0 copy-done.2
  24.2 1.5 %subtract.1 = f32[128,2048]{1,0:T(8,128)} custom-call(bf16[16,8,128]{2,1,0:T(8,128)(2,1)S(1)} %all_to_all.11.returned_ref, f32[9,128]{1,0:T(8,128)S(1)} %get-tuple-element.8.coefficient_ref, bf16[2,128,1024]{2,1,0:T(8,128)(2,1)S(1)} %copy-done.2, f32[128,2048]{1,0:T(8,128)S(1)} %copy-done.1), custom_call_target="tpu_custom_call" | custom-call | tf_op jit(solution)/shard_map/subtract/subtract/pallas_call | solution.py:297
Async XLA Ops:
  0.0 12.7 %copy-start.3 = (f32[124,128]{1,0:T(8,128)S(1)}, f32[124,128]{1,0:T(8,128)}, u32[]{:S(2)}) copy-start(f32[124,128]{1,0:T(8,128)} %constant.7.clone.lag_ref) | copy-start | bytes 190468
  0.0 12.7 %copy-start.6 = (s32[16]{0:T(128)S(1)}, s32[16]{0:T(128)}, u32[]{:S(2)}) copy-start(s32[16]{0:T(128)} %slice_ref.1) | copy-start | bytes 196
  0.0 12.7 %copy-start.5 = (s32[16]{0:T(128)S(1)}, s32[16]{0:T(128)}, u32[]{:S(2)}) copy-start(s32[16]{0:T(128)} %tile_ref.1) | copy-start | bytes 196
  0.0 12.7 %copy-start.4 = (f32[1,4,9,31]{3,1,2,0:T(4,128)S(1)}, f32[1,4,9,31]{3,1,2,0:T(4,128)}, u32[]{:S(2)}) copy-start(f32[1,4,9,31]{3,1,2,0:T(4,128)} %param.10) | copy-start | bytes 13396
  0.0 12.7 %copy-start = (bf16[2,2,1024,1024]{3,2,1,0:T(8,128)(2,1)S(1)}, bf16[2,2,1024,1024]{3,2,1,0:T(8,128)(2,1)}, u32[]{:S(2)}) copy-start(bf16[2,2,1024,1024]{3,2,1,0:T(8,128)(2,1)} %operator_ref.1) | copy-start | bytes 25165828
  1.9 22.2 %copy-start.1 = (f32[128,2048]{1,0:T(8,128)S(1)}, f32[128,2048]{1,0:T(8,128)}, u32[]{:S(2)}) copy-start(f32[128,2048]{1,0:T(8,128)} %gathers_ref.3) | copy-start | bytes 3145732
  2.0 22.2 %copy-start.2 = (bf16[2,128,1024]{2,1,0:T(8,128)(2,1)S(1)}, bf16[2,128,1024]{2,1,0:T(8,128)(2,1)}, u32[]{:S(2)}) copy-start(bf16[2,128,1024]{2,1,0:T(8,128)(2,1)} %constant.8.clone.table_ref) | copy-start | bytes 1572868

commit v14 on v10

--- a/solution.py
+++ b/solution.py
@@ -23,12 +23,16 @@
     return high, low
 
 
+def group_order(root, devices):
+    return [root] + [device for device in range(devices)[::-1] if device != root]
+
+
 def order_out(devices):
-    return list(range(devices))[::-1]
+    return group_order(3 * devices // 4 - 1, devices)
 
 
 def order_back(devices):
-    return [devices - 1] + list(range(devices - 1))
+    return group_order(3 * devices // 4 - 1, devices)
 
 
 def bins_in_order(order, slots):

time: 25.9 us -> 25.8 us (level)
  no operation moved by 1% of the time
where the time goes in v14:
time: 25.8 us; the launch traced here: 25.6 us
  blocking collectives  19.3 us (75%)
  Pallas kernels  6.26 us (24%)
    all_to_all x2, blocking collectives, exchange(): lax.all_to_all(chunks, 'freq', 0, 0, axis_index_groups=[order], tiled=True)  19.3 us
    pallas_call x1, Pallas kernels, local(): pl.pallas_call(functools.partial(predict_kernel, kept_bins), out_shape=[j...  2.92 us
    pallas_call x1, Pallas kernels, local(): pl.pallas_call(functools.partial(spectrum_kernel, chunk), out_shape=jax.S...  1.98 us
    pallas_call x1, Pallas kernels, local(): pl.pallas_call(functools.partial(subtract_kernel, length // 4), out_shape...  1.36 us

profile of v14, /device:TPU:0, one launch (start us, length us, event | category | flops | bytes accessed | tf_op | source)
XLA Modules:
  0.0 25.6 jit_solution(9672349198344354477)
XLA Ops:
  0.0 0.0 copy-start.3
  0.0 0.0 copy-start.6
  0.0 0.0 copy-start.5
  0.0 0.0 copy-start.4
  0.0 0.0 copy-start
  0.0 2.0 %spectrum.1 = f32[16,4,128]{2,1,0:T(4,128)S(1)} custom-call(f32[128,2048]{1,0:T(8,128)} %gathers_ref.3, bf16[128,2048]{1,0:T(8,128)(2,1)} %constant.6.clone.table_ref), custom_call_target="tpu_custom_call" | custom-call | flops 99999997952 | bytes 40000000 | tf_op jit(solution)/shard_map/spectrum/spectrum/pallas_call | solution.py:254
  2.0 0.0 copy-start.1
  2.0 0.0 copy-start.2
  2.0 11.1 %all_to_all.10.incoming_ref = f32[16,4,128]{2,1,0:T(4,128)S(1)} all-to-all(f32[16,4,128]{2,1,0:T(4,128)S(1)} %spectrum.1), channel_id=1, replica_groups={{11,15,14,13,12,10,9,8,7,6,5,4,3,2,1,0},{27,31,30,29,28,26,25,24,23,22,..., dimensions={0} | all-to-all | bytes 65536 | tf_op jit(solution)/shard_map/all_to_all | solution.py:232
  13.2 0.0 copy-done.3
  13.2 0.0 copy-done.6
  13.2 0.0 copy-done.5
  13.2 0.0 copy-done.4
  13.2 0.0 copy-done
  13.2 2.9 %predict.1 = (bf16[16,8,128]{2,1,0:T(8,128)(2,1)S(1)}, f32[9,128]{1,0:T(8,128)S(1)}) custom-call(s32[16]{0:T(128)S(1)} %copy-done.5, s32[16]{0:T(128)S(1)} %copy-done.6, f32[9,4,31]{2,1,0:T(4,128)S(1)} %bitcast.3, f32[124,128]{1,0:T(8,128)S(1)} %copy-done.3, f32[16,4,128]{2,1,0:T(4,128)S(1)} %all_to_all.10.incoming_ref, bf16[2,2,1024,1024]{3,2,1,0:T(8,128)(2,1)S(1)} %copy-done), custom_call_target="tpu_custom_call" | custom-call | tf_op jit(solution)/shard_map/predict/predict/pallas_call | solution.py:270
  16.1 8.1 %all_to_all.11.returned_ref = bf16[16,8,128]{2,1,0:T(8,128)(2,1)S(1)} all-to-all(bf16[16,8,128]{2,1,0:T(8,128)(2,1)S(1)} %get-tuple-element.7), channel_id=1, replica_groups={{11,15,14,13,12,10,9,8,7,6,5,4,3,2,1,0},{27,31,30,29,28,26,25,24,23,22,..., dimensions={0} | all-to-all | bytes 65536 | tf_op jit(solution)/shard_map/all_to_all | solution.py:232
  24.3 0.0 copy-done.1
  24.3 0.0 copy-done.2
  24.3 1.4 %subtract.1 = f32[128,2048]{1,0:T(8,128)} custom-call(bf16[16,8,128]{2,1,0:T(8,128)(2,1)S(1)} %all_to_all.11.returned_ref, f32[9,128]{1,0:T(8,128)S(1)} %get-tuple-element.8.coefficient_ref, bf16[192,2048]{1,0:T(8,128)(2,1)S(1)} %copy-done.2, f32[128,2048]{1,0:T(8,128)S(1)} %copy-done.1), custom_call_target="tpu_custom_call" | custom-call | tf_op jit(solution)/shard_map/subtract/subtract/pallas_call | solution.py:291
Async XLA Ops:
  0.0 13.2 %copy-start.3 = (f32[124,128]{1,0:T(8,128)S(1)}, f32[124,128]{1,0:T(8,128)}, u32[]{:S(2)}) copy-start(f32[124,128]{1,0:T(8,128)} %constant.7.clone.lag_ref) | copy-start | bytes 190468
  0.0 13.2 %copy-start.6 = (s32[16]{0:T(128)S(1)}, s32[16]{0:T(128)}, u32[]{:S(2)}) copy-start(s32[16]{0:T(128)} %slice_ref.1) | copy-start | bytes 196
  0.0 13.2 %copy-start.5 = (s32[16]{0:T(128)S(1)}, s32[16]{0:T(128)}, u32[]{:S(2)}) copy-start(s32[16]{0:T(128)} %tile_ref.1) | copy-start | bytes 196
  0.0 13.2 %copy-start.4 = (f32[1,4,9,31]{3,1,2,0:T(4,128)S(1)}, f32[1,4,9,31]{3,1,2,0:T(4,128)}, u32[]{:S(2)}) copy-start(f32[1,4,9,31]{3,1,2,0:T(4,128)} %param.10) | copy-start | bytes 13396
  0.0 13.2 %copy-start = (bf16[2,2,1024,1024]{3,2,1,0:T(8,128)(2,1)S(1)}, bf16[2,2,1024,1024]{3,2,1,0:T(8,128)(2,1)}, u32[]{:S(2)}) copy-start(bf16[2,2,1024,1024]{3,2,1,0:T(8,128)(2,1)} %operator_ref.1) | copy-start | bytes 25165828
  2.0 22.3 %copy-start.1 = (f32[128,2048]{1,0:T(8,128)S(1)}, f32[128,2048]{1,0:T(8,128)}, u32[]{:S(2)}) copy-start(f32[128,2048]{1,0:T(8,128)} %gathers_ref.3) | copy-start | bytes 3145732
  2.0 22.2 %copy-start.2 = (bf16[192,2048]{1,0:T(8,128)(2,1)S(1)}, bf16[192,2048]{1,0:T(8,128)(2,1)}, u32[]{:S(2)}) copy-start(bf16[192,2048]{1,0:T(8,128)(2,1)} %constant.8.clone.table_ref) | copy-start | bytes 2359300

commit v15 on v14

--- a/solution.py
+++ b/solution.py
@@ -136,7 +136,7 @@
     holder,
 ):
     devices, group_rows, traces = incoming_ref.shape
-    slots, _, receivers, _ = operator_ref.shape
+    slots, receivers = operator_ref.shape[0], 8 * operator_ref.shape[2]
     per_shot = receivers // traces
     shots = devices // per_shot
     rows = shots * group_rows
@@ -150,19 +150,30 @@
             incoming_ref[holder[0, s * per_shot + q]].astype(jnp.float32) for s in range(shots)
         ]
         columns.append(jnp.concatenate(parts, axis=0))
-    spectrum = jnp.concatenate(columns, axis=1).astype(jnp.bfloat16)
+    spectrum = jnp.concatenate(columns, axis=1)
     row_ids = lax.broadcasted_iota(jnp.int32, (rows, receivers), 0)
-    dot = functools.partial(
-        lax.dot_general,
-        dimension_numbers=(((1,), (1,)), ((), ())),
-        preferred_element_type=jnp.float32,
-    )
-    predicted = jnp.zeros((rows, receivers), jnp.float32)
-    for slot in range(slots):
-        by_real = dot(spectrum, operator_ref[slot, 0])
-        by_imag = swap_pairs(dot(spectrum, operator_ref[slot, 1]))
-        product = jnp.where(row_ids % 2 == 0, by_real - by_imag, by_real + by_imag)
-        predicted = jnp.where(row_ids // 2 % slots == slot, product, predicted)
+    partner = swap_pairs(spectrum)
+    partner = jnp.where(row_ids % 2 == 0, -partner, partner)
+    column_ids = lax.broadcasted_iota(jnp.int32, (receivers // 2, 2 * rows), 1)
+    turned = jnp.zeros((2 * receivers, 2 * rows), jnp.float32)
+    for part, side in enumerate((spectrum, partner)):
+        tiles = [side[:, i : i + traces] for i in range(0, receivers, traces)]
+        pairs = [jnp.concatenate(tiles[half::2], axis=1) for half in range(2)]
+        both = jnp.transpose(jnp.concatenate(pairs, axis=0))
+        for slot in range(slots):
+            weights = jnp.where(column_ids // 2 % slots == slot, both, 0.0).astype(jnp.bfloat16)
+            streamed = jnp.concatenate(
+                [
+                    operator_ref[slot, part, :, p].reshape(2 * receivers, traces)
+                    for p in range(receivers // (2 * traces))
+                ],
+                axis=1,
+            )
+            turned = turned + jnp.dot(streamed, weights, preferred_element_type=jnp.float32)
+    halves = turned.reshape(receivers // 8, 2, 8, 2 * rows)
+    first = halves[:, 0].reshape(receivers, 2 * rows)
+    second = halves[:, 1].reshape(receivers, 2 * rows)
+    predicted = jnp.transpose(first)[:rows] + jnp.transpose(second)[rows:]
     lane_ids = lax.broadcasted_iota(jnp.int32, (rows, receivers), 1) % traces
     edge = jnp.zeros((rows, traces), jnp.float32)
     after = jnp.concatenate([predicted[:, traces:], edge], axis=1)
@@ -266,6 +277,8 @@
             name="spectrum",
         )(in_hbm(gathers), in_hbm(jnp.asarray(forward_table)))
     incoming = exchange(outgoing, order_out(devices))
+    stacked = operator.reshape(slots, 2, receivers // 8, 8, receivers // traces, traces)
+    stacked = jnp.swapaxes(stacked, 3, 4).reshape(slots, 2, receivers // 8, -1, 16, traces)
     with jax.named_scope("predict"):
         sending, coefficients = pl.pallas_call(
             functools.partial(predict_kernel, kept_bins),
@@ -284,7 +297,7 @@
             jnp.transpose(filters[0], (1, 0, 2)),
             jnp.asarray(tables),
             incoming,
-            operator,
+            stacked,
         )
     returned = exchange(sending, order_back(devices))
     with jax.named_scope("subtract"):

time: 25.8 us -> 26.1 us (1.012)
  Pallas kernels: 6.26 us -> 6.54 us
    pallas_call x1, Pallas kernels: 2.92 us -> 3.2 us  [local(): pl.pallas_call(functools.partial(predict_kernel, kept_bins), out_shape=[j...]
where the time goes in v15:
time: 26.1 us; the launch traced here: 25.9 us
  blocking collectives  19.3 us (74%)
  Pallas kernels  6.54 us (25%)
    all_to_all x2, blocking collectives, exchange(): lax.all_to_all(chunks, 'freq', 0, 0, axis_index_groups=[order], tiled=True)  19.3 us
    pallas_call x1, Pallas kernels, local(): pl.pallas_call(functools.partial(predict_kernel, kept_bins), out_shape=[j...  3.2 us
    pallas_call x1, Pallas kernels, local(): pl.pallas_call(functools.partial(spectrum_kernel, chunk), out_shape=jax.S...  1.98 us
    pallas_call x1, Pallas kernels, local(): pl.pallas_call(functools.partial(subtract_kernel, length // 4), out_shape...  1.36 us

profile of v15, /device:TPU:0, one launch (start us, length us, event | category | flops | bytes accessed | tf_op | source)
XLA Modules:
  0.0 25.9 jit_solution(1723641780018620781)
XLA Ops:
  0.0 0.0 copy-start.3
  0.0 0.0 copy-start.6
  0.0 0.0 copy-start.5
  0.0 0.0 copy-start.4
  0.0 0.0 copy-start
  0.0 2.0 %spectrum.1 = f32[16,4,128]{2,1,0:T(4,128)S(1)} custom-call(f32[128,2048]{1,0:T(8,128)} %gathers_ref.3, bf16[128,2048]{1,0:T(8,128)(2,1)} %constant.6.clone.table_ref), custom_call_target="tpu_custom_call" | custom-call | flops 99999997952 | bytes 40000000 | tf_op jit(solution)/shard_map/spectrum/spectrum/pallas_call | solution.py:265
  2.0 0.0 copy-start.1
  2.0 0.0 copy-start.2
  2.0 11.1 %all_to_all.10.incoming_ref = f32[16,4,128]{2,1,0:T(4,128)S(1)} all-to-all(f32[16,4,128]{2,1,0:T(4,128)S(1)} %spectrum.1), channel_id=1, replica_groups={{11,15,14,13,12,10,9,8,7,6,5,4,3,2,1,0},{27,31,30,29,28,26,25,24,23,22,..., dimensions={0} | all-to-all | bytes 65536 | tf_op jit(solution)/shard_map/all_to_all | solution.py:243
  13.2 0.0 copy-done.3
  13.2 0.0 copy-done.6
  13.2 0.0 copy-done.5
  13.2 0.0 copy-done.4
  13.2 0.0 copy-done
  13.2 3.2 %predict.1 = (bf16[16,8,128]{2,1,0:T(8,128)(2,1)S(1)}, f32[9,128]{1,0:T(8,128)S(1)}) custom-call(s32[16]{0:T(128)S(1)} %copy-done.5, s32[16]{0:T(128)S(1)} %copy-done.6, f32[9,4,31]{2,1,0:T(4,128)S(1)} %bitcast.9, f32[124,128]{1,0:T(8,128)S(1)} %copy-done.3, f32[16,4,128]{2,1,0:T(4,128)S(1)} %all_to_all.10.incoming_ref, ...), custom_call_target="tpu_custom_call" | custom-call | tf_op jit(solution)/shard_map/predict/predict/pallas_call | solution.py:283
  16.4 8.1 %all_to_all.11.returned_ref = bf16[16,8,128]{2,1,0:T(8,128)(2,1)S(1)} all-to-all(bf16[16,8,128]{2,1,0:T(8,128)(2,1)S(1)} %get-tuple-element.7), channel_id=1, replica_groups={{11,15,14,13,12,10,9,8,7,6,5,4,3,2,1,0},{27,31,30,29,28,26,25,24,23,22,..., dimensions={0} | all-to-all | bytes 65536 | tf_op jit(solution)/shard_map/all_to_all | solution.py:243
  24.5 0.0 copy-done.1
  24.5 0.0 copy-done.2
  24.5 1.4 %subtract.1 = f32[128,2048]{1,0:T(8,128)} custom-call(bf16[16,8,128]{2,1,0:T(8,128)(2,1)S(1)} %all_to_all.11.returned_ref, f32[9,128]{1,0:T(8,128)S(1)} %get-tuple-element.8.coefficient_ref, bf16[192,2048]{1,0:T(8,128)(2,1)S(1)} %copy-done.2, f32[128,2048]{1,0:T(8,128)S(1)} %copy-done.1), custom_call_target="tpu_custom_call" | custom-call | tf_op jit(solution)/shard_map/subtract/subtract/pallas_call | solution.py:304
Async XLA Ops:
  0.0 13.2 %copy-start.3 = (f32[124,128]{1,0:T(8,128)S(1)}, f32[124,128]{1,0:T(8,128)}, u32[]{:S(2)}) copy-start(f32[124,128]{1,0:T(8,128)} %constant.7.clone.lag_ref) | copy-start | bytes 190468
  0.0 13.2 %copy-start.6 = (s32[16]{0:T(128)S(1)}, s32[16]{0:T(128)}, u32[]{:S(2)}) copy-start(s32[16]{0:T(128)} %slice_ref.1) | copy-start | bytes 196
  0.0 13.2 %copy-start.5 = (s32[16]{0:T(128)S(1)}, s32[16]{0:T(128)}, u32[]{:S(2)}) copy-start(s32[16]{0:T(128)} %tile_ref.1) | copy-start | bytes 196
  0.0 13.2 %copy-start.4 = (f32[1,4,9,31]{3,1,2,0:T(4,128)S(1)}, f32[1,4,9,31]{3,1,2,0:T(4,128)}, u32[]{:S(2)}) copy-start(f32[1,4,9,31]{3,1,2,0:T(4,128)} %param.10) | copy-start | bytes 13396
  0.0 13.2 %copy-start = (bf16[2,2,1024,1024]{3,2,1,0:T(8,128)(2,1)S(1)}, bf16[2,2,1024,1024]{3,2,1,0:T(8,128)(2,1)}, u32[]{:S(2)}) copy-start(bf16[2,2,1024,1024]{3,2,1,0:T(8,128)(2,1)} %param.9) | copy-start | bytes 25165828
  2.0 22.5 %copy-start.1 = (f32[128,2048]{1,0:T(8,128)S(1)}, f32[128,2048]{1,0:T(8,128)}, u32[]{:S(2)}) copy-start(f32[128,2048]{1,0:T(8,128)} %gathers_ref.3) | copy-start | bytes 3145732
  2.0 22.5 %copy-start.2 = (bf16[192,2048]{1,0:T(8,128)(2,1)S(1)}, bf16[192,2048]{1,0:T(8,128)(2,1)}, u32[]{:S(2)}) copy-start(bf16[192,2048]{1,0:T(8,128)(2,1)} %constant.8.clone.table_ref) | copy-start | bytes 2359300

commit v16 on v14

--- a/solution.py
+++ b/solution.py
@@ -91,50 +91,51 @@
     return total * jnp.where(slot < count, math.sqrt(2.0 / kept_bins), 0.0)
 
 
-def spectrum_kernel(chunk, gathers_ref, table_ref, out_ref, held, table, sems):
-    length = gathers_ref.shape[1]
+def spectrum_kernel(
+    kept_bins,
+    slots,
+    slice_ref,
+    filters_ref,
+    lag_ref,
+    gathers_ref,
+    table_ref,
+    out_ref,
+    coefficient_ref,
+    counts,
+    filters,
+    lags,
+    held,
+    table,
+    sems,
+):
+    traces = gathers_ref.shape[0]
     rows = table_ref.shape[0] // 2
-    copies = []
-    for step in range(length // chunk):
-        part = pl.ds(step * chunk, chunk)
-        copies.append(
-            (
-                pltpu.make_async_copy(gathers_ref.at[:, part], held.at[:, part], sems.at[0, step]),
-                pltpu.make_async_copy(table_ref.at[:, part], table.at[:, part], sems.at[1, step]),
-            )
-        )
-    for pair in copies:
-        for copy in pair:
-            copy.start()
+    parts = [pl.ds(0, traces // 2), pl.ds(traces // 2, traces // 2)]
+    pairs = [(gathers_ref.at[part], held.at[part]) for part in parts]
+    pairs += [(table_ref, table), (slice_ref, counts), (filters_ref, filters), (lag_ref, lags)]
+    copies = [
+        pltpu.make_async_copy(source, target, sems.at[i])
+        for i, (source, target) in enumerate(pairs)
+    ]
+    for copy in copies:
+        copy.start()
+    for copy in copies[3:]:
+        copy.wait()
+    coefficient_ref[...] = filter_lanes(kept_bins, slots, counts, filters, lags)
+    for copy in copies[:3]:
+        copy.wait()
     dot = functools.partial(
         lax.dot_general,
         dimension_numbers=(((1,), (1,)), ((), ())),
         preferred_element_type=jnp.float32,
     )
-    total = jnp.zeros((rows, held.shape[0]), jnp.float32)
-    for step, pair in enumerate(copies):
-        for copy in pair:
-            copy.wait()
-        part = pl.ds(step * chunk, chunk)
-        high, low = split_array(held[:, part])
-        weights = table[:, part]
-        both = dot(weights, high)
-        total = total + both[:rows] + (both[rows:] + dot(weights[:rows], low))
+    high, low = split_array(held[...])
+    both = dot(table[...], high)
+    total = both[:rows] + (both[rows:] + dot(table[:rows], low))
     out_ref[...] = total.astype(jnp.bfloat16).astype(out_ref.dtype).reshape(out_ref.shape)
 
 
-def predict_kernel(
-    kept_bins,
-    tile_ref,
-    slice_ref,
-    filters_ref,
-    lag_ref,
-    incoming_ref,
-    operator_ref,
-    out_ref,
-    coefficient_ref,
-    holder,
-):
+def predict_kernel(tile_ref, incoming_ref, operator_ref, out_ref, holder):
     devices, group_rows, traces = incoming_ref.shape
     slots, _, receivers, _ = operator_ref.shape
     per_shot = receivers // traces
@@ -173,7 +174,6 @@
             where = (slice(s * group_rows, (s + 1) * group_rows), slice(q * traces, (q + 1) * traces))
             both = jnp.concatenate([predicted[where], halo[where]], axis=0)
             out_ref[holder[1, s * per_shot + q]] = both.astype(jnp.bfloat16)
-    coefficient_ref[...] = filter_lanes(kept_bins, slots, slice_ref, filters_ref, lag_ref)
 
 
 def subtract_kernel(
@@ -241,7 +241,6 @@
     group_rows = 2 * slots
     kept_bins = 5 * devices // 4
     offsets, lags = filters.shape[2], filters.shape[3]
-    chunk = length
     params = pltpu.CompilerParams(vmem_limit_bytes=VMEM_LIMIT)
     bins_out = bins_in_order(order_out(devices), slots)
     bins_back = bins_in_order(order_back(devices), slots)
@@ -251,41 +250,43 @@
     back_table = np.concatenate([back_high, back_high, back_low], axis=0)
     tables = lag_tables(bins_back, lags, length)
     with jax.named_scope("spectrum"):
-        outgoing = pl.pallas_call(
-            functools.partial(spectrum_kernel, chunk),
-            out_shape=jax.ShapeDtypeStruct((devices, group_rows, traces), jnp.float32),
-            in_specs=[hbm_spec()] * 2,
-            out_specs=vmem_spec(),
+        outgoing, coefficients = pl.pallas_call(
+            functools.partial(spectrum_kernel, kept_bins, slots),
+            out_shape=[
+                jax.ShapeDtypeStruct((devices, group_rows, traces), jnp.float32),
+                jax.ShapeDtypeStruct((offsets, 2 * rows), jnp.float32),
+            ],
+            in_specs=[hbm_spec()] * 5,
+            out_specs=[vmem_spec()] * 2,
             scratch_shapes=[
+                pltpu.SMEM(slice_len.shape, jnp.int32),
+                pltpu.VMEM((offsets, filters.shape[1], lags), jnp.float32),
+                pltpu.VMEM(tables.shape, jnp.float32),
                 pltpu.VMEM((traces, length), jnp.float32),
                 pltpu.VMEM((2 * rows, length), jnp.bfloat16),
-                pltpu.SemaphoreType.DMA((2, length // chunk)),
+                pltpu.SemaphoreType.DMA((6,)),
             ],
             compiler_params=params,
             cost_estimate=pl.CostEstimate(flops=COST[0], bytes_accessed=COST[1], transcendentals=0),
             name="spectrum",
-        )(in_hbm(gathers), in_hbm(jnp.asarray(forward_table)))
+        )(
+            in_hbm(slice_len),
+            in_hbm(jnp.transpose(filters[0], (1, 0, 2))),
+            in_hbm(jnp.asarray(tables)),
+            in_hbm(gathers),
+            in_hbm(jnp.asarray(forward_table)),
+        )
     incoming = exchange(outgoing, order_out(devices))
     with jax.named_scope("predict"):
-        sending, coefficients = pl.pallas_call(
-            functools.partial(predict_kernel, kept_bins),
-            out_shape=[
-                jax.ShapeDtypeStruct((devices, 2 * group_rows, traces), jnp.bfloat16),
-                jax.ShapeDtypeStruct((offsets, 2 * rows), jnp.float32),
-            ],
-            in_specs=[smem_spec()] * 2 + [vmem_spec()] * 4,
-            out_specs=[vmem_spec()] * 2,
+        sending = pl.pallas_call(
+            predict_kernel,
+            out_shape=jax.ShapeDtypeStruct((devices, 2 * group_rows, traces), jnp.bfloat16),
+            in_specs=[smem_spec(), vmem_spec(), vmem_spec()],
+            out_specs=vmem_spec(),
             scratch_shapes=[pltpu.SMEM((2, devices), jnp.int32)],
             compiler_params=params,
             name="predict",
-        )(
-            tile_of,
-            slice_len,
-            jnp.transpose(filters[0], (1, 0, 2)),
-            jnp.asarray(tables),
-            incoming,
-            operator,
-        )
+        )(tile_of, incoming, operator)
     returned = exchange(sending, order_back(devices))
     with jax.named_scope("subtract"):
         return pl.pallas_call(

time: 25.8 us -> 26 us (level)
  no operation moved by 1% of the time
where the time goes in v16:
time: 26 us; the launch traced here: 25.8 us
  blocking collectives  19.3 us (74%)
  Pallas kernels  6.51 us (25%)
    all_to_all x2, blocking collectives, exchange(): lax.all_to_all(chunks, 'freq', 0, 0, axis_index_groups=[order], tiled=True)  19.3 us
    pallas_call x1, Pallas kernels, local(): pl.pallas_call(predict_kernel, out_shape=jax.ShapeDtypeStruct((devices, 2...  2.83 us
    pallas_call x1, Pallas kernels, local(): pl.pallas_call(functools.partial(spectrum_kernel, kept_bins, slots), out_...  2.32 us
    pallas_call x1, Pallas kernels, local(): pl.pallas_call(functools.partial(subtract_kernel, length // 4), out_shape...  1.36 us

profile of v16, /device:TPU:0, one launch (start us, length us, event | category | flops | bytes accessed | tf_op | source)
XLA Modules:
  0.0 25.8 jit_solution(17897944608486768151)
XLA Ops:
  0.0 0.0 copy-start
  0.0 0.0 copy-start.3
  0.0 2.3 %spectrum.1 = (f32[16,4,128]{2,1,0:T(4,128)S(1)}, f32[9,128]{1,0:T(8,128)S(1)}) custom-call(s32[16]{0:T(128)} %slice_ref.1, f32[9,4,31]{2,1,0:T(4,128)} %bitcast.3, f32[124,128]{1,0:T(8,128)} %constant.6.clone.lag_ref, f32[128,2048]{1,0:T(8,128)} %gathers_ref.3, bf16[128,2048]{1,0:T(8,128)(2,1)} %constant.7.clone.table_ref), custom_call_target="tpu_custom_call" | custom-call | flops 99999997952 | bytes 40000000 | tf_op jit(solution)/shard_map/spectrum/spectrum/pallas_call | solution.py:253
  2.3 0.0 copy-start.1
  2.3 0.0 copy-start.2
  2.4 11.1 %all_to_all.10.incoming_ref = f32[16,4,128]{2,1,0:T(4,128)S(1)} all-to-all(f32[16,4,128]{2,1,0:T(4,128)S(1)} %get-tuple-element.7), channel_id=1, replica_groups={{11,15,14,13,12,10,9,8,7,6,5,4,3,2,1,0},{27,31,30,29,28,26,25,24,23,22,..., dimensions={0} | all-to-all | bytes 65536 | tf_op jit(solution)/shard_map/all_to_all | solution.py:232
  13.5 0.0 copy-done
  13.5 0.0 copy-done.3
  13.5 2.8 %predict.1 = bf16[16,8,128]{2,1,0:T(8,128)(2,1)S(1)} custom-call(s32[16]{0:T(128)S(1)} %copy-done.3, f32[16,4,128]{2,1,0:T(4,128)S(1)} %all_to_all.10.incoming_ref, bf16[2,2,1024,1024]{3,2,1,0:T(8,128)(2,1)S(1)} %copy-done), custom_call_target="tpu_custom_call" | custom-call | tf_op jit(solution)/shard_map/predict/predict/pallas_call | solution.py:281
  16.3 8.1 %all_to_all.11.returned_ref = bf16[16,8,128]{2,1,0:T(8,128)(2,1)S(1)} all-to-all(bf16[16,8,128]{2,1,0:T(8,128)(2,1)S(1)} %predict.1), channel_id=1, replica_groups={{11,15,14,13,12,10,9,8,7,6,5,4,3,2,1,0},{27,31,30,29,28,26,25,24,23,22,..., dimensions={0} | all-to-all | bytes 65536 | tf_op jit(solution)/shard_map/all_to_all | solution.py:232
  24.5 0.0 copy-done.1
  24.5 0.0 copy-done.2
  24.5 1.4 %subtract.1 = f32[128,2048]{1,0:T(8,128)} custom-call(bf16[16,8,128]{2,1,0:T(8,128)(2,1)S(1)} %all_to_all.11.returned_ref, f32[9,128]{1,0:T(8,128)S(1)} %get-tuple-element.8.coefficient_ref, bf16[192,2048]{1,0:T(8,128)(2,1)S(1)} %copy-done.2, f32[128,2048]{1,0:T(8,128)S(1)} %copy-done.1), custom_call_target="tpu_custom_call" | custom-call | tf_op jit(solution)/shard_map/subtract/subtract/pallas_call | solution.py:292
Async XLA Ops:
  0.0 13.5 %copy-start = (bf16[2,2,1024,1024]{3,2,1,0:T(8,128)(2,1)S(1)}, bf16[2,2,1024,1024]{3,2,1,0:T(8,128)(2,1)}, u32[]{:S(2)}) copy-start(bf16[2,2,1024,1024]{3,2,1,0:T(8,128)(2,1)} %operator_ref.1) | copy-start | bytes 25165828
  0.0 13.5 %copy-start.3 = (s32[16]{0:T(128)S(1)}, s32[16]{0:T(128)}, u32[]{:S(2)}) copy-start(s32[16]{0:T(128)} %tile_ref.1) | copy-start | bytes 196
  2.3 22.1 %copy-start.1 = (f32[128,2048]{1,0:T(8,128)S(1)}, f32[128,2048]{1,0:T(8,128)}, u32[]{:S(2)}) copy-start(f32[128,2048]{1,0:T(8,128)} %gathers_ref.3) | copy-start | bytes 3145732
  2.3 22.1 %copy-start.2 = (bf16[192,2048]{1,0:T(8,128)(2,1)S(1)}, bf16[192,2048]{1,0:T(8,128)(2,1)}, u32[]{:S(2)}) copy-start(bf16[192,2048]{1,0:T(8,128)(2,1)} %constant.8.clone.table_ref) | copy-start | bytes 2359300

commit v17 on v14

--- a/solution.py
+++ b/solution.py
@@ -32,7 +32,7 @@
 
 
 def order_back(devices):
-    return group_order(3 * devices // 4 - 1, devices)
+    return group_order(devices - 1, devices)
 
 
 def bins_in_order(order, slots):

time: 25.8 us -> 25.7 us (level)
  no operation moved by 1% of the time
where the time goes in v17:
time: 25.7 us; the launch traced here: 25.5 us
  blocking collectives  19.2 us (75%)
  Pallas kernels  6.26 us (24%)
    all_to_all x2, blocking collectives, exchange(): lax.all_to_all(chunks, 'freq', 0, 0, axis_index_groups=[order], tiled=True)  19.2 us
    pallas_call x1, Pallas kernels, local(): pl.pallas_call(functools.partial(predict_kernel, kept_bins), out_shape=[j...  2.92 us
    pallas_call x1, Pallas kernels, local(): pl.pallas_call(functools.partial(spectrum_kernel, chunk), out_shape=jax.S...  1.98 us
    pallas_call x1, Pallas kernels, local(): pl.pallas_call(functools.partial(subtract_kernel, length // 4), out_shape...  1.36 us

profile of v17, /device:TPU:0, one launch (start us, length us, event | category | flops | bytes accessed | tf_op | source)
XLA Modules:
  0.0 25.5 jit_solution(12821168915122390723)
XLA Ops:
  0.0 0.0 copy-start.3
  0.0 0.0 copy-start.6
  0.0 0.0 copy-start.5
  0.0 0.0 copy-start.4
  0.0 0.0 copy-start
  0.0 2.0 %spectrum.1 = f32[16,4,128]{2,1,0:T(4,128)S(1)} custom-call(f32[128,2048]{1,0:T(8,128)} %gathers_ref.3, bf16[128,2048]{1,0:T(8,128)(2,1)} %constant.6.clone.table_ref), custom_call_target="tpu_custom_call" | custom-call | flops 99999997952 | bytes 40000000 | tf_op jit(solution)/shard_map/spectrum/spectrum/pallas_call | solution.py:254
  2.0 0.0 copy-start.1
  2.0 0.0 copy-start.2
  2.0 11.1 %all_to_all.10.incoming_ref = f32[16,4,128]{2,1,0:T(4,128)S(1)} all-to-all(f32[16,4,128]{2,1,0:T(4,128)S(1)} %spectrum.1), channel_id=1, replica_groups={{11,15,14,13,12,10,9,8,7,6,5,4,3,2,1,0},{27,31,30,29,28,26,25,24,23,22,..., dimensions={0} | all-to-all | bytes 65536 | tf_op jit(solution)/shard_map/all_to_all | solution.py:232
  13.2 0.0 copy-done.3
  13.2 0.0 copy-done.6
  13.2 0.0 copy-done.5
  13.2 0.0 copy-done.4
  13.2 0.0 copy-done
  13.2 2.9 %predict.1 = (bf16[16,8,128]{2,1,0:T(8,128)(2,1)S(1)}, f32[9,128]{1,0:T(8,128)S(1)}) custom-call(s32[16]{0:T(128)S(1)} %copy-done.5, s32[16]{0:T(128)S(1)} %copy-done.6, f32[9,4,31]{2,1,0:T(4,128)S(1)} %bitcast.3, f32[124,128]{1,0:T(8,128)S(1)} %copy-done.3, f32[16,4,128]{2,1,0:T(4,128)S(1)} %all_to_all.10.incoming_ref, bf16[2,2,1024,1024]{3,2,1,0:T(8,128)(2,1)S(1)} %copy-done), custom_call_target="tpu_custom_call" | custom-call | tf_op jit(solution)/shard_map/predict/predict/pallas_call | solution.py:270
  16.1 8.0 %all_to_all.11.returned_ref = bf16[16,8,128]{2,1,0:T(8,128)(2,1)S(1)} all-to-all(bf16[16,8,128]{2,1,0:T(8,128)(2,1)S(1)} %get-tuple-element.7), channel_id=1, replica_groups={{15,14,13,12,11,10,9,8,7,6,5,4,3,2,1,0},{31,30,29,28,27,26,25,24,23,22,..., dimensions={0} | all-to-all | bytes 65536 | tf_op jit(solution)/shard_map/all_to_all | solution.py:232
  24.1 0.0 copy-done.1
  24.2 0.0 copy-done.2
  24.2 1.4 %subtract.1 = f32[128,2048]{1,0:T(8,128)} custom-call(bf16[16,8,128]{2,1,0:T(8,128)(2,1)S(1)} %all_to_all.11.returned_ref, f32[9,128]{1,0:T(8,128)S(1)} %get-tuple-element.8.coefficient_ref, bf16[192,2048]{1,0:T(8,128)(2,1)S(1)} %copy-done.2, f32[128,2048]{1,0:T(8,128)S(1)} %copy-done.1), custom_call_target="tpu_custom_call" | custom-call | tf_op jit(solution)/shard_map/subtract/subtract/pallas_call | solution.py:291
Async XLA Ops:
  0.0 13.2 %copy-start.3 = (f32[124,128]{1,0:T(8,128)S(1)}, f32[124,128]{1,0:T(8,128)}, u32[]{:S(2)}) copy-start(f32[124,128]{1,0:T(8,128)} %constant.7.clone.lag_ref) | copy-start | bytes 190468
  0.0 13.2 %copy-start.6 = (s32[16]{0:T(128)S(1)}, s32[16]{0:T(128)}, u32[]{:S(2)}) copy-start(s32[16]{0:T(128)} %slice_ref.1) | copy-start | bytes 196
  0.0 13.2 %copy-start.5 = (s32[16]{0:T(128)S(1)}, s32[16]{0:T(128)}, u32[]{:S(2)}) copy-start(s32[16]{0:T(128)} %tile_ref.1) | copy-start | bytes 196
  0.0 13.2 %copy-start.4 = (f32[1,4,9,31]{3,1,2,0:T(4,128)S(1)}, f32[1,4,9,31]{3,1,2,0:T(4,128)}, u32[]{:S(2)}) copy-start(f32[1,4,9,31]{3,1,2,0:T(4,128)} %param.10) | copy-start | bytes 13396
  0.0 13.2 %copy-start = (bf16[2,2,1024,1024]{3,2,1,0:T(8,128)(2,1)S(1)}, bf16[2,2,1024,1024]{3,2,1,0:T(8,128)(2,1)}, u32[]{:S(2)}) copy-start(bf16[2,2,1024,1024]{3,2,1,0:T(8,128)(2,1)} %operator_ref.1) | copy-start | bytes 25165828
  2.0 22.2 %copy-start.1 = (f32[128,2048]{1,0:T(8,128)S(1)}, f32[128,2048]{1,0:T(8,128)}, u32[]{:S(2)}) copy-start(f32[128,2048]{1,0:T(8,128)} %gathers_ref.3) | copy-start | bytes 3145732
  2.0 22.1 %copy-start.2 = (bf16[192,2048]{1,0:T(8,128)(2,1)S(1)}, bf16[192,2048]{1,0:T(8,128)(2,1)}, u32[]{:S(2)}) copy-start(bf16[192,2048]{1,0:T(8,128)(2,1)} %constant.8.clone.table_ref) | copy-start | bytes 2359300

commit v18 on v17

--- a/solution.py
+++ b/solution.py
@@ -91,36 +91,33 @@
     return total * jnp.where(slot < count, math.sqrt(2.0 / kept_bins), 0.0)
 
 
-def spectrum_kernel(chunk, gathers_ref, table_ref, out_ref, held, table, sems):
-    length = gathers_ref.shape[1]
+def spectrum_kernel(gathers_ref, table_ref, out_ref, held, table, sems):
+    traces, length = gathers_ref.shape
     rows = table_ref.shape[0] // 2
-    copies = []
-    for step in range(length // chunk):
-        part = pl.ds(step * chunk, chunk)
-        copies.append(
-            (
-                pltpu.make_async_copy(gathers_ref.at[:, part], held.at[:, part], sems.at[0, step]),
-                pltpu.make_async_copy(table_ref.at[:, part], table.at[:, part], sems.at[1, step]),
-            )
-        )
-    for pair in copies:
-        for copy in pair:
-            copy.start()
+    devices, group_rows, _ = out_ref.shape
+    copies = [
+        pltpu.make_async_copy(gathers_ref, held, sems.at[0]),
+        pltpu.make_async_copy(table_ref, table, sems.at[1]),
+    ]
+    for copy in copies:
+        copy.start()
+    for copy in copies:
+        copy.wait()
     dot = functools.partial(
         lax.dot_general,
         dimension_numbers=(((1,), (1,)), ((), ())),
         preferred_element_type=jnp.float32,
     )
-    total = jnp.zeros((rows, held.shape[0]), jnp.float32)
-    for step, pair in enumerate(copies):
-        for copy in pair:
-            copy.wait()
-        part = pl.ds(step * chunk, chunk)
-        high, low = split_array(held[:, part])
-        weights = table[:, part]
+    early, late = held[:, : length // 2], held[:, length // 2 :]
+    pieces = []
+    for parity, folded in enumerate((early + late, early - late)):
+        high, low = split_array(folded)
+        weights = table[parity * rows : (parity + 1) * rows]
         both = dot(weights, high)
-        total = total + both[:rows] + (both[rows:] + dot(weights[:rows], low))
-    out_ref[...] = total.astype(jnp.bfloat16).astype(out_ref.dtype).reshape(out_ref.shape)
+        total = both[: rows // 2] + (both[rows // 2 :] + dot(weights[: rows // 2], low))
+        total = total.astype(jnp.bfloat16).astype(out_ref.dtype)
+        pieces.append(total.reshape(devices, group_rows // 2, traces))
+    out_ref[...] = jnp.concatenate(pieces, axis=1)
 
 
 def predict_kernel(
@@ -201,8 +198,10 @@
     mixed = jnp.where(lane_ids < rows, high, total - high)
     stacked = jnp.concatenate([mixed, high[:, :rows]], axis=1).astype(jnp.bfloat16)
     copies = []
-    for step in range(length // chunk):
-        part = pl.ds(step * chunk, chunk)
+    start = 0
+    for step, width in enumerate((3 * chunk, 2 * chunk, 2 * chunk, chunk)):
+        part = pl.ds(start, width)
+        start += width
         response = jnp.dot(stacked, table_ref[:, part], preferred_element_type=jnp.float32)
         result[:, part] = gathers_ref[:, part] - response
         copy = pltpu.make_async_copy(result.at[:, part], out_ref.at[:, part], sems.at[step])
@@ -241,25 +240,30 @@
     group_rows = 2 * slots
     kept_bins = 5 * devices // 4
     offsets, lags = filters.shape[2], filters.shape[3]
-    chunk = length
     params = pltpu.CompilerParams(vmem_limit_bytes=VMEM_LIMIT)
     bins_out = bins_in_order(order_out(devices), slots)
     bins_back = bins_in_order(order_back(devices), slots)
-    forward = row_tables(bins_out, length) / math.sqrt(length)
-    forward_table = np.concatenate(split_halves(forward), axis=0)
+    forward_table = np.concatenate([
+        half
+        for parity in range(2)
+        for half in split_halves(
+            row_tables(bins_out[bins_out % 2 == parity], length)[:, : length // 2]
+            / math.sqrt(length)
+        )
+    ])
     back_high, back_low = split_halves(row_tables(bins_back, length))
     back_table = np.concatenate([back_high, back_high, back_low], axis=0)
     tables = lag_tables(bins_back, lags, length)
     with jax.named_scope("spectrum"):
         outgoing = pl.pallas_call(
-            functools.partial(spectrum_kernel, chunk),
+            spectrum_kernel,
             out_shape=jax.ShapeDtypeStruct((devices, group_rows, traces), jnp.float32),
             in_specs=[hbm_spec()] * 2,
             out_specs=vmem_spec(),
             scratch_shapes=[
                 pltpu.VMEM((traces, length), jnp.float32),
-                pltpu.VMEM((2 * rows, length), jnp.bfloat16),
-                pltpu.SemaphoreType.DMA((2, length // chunk)),
+                pltpu.VMEM((2 * rows, length // 2), jnp.bfloat16),
+                pltpu.SemaphoreType.DMA((2,)),
             ],
             compiler_params=params,
             cost_estimate=pl.CostEstimate(flops=COST[0], bytes_accessed=COST[1], transcendentals=0),
@@ -289,7 +293,7 @@
     returned = exchange(sending, order_back(devices))
     with jax.named_scope("subtract"):
         return pl.pallas_call(
-            functools.partial(subtract_kernel, length // 4),
+            functools.partial(subtract_kernel, length // 8),
             out_shape=jax.ShapeDtypeStruct((traces, length), jnp.float32),
             in_specs=[vmem_spec()] * 4,
             out_specs=hbm_spec(),

time: 25.7 us -> 25.7 us (level)
  no operation moved by 1% of the time
where the time goes in v18:
time: 25.7 us; the launch traced here: 25.5 us
  blocking collectives  19.2 us (75%)
  Pallas kernels  6.24 us (24%)
    all_to_all x2, blocking collectives, exchange(): lax.all_to_all(chunks, 'freq', 0, 0, axis_index_groups=[order], tiled=True)  19.2 us
    pallas_call x1, Pallas kernels, local(): pl.pallas_call(functools.partial(predict_kernel, kept_bins), out_shape=[j...  2.92 us
    pallas_call x1, Pallas kernels, local(): pl.pallas_call(spectrum_kernel, out_shape=jax.ShapeDtypeStruct((devices,...  1.92 us
    pallas_call x1, Pallas kernels, local(): pl.pallas_call(functools.partial(subtract_kernel, length // 8), out_shape...  1.4 us

profile of v18, /device:TPU:0, one launch (start us, length us, event | category | flops | bytes accessed | tf_op | source)
XLA Modules:
  0.0 25.5 jit_solution(6787858896068161729)
XLA Ops:
  0.0 0.0 copy-start.3
  0.0 0.0 copy-start.6
  0.0 0.0 copy-start.5
  0.0 0.0 copy-start.4
  0.0 0.0 copy-start
  0.0 1.9 %spectrum.1 = f32[16,4,128]{2,1,0:T(4,128)S(1)} custom-call(f32[128,2048]{1,0:T(8,128)} %gathers_ref.3, bf16[128,1024]{1,0:T(8,128)(2,1)} %constant.6.clone.table_ref), custom_call_target="tpu_custom_call" | custom-call | flops 99999997952 | bytes 40000000 | tf_op jit(solution)/shard_map/spectrum/spectrum/pallas_call | solution.py:258
  1.9 0.0 copy-start.1
  2.0 0.0 copy-start.2
  2.0 11.1 %all_to_all.10.incoming_ref = f32[16,4,128]{2,1,0:T(4,128)S(1)} all-to-all(f32[16,4,128]{2,1,0:T(4,128)S(1)} %spectrum.1), channel_id=1, replica_groups={{11,15,14,13,12,10,9,8,7,6,5,4,3,2,1,0},{27,31,30,29,28,26,25,24,23,22,..., dimensions={0} | all-to-all | bytes 65536 | tf_op jit(solution)/shard_map/all_to_all | solution.py:231
  13.1 0.0 copy-done.3
  13.1 0.0 copy-done.6
  13.1 0.0 copy-done.5
  13.1 0.0 copy-done.4
  13.1 0.0 copy-done
  13.1 2.9 %predict.1 = (bf16[16,8,128]{2,1,0:T(8,128)(2,1)S(1)}, f32[9,128]{1,0:T(8,128)S(1)}) custom-call(s32[16]{0:T(128)S(1)} %copy-done.5, s32[16]{0:T(128)S(1)} %copy-done.6, f32[9,4,31]{2,1,0:T(4,128)S(1)} %bitcast.3, f32[124,128]{1,0:T(8,128)S(1)} %copy-done.3, f32[16,4,128]{2,1,0:T(4,128)S(1)} %all_to_all.10.incoming_ref, bf16[2,2,1024,1024]{3,2,1,0:T(8,128)(2,1)S(1)} %copy-done), custom_call_target="tpu_custom_call" | custom-call | tf_op jit(solution)/shard_map/predict/predict/pallas_call | solution.py:274
  16.1 8.0 %all_to_all.11.returned_ref = bf16[16,8,128]{2,1,0:T(8,128)(2,1)S(1)} all-to-all(bf16[16,8,128]{2,1,0:T(8,128)(2,1)S(1)} %get-tuple-element.7), channel_id=1, replica_groups={{15,14,13,12,11,10,9,8,7,6,5,4,3,2,1,0},{31,30,29,28,27,26,25,24,23,22,..., dimensions={0} | all-to-all | bytes 65536 | tf_op jit(solution)/shard_map/all_to_all | solution.py:231
  24.1 0.0 copy-done.1
  24.1 0.0 copy-done.2
  24.1 1.4 %subtract.1 = f32[128,2048]{1,0:T(8,128)} custom-call(bf16[16,8,128]{2,1,0:T(8,128)(2,1)S(1)} %all_to_all.11.returned_ref, f32[9,128]{1,0:T(8,128)S(1)} %get-tuple-element.8.coefficient_ref, bf16[192,2048]{1,0:T(8,128)(2,1)S(1)} %copy-done.2, f32[128,2048]{1,0:T(8,128)S(1)} %copy-done.1), custom_call_target="tpu_custom_call" | custom-call | tf_op jit(solution)/shard_map/subtract/subtract/pallas_call | solution.py:295
Async XLA Ops:
  0.0 13.1 %copy-start.3 = (f32[124,128]{1,0:T(8,128)S(1)}, f32[124,128]{1,0:T(8,128)}, u32[]{:S(2)}) copy-start(f32[124,128]{1,0:T(8,128)} %constant.7.clone.lag_ref) | copy-start | bytes 190468
  0.0 13.1 %copy-start.6 = (s32[16]{0:T(128)S(1)}, s32[16]{0:T(128)}, u32[]{:S(2)}) copy-start(s32[16]{0:T(128)} %slice_ref.1) | copy-start | bytes 196
  0.0 13.1 %copy-start.5 = (s32[16]{0:T(128)S(1)}, s32[16]{0:T(128)}, u32[]{:S(2)}) copy-start(s32[16]{0:T(128)} %tile_ref.1) | copy-start | bytes 196
  0.0 13.1 %copy-start.4 = (f32[1,4,9,31]{3,1,2,0:T(4,128)S(1)}, f32[1,4,9,31]{3,1,2,0:T(4,128)}, u32[]{:S(2)}) copy-start(f32[1,4,9,31]{3,1,2,0:T(4,128)} %param.10) | copy-start | bytes 13396
  0.0 13.1 %copy-start = (bf16[2,2,1024,1024]{3,2,1,0:T(8,128)(2,1)S(1)}, bf16[2,2,1024,1024]{3,2,1,0:T(8,128)(2,1)}, u32[]{:S(2)}) copy-start(bf16[2,2,1024,1024]{3,2,1,0:T(8,128)(2,1)} %operator_ref.1) | copy-start | bytes 25165828
  1.9 22.2 %copy-start.1 = (f32[128,2048]{1,0:T(8,128)S(1)}, f32[128,2048]{1,0:T(8,128)}, u32[]{:S(2)}) copy-start(f32[128,2048]{1,0:T(8,128)} %gathers_ref.3) | copy-start | bytes 3145732
  2.0 22.1 %copy-start.2 = (bf16[192,2048]{1,0:T(8,128)(2,1)S(1)}, bf16[192,2048]{1,0:T(8,128)(2,1)}, u32[]{:S(2)}) copy-start(bf16[192,2048]{1,0:T(8,128)(2,1)} %constant.8.clone.table_ref) | copy-start | bytes 2359300

commit v19 on v18

--- a/solution.py
+++ b/solution.py
@@ -155,9 +155,13 @@
         preferred_element_type=jnp.float32,
     )
     predicted = jnp.zeros((rows, receivers), jnp.float32)
+    products = dot(spectrum, operator_ref[...].reshape(2 * slots * receivers, receivers))
     for slot in range(slots):
-        by_real = dot(spectrum, operator_ref[slot, 0])
-        by_imag = swap_pairs(dot(spectrum, operator_ref[slot, 1]))
+        by_real, by_imag = (
+            products[:, (2 * slot + part) * receivers : (2 * slot + part + 1) * receivers]
+            for part in range(2)
+        )
+        by_imag = swap_pairs(by_imag)
         product = jnp.where(row_ids % 2 == 0, by_real - by_imag, by_real + by_imag)
         predicted = jnp.where(row_ids // 2 % slots == slot, product, predicted)
     lane_ids = lax.broadcasted_iota(jnp.int32, (rows, receivers), 1) % traces

time: 25.7 us -> 25.7 us (level)
  no operation moved by 1% of the time
where the time goes in v19:
time: 25.7 us; the launch traced here: 25.5 us
  blocking collectives  19.2 us (75%)
  Pallas kernels  6.24 us (24%)
    all_to_all x2, blocking collectives, exchange(): lax.all_to_all(chunks, 'freq', 0, 0, axis_index_groups=[order], tiled=True)  19.2 us
    pallas_call x1, Pallas kernels, local(): pl.pallas_call(functools.partial(predict_kernel, kept_bins), out_shape=[j...  2.92 us
    pallas_call x1, Pallas kernels, local(): pl.pallas_call(spectrum_kernel, out_shape=jax.ShapeDtypeStruct((devices,...  1.92 us
    pallas_call x1, Pallas kernels, local(): pl.pallas_call(functools.partial(subtract_kernel, length // 8), out_shape...  1.4 us

profile of v19, /device:TPU:0, one launch (start us, length us, event | category | flops | bytes accessed | tf_op | source)
XLA Modules:
  0.0 25.5 jit_solution(6787858896068161729)
XLA Ops:
  0.0 0.0 copy-start.3
  0.0 0.0 copy-start.6
  0.0 0.0 copy-start.5
  0.0 0.0 copy-start.4
  0.0 0.0 copy-start
  0.0 1.9 %spectrum.1 = f32[16,4,128]{2,1,0:T(4,128)S(1)} custom-call(f32[128,2048]{1,0:T(8,128)} %gathers_ref.3, bf16[128,1024]{1,0:T(8,128)(2,1)} %constant.6.clone.table_ref), custom_call_target="tpu_custom_call" | custom-call | flops 99999997952 | bytes 40000000 | tf_op jit(solution)/shard_map/spectrum/spectrum/pallas_call | solution.py:262
  1.9 0.0 copy-start.1
  2.0 0.0 copy-start.2
  2.0 11.1 %all_to_all.10.incoming_ref = f32[16,4,128]{2,1,0:T(4,128)S(1)} all-to-all(f32[16,4,128]{2,1,0:T(4,128)S(1)} %spectrum.1), channel_id=1, replica_groups={{11,15,14,13,12,10,9,8,7,6,5,4,3,2,1,0},{27,31,30,29,28,26,25,24,23,22,..., dimensions={0} | all-to-all | bytes 65536 | tf_op jit(solution)/shard_map/all_to_all | solution.py:235
  13.1 0.0 copy-done.3
  13.1 0.0 copy-done.6
  13.1 0.0 copy-done.5
  13.1 0.0 copy-done.4
  13.1 0.0 copy-done
  13.1 2.9 %predict.1 = (bf16[16,8,128]{2,1,0:T(8,128)(2,1)S(1)}, f32[9,128]{1,0:T(8,128)S(1)}) custom-call(s32[16]{0:T(128)S(1)} %copy-done.5, s32[16]{0:T(128)S(1)} %copy-done.6, f32[9,4,31]{2,1,0:T(4,128)S(1)} %bitcast.3, f32[124,128]{1,0:T(8,128)S(1)} %copy-done.3, f32[16,4,128]{2,1,0:T(4,128)S(1)} %all_to_all.10.incoming_ref, bf16[2,2,1024,1024]{3,2,1,0:T(8,128)(2,1)S(1)} %copy-done), custom_call_target="tpu_custom_call" | custom-call | tf_op jit(solution)/shard_map/predict/predict/pallas_call | solution.py:278
  16.1 8.0 %all_to_all.11.returned_ref = bf16[16,8,128]{2,1,0:T(8,128)(2,1)S(1)} all-to-all(bf16[16,8,128]{2,1,0:T(8,128)(2,1)S(1)} %get-tuple-element.7), channel_id=1, replica_groups={{15,14,13,12,11,10,9,8,7,6,5,4,3,2,1,0},{31,30,29,28,27,26,25,24,23,22,..., dimensions={0} | all-to-all | bytes 65536 | tf_op jit(solution)/shard_map/all_to_all | solution.py:235
  24.1 0.0 copy-done.1
  24.1 0.0 copy-done.2
  24.1 1.4 %subtract.1 = f32[128,2048]{1,0:T(8,128)} custom-call(bf16[16,8,128]{2,1,0:T(8,128)(2,1)S(1)} %all_to_all.11.returned_ref, f32[9,128]{1,0:T(8,128)S(1)} %get-tuple-element.8.coefficient_ref, bf16[192,2048]{1,0:T(8,128)(2,1)S(1)} %copy-done.2, f32[128,2048]{1,0:T(8,128)S(1)} %copy-done.1), custom_call_target="tpu_custom_call" | custom-call | tf_op jit(solution)/shard_map/subtract/subtract/pallas_call | solution.py:299
Async XLA Ops:
  0.0 13.1 %copy-start.3 = (f32[124,128]{1,0:T(8,128)S(1)}, f32[124,128]{1,0:T(8,128)}, u32[]{:S(2)}) copy-start(f32[124,128]{1,0:T(8,128)} %constant.7.clone.lag_ref) | copy-start | bytes 190468
  0.0 13.1 %copy-start.6 = (s32[16]{0:T(128)S(1)}, s32[16]{0:T(128)}, u32[]{:S(2)}) copy-start(s32[16]{0:T(128)} %slice_ref.1) | copy-start | bytes 196
  0.0 13.1 %copy-start.5 = (s32[16]{0:T(128)S(1)}, s32[16]{0:T(128)}, u32[]{:S(2)}) copy-start(s32[16]{0:T(128)} %tile_ref.1) | copy-start | bytes 196
  0.0 13.1 %copy-start.4 = (f32[1,4,9,31]{3,1,2,0:T(4,128)S(1)}, f32[1,4,9,31]{3,1,2,0:T(4,128)}, u32[]{:S(2)}) copy-start(f32[1,4,9,31]{3,1,2,0:T(4,128)} %param.10) | copy-start | bytes 13396
  0.0 13.1 %copy-start = (bf16[2,2,1024,1024]{3,2,1,0:T(8,128)(2,1)S(1)}, bf16[2,2,1024,1024]{3,2,1,0:T(8,128)(2,1)}, u32[]{:S(2)}) copy-start(bf16[2,2,1024,1024]{3,2,1,0:T(8,128)(2,1)} %operator_ref.1) | copy-start | bytes 25165828
  1.9 22.1 %copy-start.1 = (f32[128,2048]{1,0:T(8,128)S(1)}, f32[128,2048]{1,0:T(8,128)}, u32[]{:S(2)}) copy-start(f32[128,2048]{1,0:T(8,128)} %gathers_ref.3) | copy-start | bytes 3145732
  2.0 22.1 %copy-start.2 = (bf16[192,2048]{1,0:T(8,128)(2,1)S(1)}, bf16[192,2048]{1,0:T(8,128)(2,1)}, u32[]{:S(2)}) copy-start(bf16[192,2048]{1,0:T(8,128)(2,1)} %constant.8.clone.table_ref) | copy-start | bytes 2359300

commit v20 on v18

--- a/solution.py
+++ b/solution.py
@@ -257,7 +257,7 @@
     with jax.named_scope("spectrum"):
         outgoing = pl.pallas_call(
             spectrum_kernel,
-            out_shape=jax.ShapeDtypeStruct((devices, group_rows, traces), jnp.float32),
+            out_shape=jax.ShapeDtypeStruct((devices, group_rows, traces), jnp.bfloat16),
             in_specs=[hbm_spec()] * 2,
             out_specs=vmem_spec(),
             scratch_shapes=[

time: 25.7 us -> 25.6 us (level)
  no operation moved by 1% of the time
where the time goes in v20:
time: 25.6 us; the launch traced here: 25.4 us
  blocking collectives  19 us (74%)
  Pallas kernels  6.24 us (24%)
    all_to_all x2, blocking collectives, exchange(): lax.all_to_all(chunks, 'freq', 0, 0, axis_index_groups=[order], tiled=True)  19 us
    pallas_call x1, Pallas kernels, local(): pl.pallas_call(functools.partial(predict_kernel, kept_bins), out_shape=[j...  2.92 us
    pallas_call x1, Pallas kernels, local(): pl.pallas_call(spectrum_kernel, out_shape=jax.ShapeDtypeStruct((devices,...  1.92 us
    pallas_call x1, Pallas kernels, local(): pl.pallas_call(functools.partial(subtract_kernel, length // 8), out_shape...  1.4 us

profile of v20, /device:TPU:0, one launch (start us, length us, event | category | flops | bytes accessed | tf_op | source)
XLA Modules:
  0.0 25.4 jit_solution(7499030796489754272)
XLA Ops:
  0.0 0.0 copy-start.3
  0.0 0.0 copy-start.6
  0.0 0.0 copy-start.5
  0.0 0.0 copy-start.4
  0.0 0.0 copy-start
  0.0 1.9 %spectrum.1 = bf16[16,4,128]{2,1,0:T(4,128)(2,1)S(1)} custom-call(f32[128,2048]{1,0:T(8,128)} %gathers_ref.3, bf16[128,1024]{1,0:T(8,128)(2,1)} %constant.6.clone.table_ref), custom_call_target="tpu_custom_call" | custom-call | flops 99999997952 | bytes 40000000 | tf_op jit(solution)/shard_map/spectrum/spectrum/pallas_call | solution.py:258
  1.9 0.0 copy-start.1
  2.0 0.0 copy-start.2
  2.0 11.0 %all_to_all.10.incoming_ref = bf16[16,4,128]{2,1,0:T(4,128)(2,1)S(1)} all-to-all(bf16[16,4,128]{2,1,0:T(4,128)(2,1)S(1)} %spectrum.1), channel_id=1, replica_groups={{11,15,14,13,12,10,9,8,7,6,5,4,3,2,1,0},{27,31,30,29,28,26,25,24,23,22,..., dimensions={0} | all-to-all | bytes 32768 | tf_op jit(solution)/shard_map/all_to_all | solution.py:231
  13.0 0.0 copy-done.3
  13.0 0.0 copy-done.6
  13.0 0.0 copy-done.5
  13.0 0.0 copy-done.4
  13.0 0.0 copy-done
  13.0 2.9 %predict.1 = (bf16[16,8,128]{2,1,0:T(8,128)(2,1)S(1)}, f32[9,128]{1,0:T(8,128)S(1)}) custom-call(s32[16]{0:T(128)S(1)} %copy-done.5, s32[16]{0:T(128)S(1)} %copy-done.6, f32[9,4,31]{2,1,0:T(4,128)S(1)} %bitcast.3, f32[124,128]{1,0:T(8,128)S(1)} %copy-done.3, bf16[16,4,128]{2,1,0:T(4,128)(2,1)S(1)} %all_to_all.10.incoming_ref, ...), custom_call_target="tpu_custom_call" | custom-call | tf_op jit(solution)/shard_map/predict/predict/pallas_call | solution.py:274
  15.9 8.0 %all_to_all.11.returned_ref = bf16[16,8,128]{2,1,0:T(8,128)(2,1)S(1)} all-to-all(bf16[16,8,128]{2,1,0:T(8,128)(2,1)S(1)} %get-tuple-element.7), channel_id=1, replica_groups={{15,14,13,12,11,10,9,8,7,6,5,4,3,2,1,0},{31,30,29,28,27,26,25,24,23,22,..., dimensions={0} | all-to-all | bytes 65536 | tf_op jit(solution)/shard_map/all_to_all | solution.py:231
  24.0 0.0 copy-done.1
  24.0 0.0 copy-done.2
  24.0 1.4 %subtract.1 = f32[128,2048]{1,0:T(8,128)} custom-call(bf16[16,8,128]{2,1,0:T(8,128)(2,1)S(1)} %all_to_all.11.returned_ref, f32[9,128]{1,0:T(8,128)S(1)} %get-tuple-element.8.coefficient_ref, bf16[192,2048]{1,0:T(8,128)(2,1)S(1)} %copy-done.2, f32[128,2048]{1,0:T(8,128)S(1)} %copy-done.1), custom_call_target="tpu_custom_call" | custom-call | tf_op jit(solution)/shard_map/subtract/subtract/pallas_call | solution.py:295
Async XLA Ops:
  0.0 13.0 %copy-start.3 = (f32[124,128]{1,0:T(8,128)S(1)}, f32[124,128]{1,0:T(8,128)}, u32[]{:S(2)}) copy-start(f32[124,128]{1,0:T(8,128)} %constant.7.clone.lag_ref) | copy-start | bytes 190468
  0.0 13.0 %copy-start.6 = (s32[16]{0:T(128)S(1)}, s32[16]{0:T(128)}, u32[]{:S(2)}) copy-start(s32[16]{0:T(128)} %slice_ref.1) | copy-start | bytes 196
  0.0 13.0 %copy-start.5 = (s32[16]{0:T(128)S(1)}, s32[16]{0:T(128)}, u32[]{:S(2)}) copy-start(s32[16]{0:T(128)} %tile_ref.1) | copy-start | bytes 196
  0.0 13.0 %copy-start.4 = (f32[1,4,9,31]{3,1,2,0:T(4,128)S(1)}, f32[1,4,9,31]{3,1,2,0:T(4,128)}, u32[]{:S(2)}) copy-start(f32[1,4,9,31]{3,1,2,0:T(4,128)} %param.10) | copy-start | bytes 13396
  0.0 13.0 %copy-start = (bf16[2,2,1024,1024]{3,2,1,0:T(8,128)(2,1)S(1)}, bf16[2,2,1024,1024]{3,2,1,0:T(8,128)(2,1)}, u32[]{:S(2)}) copy-start(bf16[2,2,1024,1024]{3,2,1,0:T(8,128)(2,1)} %operator_ref.1) | copy-start | bytes 25165828
  1.9 22.0 %copy-start.1 = (f32[128,2048]{1,0:T(8,128)S(1)}, f32[128,2048]{1,0:T(8,128)}, u32[]{:S(2)}) copy-start(f32[128,2048]{1,0:T(8,128)} %gathers_ref.3) | copy-start | bytes 3145732
  2.0 22.0 %copy-start.2 = (bf16[192,2048]{1,0:T(8,128)(2,1)S(1)}, bf16[192,2048]{1,0:T(8,128)(2,1)}, u32[]{:S(2)}) copy-start(bf16[192,2048]{1,0:T(8,128)(2,1)} %constant.8.clone.table_ref) | copy-start | bytes 2359300
